TPU v7x, 128 devices: a whole 4x4x4 slice. The times are simulated.
128 devices in a mesh: fsdp: 32 (over x, y_lo, z), seq: 4 (over y_hi, core).
Axes of the slice: x: 4, y: 4 (y_hi: 2, y_lo: 2; y = y_hi * 2 + y_lo), z: 4, core: 2. Of those that a mesh axis runs over, the one named last changes fastest.
Arguments:
- tokens: bfloat16 [1024, 6144], P('seq'), may hold values from -6 to 6
- target: bfloat16 [1024, 6144], P('seq'), may hold values from -6 to 6
- norm_gain: float32 [6144], replicated, may hold values from 0.1 to 1.9
- qkv_weight: bfloat16 [6144, 9216], P(None, 'fsdp'), may hold values from -1 to 1
- out_weight: bfloat16 [3072, 6144], P('fsdp'), may hold values from -0.109375 to 0.109375
- probe_seed: int32 [1], replicated, may hold values from 0 to 1073741823
- block_order: int32 [4], P('seq'), may hold values from 0 to 3, each once
Outputs:
- qkv_curv: float32 [6144, 9216], P('seq', 'fsdp')
- out_curv: float32 [3072, 6144], P('fsdp', 'seq')
Inputs may be any that keep to these rules, and one draw needn't show every extreme that they name: block_order is a permutation: each block of 256 tokens has its own place in the sequence.
All inputs are finite; a program needn't handle non-finite values.
Results may differ from a plain program's by a relative error of at most 0.02.
Values may be sent and summed in bfloat16 or wider, within the bound.
A program may use at most 128 MiB of HBM per device.

v0:
```python
import math

import jax
import jax.numpy as jnp
from jax import lax
from jax.sharding import PartitionSpec as P

HS = 96
ROT = 24


mix_one = -1640531535
mix_two = -2048144789
mix_three = -1028477387


def probe_signs(probe_seed, flat_index):
    state = flat_index * jnp.int32(mix_one) + probe_seed[0]
    state = state ^ lax.shift_right_logical(state, jnp.int32(16))
    state = state * jnp.int32(mix_two)
    state = state ^ lax.shift_right_logical(state, jnp.int32(13))
    state = state * jnp.int32(mix_three)
    state = state ^ lax.shift_right_logical(state, jnp.int32(16))
    chosen = lax.shift_right_logical(state, jnp.int32(7)) & jnp.int32(1)
    return (1 - 2 * chosen).astype(jnp.float32)


def layer_norm(tokens, norm_gain):
    values = tokens.astype(jnp.float32)
    average = jnp.mean(values, axis=-1, keepdims=True)
    centred = values - average
    spread = jnp.mean(centred * centred, axis=-1, keepdims=True)
    return (centred * lax.rsqrt(spread + 1e-05) * norm_gain).astype(jnp.bfloat16)


def rotate(field, positions):
    half_rot = ROT // 2
    inverse = 10000.0 ** (-2.0 * jnp.arange(half_rot, dtype=jnp.float32) / ROT)
    angles = positions.astype(jnp.float32)[:, None] * inverse[None, :]
    cosine = jnp.cos(angles)[:, None, :]
    sine = jnp.sin(angles)[:, None, :]
    lower_half = field[..., :half_rot]
    upper_half = field[..., half_rot:ROT]
    remainder = field[..., ROT:]
    return jnp.concatenate(
        [
            lower_half * cosine - upper_half * sine,
            upper_half * cosine + lower_half * sine,
            remainder,
        ],
        axis=-1,
    )


def prepare(qkv, positions):
    grid = qkv.reshape(qkv.shape[0], qkv.shape[1] // (3 * HS), 3, HS)
    query = rotate(grid[:, :, 0], positions).astype(jnp.bfloat16)
    keys = rotate(grid[:, :, 1], positions).astype(jnp.bfloat16)
    values = grid[:, :, 2].astype(jnp.bfloat16)
    return (query, keys, values)


def widened(qkv, positions):
    return tuple((part.astype(jnp.float32) for part in prepare(qkv, positions)))


def attend(query, keys, values, query_pos, key_pos):
    scores = jnp.einsum("qhd,khd->hqk", query, keys) / math.sqrt(query.shape[-1])
    allowed = key_pos[None, None, :] <= query_pos[None, :, None]
    scores = jnp.where(allowed, scores, -1e30)
    highest = lax.stop_gradient(jnp.max(scores, axis=-1, keepdims=True))
    weights = jnp.exp(scores - highest)
    weights = weights / jnp.sum(weights, axis=-1, keepdims=True)
    rounded = weights.astype(jnp.bfloat16).astype(jnp.float32)
    result = jnp.einsum("hqk,khd->qhd", rounded, values)
    return result.reshape(query.shape[0], -1).astype(jnp.bfloat16)


def per_device(tokens, target, norm_gain, qkv_weight, out_weight, probe_seed, block_order):
    tok_rows, width = tokens.shape
    col_count = qkv_weight.shape[1]
    inner_local = out_weight.shape[0]
    fsdp_count = lax.axis_size("fsdp")
    seq_count = lax.axis_size("seq")
    fsdp_index = lax.axis_index("fsdp")
    seq_index = lax.axis_index("seq")
    total_cols = col_count * fsdp_count
    total_inner = inner_local * fsdp_count
    offsets = jnp.arange(tok_rows, dtype=jnp.int32)
    positions = block_order[0] * tok_rows + offsets
    normed = layer_norm(tokens, norm_gain)
    row_ids = lax.broadcasted_iota(jnp.int32, (width, col_count), 0)
    col_ids = lax.broadcasted_iota(jnp.int32, (width, col_count), 1)
    qkv_signs = probe_signs(probe_seed, row_ids * total_cols + fsdp_index * col_count + col_ids)
    out_rows = lax.broadcasted_iota(jnp.int32, (inner_local, width), 0)
    out_cols = lax.broadcasted_iota(jnp.int32, (inner_local, width), 1)
    out_signs = probe_signs(
        probe_seed, width * total_cols + (fsdp_index * inner_local + out_rows) * width + out_cols
    )
    qkv_probe = (qkv_signs / math.sqrt(width)).astype(jnp.bfloat16)
    out_probe = (out_signs / math.sqrt(total_inner)).astype(jnp.bfloat16)
    qkv = jnp.dot(normed, qkv_weight, preferred_element_type=jnp.float32)
    qkv_tan = jnp.dot(normed, qkv_probe, preferred_element_type=jnp.float32)
    own_parts, own_tans = jax.jvp(lambda field: prepare(field, positions), (qkv,), (qkv_tan,))
    keys, values, keys_tan, values_tan, orders = (
        lax.all_gather(own_parts[1], "seq", axis=0, tiled=True),
        lax.all_gather(own_parts[2], "seq", axis=0, tiled=True),
        lax.all_gather(own_tans[1], "seq", axis=0, tiled=True),
        lax.all_gather(own_tans[2], "seq", axis=0, tiled=True),
        lax.all_gather(block_order, "seq", axis=0, tiled=True),
    )
    key_pos = (orders[:, None] * tok_rows + offsets[None, :]).reshape(-1)

    def local_attend(query, key_all, value_all):
        return attend(query, key_all, value_all, positions, key_pos)

    primals = (
        own_parts[0].astype(jnp.float32),
        keys.astype(jnp.float32),
        values.astype(jnp.float32),
    )
    tangents = (
        own_tans[0].astype(jnp.float32),
        keys_tan.astype(jnp.float32),
        values_tan.astype(jnp.float32),
    )
    attn, attn_tan = jax.jvp(local_attend, primals, tangents)
    mixed_part = jnp.dot(attn, out_weight, preferred_element_type=jnp.float32)
    mixed_tan_part = jnp.dot(attn_tan, out_weight, preferred_element_type=jnp.float32) + jnp.dot(
        attn, out_probe, preferred_element_type=jnp.float32
    )
    seq_total = tok_rows * seq_count
    mixed, mixed_tan = lax.psum((mixed_part, mixed_tan_part), "fsdp")
    resid = tokens.astype(jnp.float32) + mixed - target.astype(jnp.float32)
    grad_out = (resid / seq_total).astype(jnp.bfloat16)
    grad_tan = (mixed_tan / seq_total).astype(jnp.bfloat16)
    back = jnp.dot(grad_out, out_weight.T, preferred_element_type=jnp.float32).astype(jnp.bfloat16)
    back_tan = (
        jnp.dot(grad_tan, out_weight.T, preferred_element_type=jnp.float32)
        + jnp.dot(grad_out, out_probe.T, preferred_element_type=jnp.float32)
    ).astype(jnp.bfloat16)
    out_terms = jnp.dot(attn_tan.T, grad_out, preferred_element_type=jnp.float32) + jnp.dot(
        attn.T, grad_tan, preferred_element_type=jnp.float32
    )
    out_hv = lax.psum_scatter(
        out_terms.astype(jnp.bfloat16), "seq", scatter_dimension=1, tiled=True
    ).astype(jnp.float32)

    def pull_back(query, key_all, value_all, cotangent):
        return jax.vjp(local_attend, query, key_all, value_all)[1](cotangent)

    cot_query, cot_keys, cot_values = jax.jvp(pull_back, primals + (back,), tangents + (back_tan,))[
        1
    ]
    own_keys, own_values = (
        lax.psum_scatter(
            cot_keys.astype(jnp.bfloat16), "seq", scatter_dimension=0, tiled=True
        ).astype(jnp.float32),
        lax.psum_scatter(
            cot_values.astype(jnp.bfloat16), "seq", scatter_dimension=0, tiled=True
        ).astype(jnp.float32),
    )
    qkv_cot = jax.vjp(lambda field: widened(field, positions), qkv)[1](
        (cot_query, own_keys, own_values)
    )[0]
    cot_rounded = qkv_cot.astype(jnp.bfloat16)
    rows_share = width // seq_count
    qkv_hv = lax.psum_scatter(
        jnp.dot(normed.T, cot_rounded, preferred_element_type=jnp.float32).astype(jnp.bfloat16),
        "seq",
        scatter_dimension=0,
        tiled=True,
    ).astype(jnp.float32)
    qkv_sign_share = lax.dynamic_slice_in_dim(qkv_signs, seq_index * rows_share, rows_share, 0)
    out_sign_share = lax.dynamic_slice_in_dim(out_signs, seq_index * rows_share, rows_share, 1)
    return (
        qkv_hv * qkv_sign_share * math.sqrt(width),
        out_hv * out_sign_share * math.sqrt(total_inner),
    )


def solution(mesh):
    placed = (P("seq", None), P("seq", None), P(), P(None, "fsdp"), P("fsdp", None), P(), P("seq"))
    return jax.shard_map(
        per_device,
        mesh=mesh,
        in_specs=placed,
        out_specs=(P("seq", "fsdp"), P("fsdp", "seq")),
        check_vma=False,
    )
```

profile of v0, /device:TPU:1, one launch (start us, length us, event | category | flops | bytes accessed | tf_op | source)
XLA Modules:
  0.0 610.1 jit_solution(16076377025320448087)
XLA Ops:
  7.2 0.6 multiply_power_fusion
  8.9 0.5 fusion.128
  9.4 0.6 iota_add_fusion
  10.0 2.4 convert_reduce_fusion
  12.4 1.0 fusion.10
  14.1 7.3 %fusion.16 = f32[256,288]{0,1:T(8,128)S(1)} fusion(s32[]{:T(128)} %bitcast.131, s32[6144]{0:T(1024)S(1)} %multiply_add_fusion, bf16[256,6144]{1,0:T(8,128)(2,1)} %param.7, f32[6144]{0:T(1024)} %param.9, f32[256]{0:T(256)S(1)} %add_rsqrt_fusion, f32[256]{0:T(256)S(1)} %broadcast_multiply_fusion), kind=kOutput, calls=%fused_computation.27 | convolution fusion | flops 945684480 | bytes 3491844 | tf_op jit(solution)/shard_map/dot_general | solution.py:103
  21.5 0.6 slice.143
  22.2 1.3 fusion.163
  23.8 0.4 copy-done.30
  24.2 8.4 %all_gather.17 = bf16[1024,1,96]{0,2,1:T(8,128)(2,1)S(1)} all-gather(bf16[256,1,96]{0,2,1:T(8,128)(2,1)S(1)} %pad_maximum_fusion.1), channel_id=1, replica_groups=mesh['fsdp'=32,'seq'=4] {'seq'}, dimensions={0}, use_global_device_ids=true | all-gather | bytes 245760 | tf_op jit(solution)/shard_map/all_gather | solution.py:106
  32.7 1.3 dynamic-slice
  34.0 0.8 dynamic-update-slice
  34.8 0.9 slice.142
  35.7 5.8 all-reduce.9
  41.6 8.0 %all_gather.19 = bf16[1024,1,96]{0,2,1:T(8,128)(2,1)S(1)} all-gather(bf16[256,1,96]{0,2,1:T(8,128)(2,1)S(1)} %pad_maximum_fusion.3), channel_id=1, replica_groups=mesh['fsdp'=32,'seq'=4] {'seq'}, dimensions={0}, use_global_device_ids=true | all-gather | bytes 245760 | tf_op jit(solution)/shard_map/all_gather | solution.py:108
  49.5 7.3 %all-gather = bf16[1024,1,1,96]{0,3,2,1:T(8,128)(2,1)S(1)} all-gather(bf16[256,1,1,96]{0,3,2,1:T(8,128)(2,1)} %slice.143), channel_id=2, replica_groups=mesh['fsdp'=32,'seq'=4] {'seq'}, dimensions={0}, use_global_device_ids=true | all-gather | bytes 245760 | tf_op jit(solution)/shard_map/all_gather | solution.py:109
  56.9 7.3 %all-gather.1 = bf16[1024,1,1,96]{0,3,2,1:T(8,128)(2,1)S(1)} all-gather(bf16[256,1,1,96]{0,3,2,1:T(8,128)(2,1)S(1)} %slice.142), channel_id=3, replica_groups=mesh['fsdp'=32,'seq'=4] {'seq'}, dimensions={0}, use_global_device_ids=true | all-gather | bytes 245760 | tf_op jit(solution)/shard_map/all_gather | solution.py:107
  64.1 1.1 fusion.166
  65.2 0.3 fusion.161
  65.6 0.3 fusion.69
  65.9 0.6 fusion.167
  66.5 0.6 fusion.127
  67.1 1.2 add_convert_fusion
  68.3 0.3 fusion.73
  68.6 0.5 copy-done.12
  69.1 0.3 fusion.42
  69.5 1.3 fusion.45
  70.8 1.0 fusion.168
  71.9 3.6 fusion.169
  75.5 5.0 convolution_add_fusion
  80.5 0.3 reduce-scatter.7.cloned.1.call-start
  80.8 348.9 %all-reduce.13.cloned.1.call-done = (f32[256,6144]{1,0:T(8,128)}, f32[256,6144]{1,0:T(8,128)}) async-done(((f32[256,6144]{1,0:T(8,128)}, f32[256,6144]{1,0:T(8,128)}), (f32[256,6144]{1,0:T(8,128)}, f32[256,6144]{1,0:T(8,128)})) %all-reduce.13.cloned.1.call-update) | async-done | bytes 12582928 | tf_op jit(solution)/shard_map/psum | solution.py:133
  429.6 5.1 fusion.15
  434.8 1.1 fusion.43
  436.0 1.9 fusion.59
  437.9 0.3 slice-done
  438.1 0.7 slice-done.1
  438.8 1.1 fusion.44
  440.0 1.0 fusion.170
  441.0 0.3 fusion.63
  441.3 0.3 fusion.28
  441.7 0.8 fusion.47
  442.6 1.6 fusion.57
  444.2 0.8 copy-done.15
  445.3 0.9 fusion.35
  446.3 2.0 fusion.34
  448.2 4.0 fusion.171
  452.3 5.3 fusion.9
  457.6 0.3 reduce-scatter.9.cloned.1.call-start
  457.9 1.3 fusion.67
  459.3 1.3 fusion.41
  460.6 26.3 %reduce-scatter.7.cloned.1.call-done = bf16[256,1,96]{0,2,1:T(8,128)(2,1)} async-done(((bf16[1024,1,96]{0,2,1:T(8,128)(2,1)}), bf16[256,1,96]{0,2,1:T(8,128)(2,1)}) %reduce-scatter.7.cloned.1.call-update) | async-done | bytes 49168 | tf_op jit(solution)/shard_map/reduce_scatter | solution.py:156
  486.9 0.8 convert_element_type.249
  487.7 0.8 split.24
  488.7 26.9 %reduce-scatter.5.cloned.1.call-done = bf16[256,1,96]{0,2,1:T(8,128)(2,1)} async-done(((bf16[1024,1,96]{0,2,1:T(8,128)(2,1)}), bf16[256,1,96]{0,2,1:T(8,128)(2,1)}) %reduce-scatter.5.cloned.1.call-update) | async-done | bytes 49168 | tf_op jit(solution)/shard_map/reduce_scatter | solution.py:159
  515.6 0.8 add_convert_fusion.1
  516.4 4.1 convolution_convert_fusion
  520.5 0.6 copy-done.53
  521.0 2.8 fusion.25
  523.9 6.3 %fusion.8 = f32[6144,288]{0,1:T(8,128)} fusion(s32[]{:T(128)} %bitcast.129, s32[6144]{0:T(1024)} %copy-done.31), kind=kLoop, calls=%fused_computation.17 | loop fusion | flops 28311552 | bytes 7102468 | tf_op jit(solution)/shard_map/convert_element_type | solution.py:25
  530.2 20.7 %reduce-scatter.11.cloned.1.call-done = bf16[96,1536]{1,0:T(8,128)(2,1)} async-done(((bf16[96,6144]{1,0:T(8,128)(2,1)}), bf16[96,1536]{1,0:T(8,128)(2,1)}) %reduce-scatter.11.cloned.1.call-update) | async-done | bytes 294928 | tf_op jit(solution)/shard_map/reduce_scatter | solution.py:145
  550.9 2.0 multiply_multiply_fusion.1
  552.9 47.5 %reduce-scatter.9.cloned.1.call-done = bf16[1536,288]{0,1:T(8,128)(2,1)} async-done(((bf16[6144,288]{0,1:T(8,128)(2,1)}), bf16[1536,288]{0,1:T(8,128)(2,1)}) %reduce-scatter.9.cloned.1.call-update) | async-done | bytes 884752 | tf_op jit(solution)/shard_map/reduce_scatter | solution.py:168
  600.4 3.1 multiply_multiply_fusion
  (146 shorter events, 1.2 us)
Async XLA Ops:
  7.2 15.0 %copy-start = (bf16[6144,288]{0,1:T(8,128)(2,1)S(1)}, bf16[6144,288]{0,1:T(8,128)(2,1)}, u32[]{:S(2)}) copy-start(bf16[6144,288]{0,1:T(8,128)(2,1)} %param.10) | copy-start | bytes 10616836
  7.2 422.5 %all-reduce.13.cloned.1.call-start = ((), (), s32[]{:S(2)}) async-start(), calls=%async_computation.8 | async-start | bytes 25165824 | tf_op jit(solution)/shard_map/psum | solution.py:133
  7.2 5.2 copy-start.2
  12.4 9.7 %copy-start.48 = (f32[256]{0:T(256)}, f32[256]{0:T(256)S(1)}, u32[]{:S(2)}) copy-start(f32[256]{0:T(256)S(1)} %broadcast_multiply_fusion) | copy-start | bytes 3076
  13.4 8.7 %copy-start.55 = (f32[256]{0:T(256)}, f32[256]{0:T(256)S(1)}, u32[]{:S(2)}) copy-start(f32[256]{0:T(256)S(1)} %add_rsqrt_fusion) | copy-start | bytes 3076
  13.4 8.0 %copy-start.31 = (s32[6144]{0:T(1024)}, s32[6144]{0:T(1024)S(1)}, u32[]{:S(2)}) copy-start(s32[6144]{0:T(1024)S(1)} %multiply_add_fusion) | copy-start | bytes 73732
  14.1 8.0 %copy-start.3 = (bf16[256,6144]{1,0:T(8,128)(2,1)S(1)}, bf16[256,6144]{1,0:T(8,128)(2,1)}, u32[]{:S(2)}) copy-start(bf16[256,6144]{1,0:T(8,128)(2,1)} %param.7) | copy-start | bytes 9437188
  14.1 8.0 %copy-start.57 = (f32[6144]{0:T(1024)S(1)}, f32[6144]{0:T(1024)}, u32[]{:S(2)}) copy-start(f32[6144]{0:T(1024)} %param.9) | copy-start | bytes 73732
  22.1 1.5 copy-start.44
  22.1 1.5 copy-start.50
  23.5 0.7 copy-start.30
  23.5 42.4 %copy-start.46 = (s32[256]{0:T(256)S(1)}, s32[256]{0:T(256)}, u32[]{:S(2)}) copy-start(s32[256]{0:T(256)} %iota_add_fusion) | copy-start | bytes 3076
  23.6 42.3 %copy-start.28 = (bf16[256,72]{0,1:T(8,128)(2,1)}, bf16[256,72]{0,1:T(8,128)(2,1)S(1)}, u32[]{:S(2)}) copy-start(bf16[256,72]{0,1:T(8,128)(2,1)S(1)} %fusion.75) | copy-start | bytes 110596
  23.6 42.8 %copy-start.26 = (bf16[256,72]{0,1:T(8,128)(2,1)}, bf16[256,72]{0,1:T(8,128)(2,1)S(1)}, u32[]{:S(2)}) copy-start(bf16[256,72]{0,1:T(8,128)(2,1)S(1)} %fusion.76) | copy-start | bytes 110596
  23.8 42.6 %copy-start.32 = (bf16[256,12]{0,1:T(8,128)(2,1)}, bf16[256,12]{0,1:T(8,128)(2,1)S(1)}, u32[]{:S(2)}) copy-start(bf16[256,12]{0,1:T(8,128)(2,1)S(1)} %get-tuple-element.18) | copy-start | bytes 18436
  23.8 42.6 %copy-start.34 = (bf16[256,12]{0,1:T(8,128)(2,1)}, bf16[256,12]{0,1:T(8,128)(2,1)S(1)}, u32[]{:S(2)}) copy-start(bf16[256,12]{0,1:T(8,128)(2,1)S(1)} %get-tuple-element.19) | copy-start | bytes 18436
  32.7 32.9 %copy-start.16 = (bf16[1024,1,96]{0,2,1:T(8,128)(2,1)}, bf16[1024,1,96]{0,2,1:T(8,128)(2,1)S(1)}, u32[]{:S(2)}) copy-start(bf16[1024,1,96]{0,2,1:T(8,128)(2,1)S(1)} %all_gather.17) | copy-start | bytes 589828
  41.6 24.9 %copy-start.36 = (s32[1,2,4,128]{3,1,2,0:T(2,128)}, s32[1,2,4,128]{3,1,2,0:T(2,128)S(1)}, u32[]{:S(2)}) copy-start(s32[1,2,4,128]{3,1,2,0:T(2,128)S(1)} %copy.9) | copy-start | bytes 12292
  49.5 16.9 %copy-start.20 = (bf16[1024,1,96]{0,2,1:T(8,128)(2,1)}, bf16[1024,1,96]{0,2,1:T(8,128)(2,1)S(1)}, u32[]{:S(2)}) copy-start(bf16[1024,1,96]{0,2,1:T(8,128)(2,1)S(1)} %all_gather.19) | copy-start | bytes 589828
  56.9 11.5 %copy-start.18 = (bf16[1024,1,1,96]{0,3,2,1:T(8,128)(2,1)}, bf16[1024,1,1,96]{0,3,2,1:T(8,128)(2,1)S(1)}, u32[]{:S(2)}) copy-start(bf16[1024,1,1,96]{0,3,2,1:T(8,128)(2,1)S(1)} %all-gather) | copy-start | bytes 589828
  65.2 3.1 copy-start.8
  65.2 376.4 %copy-start.38 = (f32[256]{0:T(256)}, f32[256]{0:T(256)S(1)}, u32[]{:S(2)}) copy-start(f32[256]{0:T(256)S(1)} %get-tuple-element.37) | copy-start | bytes 3076
  65.5 2.8 copy-start.39
  66.5 5.3 copy-start.10
  66.5 4.3 copy-start.6
  67.1 4.7 copy-start.42
  67.1 374.5 %copy-start.41 = (f32[256]{0:T(256)}, f32[256]{0:T(256)S(1)}, u32[]{:S(2)}) copy-start(f32[256]{0:T(256)S(1)} %get-tuple-element.35) | copy-start | bytes 3076
  68.3 0.8 copy-start.12
  69.4 6.0 copy-start.23
  69.5 366.5 %copy-start.52 = (s32[96]{0:T(128)}, s32[96]{0:T(128)S(1)}, u32[]{:S(2)}) copy-start(s32[96]{0:T(128)S(1)} %multiply_add_fusion.1) | copy-start | bytes 1156
  70.8 1.0 copy-start.24
  80.5 349.2 %copy-start.4 = (bf16[256,6144]{1,0:T(8,128)(2,1)S(1)}, bf16[256,6144]{1,0:T(8,128)(2,1)}, u32[]{:S(2)}) copy-start(bf16[256,6144]{1,0:T(8,128)(2,1)} %param.7) | copy-start | bytes 9437188
  80.5 406.4 %reduce-scatter.7.cloned.1.call-start = ((), (), s32[]{:S(2)}) async-start(), calls=%async_computation.5 | async-start | bytes 245760 | tf_op jit(solution)/shard_map/reduce_scatter | solution.py:156
  429.6 5.2 copy-start.7
  434.8 3.1 copy-start.5
  435.9 5.7 copy-start.25
  435.9 2.2 slice-start
  436.0 2.9 slice-start.1
  438.8 1.1 copy-start.13
  438.8 2.5 copy-start.19
  440.0 1.7 copy-start.9
  440.0 1.7 copy-start.11
  440.0 1.7 copy-start.54
  441.0 1.6 copy-start.37
  441.0 1.6 copy-start.40
  441.0 1.6 copy-start.43
  441.0 1.6 copy-start.47
  441.7 3.3 copy-start.29
  441.7 3.3 copy-start.33
  441.7 3.3 copy-start.35
  442.5 2.8 copy-start.27
  442.6 3.7 copy-start.22
  444.2 0.8 copy-start.15
  444.2 1.1 copy-start.14
  446.2 69.3 %reduce-scatter.5.cloned.1.call-start = ((), (), s32[]{:S(2)}) async-start(), calls=%async_computation.4 | async-start | bytes 245760 | tf_op jit(solution)/shard_map/reduce_scatter | solution.py:159
  452.2 5.7 copy-start.17
  452.2 7.0 %copy-start.21 = (bf16[1024,1,96]{0,2,1:T(8,128)(2,1)S(1)}, bf16[1024,1,96]{0,2,1:T(8,128)(2,1)}, u32[]{:S(2)}) copy-start(bf16[1024,1,96]{0,2,1:T(8,128)(2,1)} %copy-done.20) | copy-start | bytes 589828
  452.2 98.6 %reduce-scatter.11.cloned.1.call-start = ((), (), s32[]{:S(2)}) async-start(), calls=%async_computation.7 | async-start | bytes 1474560 | tf_op jit(solution)/shard_map/reduce_scatter | solution.py:145
  457.6 30.9 %copy-start.45 = (f32[256]{0:T(256)S(1)}, f32[256]{0:T(256)}, u32[]{:S(2)}) copy-start(f32[256]{0:T(256)} %fusion.128) | copy-start | bytes 3076
  457.6 30.9 %copy-start.51 = (f32[12]{0:T(128)S(1)}, f32[12]{0:T(128)}, u32[]{:S(2)}) copy-start(f32[12]{0:T(128)} %multiply_power_fusion) | copy-start | bytes 148
  457.6 58.8 %copy-start.49 = (f32[256]{0:T(256)S(1)}, f32[256]{0:T(256)}, u32[]{:S(2)}) copy-start(f32[256]{0:T(256)} %copy-done.48) | copy-start | bytes 3076
  457.6 58.8 %copy-start.56 = (f32[256]{0:T(256)S(1)}, f32[256]{0:T(256)}, u32[]{:S(2)}) copy-start(f32[256]{0:T(256)} %copy-done.55) | copy-start | bytes 3076
  457.6 142.8 %reduce-scatter.9.cloned.1.call-start = ((), (), s32[]{:S(2)}) async-start(), calls=%async_computation.6 | async-start | bytes 4423680 | tf_op jit(solution)/shard_map/reduce_scatter | solution.py:168
  523.9 79.7 %copy-start.1 = (bf16[6144,288]{0,1:T(8,128)(2,1)S(1)}, bf16[6144,288]{0,1:T(8,128)(2,1)}, u32[]{:S(2)}) copy-start(bf16[6144,288]{0,1:T(8,128)(2,1)} %param.10) | copy-start | bytes 10616836
  (1 other events, 0.6 us)
Sparse Core Ops, SparseCore 0:
  80.6 348.9 all-reduce.12
  446.3 40.5 reduce-scatter.6
  489.4 26.0 reduce-scatter.4
  518.7 32.1 reduce-scatter.10
  553.6 46.7 reduce-scatter.8
where the time goes:
time: 611 us; the launch traced here: 610 us
  waiting for transfers between devices  470 us (77%)
  matrix products  47.7 us (8%)
  blocking collectives  36.8 us (6%)
  other arithmetic  30.3 us (5%)
  between operations  16.4 us (3%)
  local copies, waits for them, and re-layouts  7.93 us (1%)
    psum x1, waiting for transfers between devices, per_device(): mixed, mixed_tan = lax.psum((mixed_part, mixed_tan_part), 'fsdp')  349 us
    reduce_scatter x1, waiting for transfers between devices, per_device(): lax.psum_scatter(jnp.dot(normed.T, cot_rounded, preferred_element_type=jn...  47.5 us
    reduce_scatter x1, waiting for transfers between devices, per_device(): lax.psum_scatter(cot_values.astype(jnp.bfloat16), 'seq', scatter_dimensio...  26.9 us
    reduce_scatter x1, waiting for transfers between devices, per_device(): lax.psum_scatter(cot_keys.astype(jnp.bfloat16), 'seq', scatter_dimension=...  26.3 us
    reduce_scatter x1, waiting for transfers between devices, per_device(): lax.psum_scatter(out_terms.astype(jnp.bfloat16), 'seq', scatter_dimension...  20.7 us
  transfers between devices with their start and end apart: 5, of which 5 were waited for; matrix products, arithmetic and copies ran while one was open for 5% of the time, Pallas kernels for 0%

commit v1 on v0

v1 whole, which is shorter than its diff:
```python
import functools
import math

import jax
import jax.numpy as jnp
import numpy as np
from jax import lax
from jax.experimental import pallas as pl
from jax.experimental.pallas import tpu as pltpu
from jax.sharding import PartitionSpec as P

MESH = pl.DeviceIdType.MESH
BF = jnp.bfloat16
F32 = jnp.float32
D = 6144
HS = 96
ROT = 24
TOK = 256
COLS = 288
WIDE = 9216
INNER = 3072
SHARE = 1536
PART = 384
HALF = 48
MIX = (-1640531535, -2048144789, -1028477387)
N_REMOTE = 136
N_LOCAL = 16


def wrap(value):
    return ((value + 2**31) % 2**32) - 2**31


def shifted(state, places):
    return lax.shift_right_logical(state, jnp.full(state.shape, places, jnp.int32))


def sign_bit(state):
    state = state ^ shifted(state, 16)
    state = state * jnp.int32(MIX[1])
    state = state ^ shifted(state, 13)
    state = state * jnp.int32(MIX[2])
    return (state ^ shifted(state, 16)) & jnp.int32(128)


def dot(a, b, contract):
    return lax.dot_general(a, b, (contract, ((), ())), preferred_element_type=F32)


NN = ((1,), (0,))
NT = ((1,), (1,))
TN = ((0,), (0,))


def kernel(
    tok_in, tgt_in, gain, wq_in, wo_in, seed, block, tab_t, tab_b,
    oq, oo,
    tok, tgt, wq, nrm, acc,
    nb, nt, gkv, ta, tb, wa, wb, pa, pb, ga, gb,
    score, score_tan, prob, prob_tan, rnd, rnd_tan,
    mix_acc, mix_out, mix_in, grads, back_acc,
    sa, sb, ra1, rb1, sa2, sb2, ra2, rb2,
    ha, hb, ca, cb, xa, xb, ya, yb, fa, fb, oa, ob,
    ck, cr, cx, cy, cot, sgn,
    send, recv, local,
):
    fs = lax.axis_index("fsdp")
    s = lax.axis_index("seq")
    x = fs // 8
    yl = (fs // 4) % 2
    z = fs % 4
    yh = s // 2
    c = s % 2
    s_sib = yh * 2 + (1 - c)
    s_crs = (1 - yh) * 2 + c
    s_crd = (1 - yh) * 2 + (1 - c)
    own_cols = (x * 4 + z) * PART

    def device(px, py, pz, ps):
        return ((px * 2 + py) * 4 + pz, ps)

    def xp(d):
        return device((x + d) % 4, yl, z, s)

    def zp(d):
        return device(x, yl, (z + d) % 4, s)

    def fin(d):
        return device(s, yl, (z + d) % 4, x)

    partner = device(x, 1 - yl, z, s)
    sib = device(x, yl, z, s_sib)
    crs = device(x, yl, z, s_crs)
    crd = device(x, yl, z, s_crd)

    count = [0]
    sent = []

    def remote(src, dst, to, begin=True):
        i = count[0]
        count[0] += 1
        copy = pltpu.make_async_remote_copy(
            src_ref=src, dst_ref=dst, send_sem=send.at[i], recv_sem=recv.at[i],
            device_id=to, device_id_type=MESH,
        )
        if begin:
            copy.start()
            sent.append(copy)
        return copy

    local_count = [0]

    def stay(src, dst):
        i = local_count[0]
        local_count[0] += 1
        copy = pltpu.make_async_copy(src, dst, local.at[i])
        copy.start()
        return copy

    def arrived(copies):
        for copy in copies:
            copy.wait_recv()

    def lanes(start, size):
        return pl.ds(pl.multiple_of(start, 128), size)

    def rows(start, size):
        return pl.ds(pl.multiple_of(start, 16), size)

    tok_load = stay(tok_in, tok)
    wq_load = stay(wq_in, wq)
    tgt_load = stay(tgt_in.at[:, lanes(own_cols, PART)], tgt)
    own_ta = stay(wo_in.at[pl.ds(0, HALF), lanes(x * SHARE, SHARE)], ta.at[x])
    own_tb = [
        stay(wo_in.at[pl.ds(HALF, HALF), lanes((k * 4 + z) * PART, PART)], tb.at[z, k])
        for k in range(4)
    ]

    barrier = pltpu.get_barrier_semaphore()

    def greet(to):
        pl.semaphore_signal(barrier, inc=1, device_id=to, device_id_type=MESH)

    for d in (1, 2, 3):
        greet(xp(d))
        greet(zp(d))
    for to in (partner, sib, crs, crd):
        greet(to)

    @pl.when(x != s)
    def _():
        for d in range(4):
            greet(fin(d))

    pl.semaphore_wait(barrier, jnp.where(x != s, 14, 10))

    w_one = []
    for d in (1, 2, 3):
        other = (x + d) % 4
        w_one.append(
            remote(wo_in.at[pl.ds(0, HALF), lanes(other * SHARE, SHARE)], ta.at[x], xp(d))
        )
        other = (z + d) % 4
        for k in range(4):
            w_one.append(
                remote(
                    wo_in.at[pl.ds(HALF, HALF), lanes((k * 4 + other) * PART, PART)],
                    tb.at[z, k], zp(d),
                )
            )

    tok_load.wait()

    def norm_rows(i, carry):
        at = rows(i * 16, 16)
        values = tok[at, :].astype(F32)
        centred = values - jnp.mean(values, axis=-1, keepdims=True)
        spread = jnp.mean(centred * centred, axis=-1, keepdims=True)
        nrm[at, :] = (centred * lax.rsqrt(spread + 1e-05) * gain[...]).astype(BF)
        return carry

    lax.fori_loop(0, TOK // 16, norm_rows, 0)

    piece = jnp.where(c == 0, z * 4 + x, x * 4 + z) * 16
    n_sib = remote(nrm.at[:, lanes(s_sib * SHARE, SHARE)], nb.at[s], sib)
    n_crs = remote(
        nrm.at[rows(piece, 16), lanes(s_crs * SHARE, SHARE)], nb.at[s, rows(piece, 16)], crs
    )
    n_crd = remote(
        nrm.at[rows(piece, 16), lanes(s_crd * SHARE, SHARE)], nb.at[s, rows(piece, 16)], crd
    )

    wq_load.wait()
    acc[...] = jnp.zeros_like(acc)
    seeded = seed[0]
    q_probe = float(np.float32(1 / math.sqrt(D)).astype(jnp.bfloat16))
    o_probe = float(np.float32(1 / math.sqrt(INNER)).astype(jnp.bfloat16))
    q_rows = lax.broadcasted_iota(jnp.int32, (TOK, COLS), 0)
    q_cols = lax.broadcasted_iota(jnp.int32, (TOK, COLS), 1)
    q_base = (q_rows * WIDE + q_cols + fs * COLS) * jnp.int32(MIX[0]) + seeded

    def project(i, carry):
        at = pl.ds(pl.multiple_of(i * TOK, TOK), TOK)
        bit = sign_bit(q_base + i * jnp.int32(wrap(TOK * WIDE * MIX[0])))
        probe = jnp.where(bit == 0, F32(q_probe), F32(-q_probe)).astype(BF)
        left = nrm[:, pl.ds(pl.multiple_of(i * TOK, TOK), TOK)]
        acc[0, :, pl.ds(0, COLS)] += dot(left, wq[at, :], NN)
        acc[1, :, pl.ds(0, COLS)] += dot(left, probe, NN)
        return carry

    lax.fori_loop(0, D // TOK, project, 0)

    number = block[0]
    cos_b = jnp.zeros((ROT, TOK), F32)
    sin_b = jnp.zeros((ROT, TOK), F32)
    for k in range(4):
        here = jnp.full((ROT, TOK), number, jnp.int32) == k
        cos_b = jnp.where(here, tab_b[k, 0], cos_b)
        sin_b = jnp.where(here, tab_b[k, 1], sin_b)
    cos = cos_b * tab_t[0] - sin_b * tab_t[1]
    sin = sin_b * tab_t[0] + cos_b * tab_t[1]
    low = lax.broadcasted_iota(jnp.int32, (ROT, TOK), 0) < ROT // 2
    sin = jnp.where(low, -sin, sin)

    def rotate(field, turn):
        head = field[:ROT]
        swapped = pltpu.roll(head, ROT // 2, 0)
        return jnp.concatenate([head * cos + swapped * turn, field[ROT:]], axis=0)

    fields = []
    for k in range(2):
        turned = acc[k].T
        fields.append(
            (
                rotate(turned[0:HS], sin).astype(BF),
                rotate(turned[HS : 2 * HS], sin).astype(BF),
                turned[2 * HS : 3 * HS].astype(BF),
            )
        )
    q, q_tan = fields[0][0], fields[1][0]
    q_both = jnp.concatenate([q_tan, q], axis=0)
    gkv[s, 0:HS] = fields[0][1]
    gkv[s, HS : 2 * HS] = fields[1][1]
    gkv[s, 2 * HS : 3 * HS] = fields[0][2]
    gkv[s, 3 * HS : 4 * HS] = fields[1][2]
    gkv[s, 4 * HS : 4 * HS + 16] = jnp.full((16, TOK), number, jnp.int32).astype(F32).astype(BF)
    kv_crs = remote(gkv.at[s], gkv.at[s], crs)
    kv_sib = remote(gkv.at[s], gkv.at[s], sib)

    b0 = (1 - yh) * 2
    b1 = b0 + 1
    arrived([n_crs, n_crd])
    n_one = []
    for d in (1, 2, 3):
        at0 = nb.at[b0, rows((z * 4 + x) * 16, 16)]
        at1 = nb.at[b1, rows((x * 4 + z) * 16, 16)]
        n_one.append(remote(at0, at0, xp(d)))
        n_one.append(remote(at1, at1, zp(d)))

    for copy in [own_ta] + own_tb:
        copy.wait()
    arrived(w_one)
    w_two = []
    for d in (1, 2, 3):
        other = (z + d) % 4
        w_two.append(remote(ta.at[:, :, lanes(other * PART, PART)], wa.at[z], zp(d)))
        other = (x + d) % 4
        w_two.append(remote(tb.at[:, other], wb.at[x], xp(d)))
    own_wa = stay(ta.at[:, :, lanes(z * PART, PART)], wa.at[z])
    own_wb = stay(tb.at[:, x], wb.at[x])

    o_rows = lax.broadcasted_iota(jnp.int32, (HALF, PART), 0)
    o_lanes = lax.broadcasted_iota(jnp.int32, (HALF, PART), 1)
    o_base = (o_rows * D + o_lanes + (D * WIDE + own_cols)) * jnp.int32(MIX[0]) + seeded

    def probe_piece(i, carry):
        for k in range(4):
            first = ((k * 2 + yl) * 4 + i) * HS
            second = ((i * 2 + yl) * 4 + k) * HS + HALF
            bit = sign_bit(o_base + first * jnp.int32(wrap(D * MIX[0])))
            pa[i, k] = jnp.where(bit == 0, F32(o_probe), F32(-o_probe)).astype(BF)
            bit = sign_bit(o_base + second * jnp.int32(wrap(D * MIX[0])))
            pb[i, k] = jnp.where(bit == 0, F32(o_probe), F32(-o_probe)).astype(BF)
        return carry

    lax.fori_loop(0, 4, probe_piece, 0)

    arrived([kv_crs])
    kv_rel = remote(gkv.at[s_crs], gkv.at[s_crs], sib)

    arrived(n_one)
    n_two = []
    for d in (1, 2, 3):
        at0 = nb.at[b0, rows(z * 64, 64)]
        at1 = nb.at[b1, rows(x * 64, 64)]
        n_two.append(remote(at0, at0, zp(d)))
        n_two.append(remote(at1, at1, xp(d)))

    arrived([kv_sib, kv_rel])
    root = 1 / math.sqrt(HS)

    def keys_of(b):
        return lanes(b * TOK, TOK)

    def score_block(b, carry):
        score[:, keys_of(b)] = dot(q, gkv[b, 0:HS], TN) * root
        score_tan[:, keys_of(b)] = dot(q_both, gkv[b, 0 : 2 * HS], TN) * root
        return carry

    lax.fori_loop(0, 4, score_block, 0)
    along = lax.broadcasted_iota(jnp.int32, (1, TOK), 1).astype(F32)
    key_pos = jnp.concatenate(
        [gkv[b, 4 * HS : 4 * HS + 16].astype(F32)[0:1] * float(TOK) + along for b in range(4)], axis=1
    )
    number_f = jnp.full((32, 1), number, jnp.int32).astype(F32)
    down = lax.broadcasted_iota(jnp.int32, (32, 1), 0)

    def soft_rows(i, carry):
        at = pl.ds(pl.multiple_of(i * 32, 32), 32)
        query_pos = number_f * float(TOK) + (down + i * 32).astype(F32)
        allowed = key_pos <= query_pos
        values = jnp.where(allowed, score[at, :], -1e30)
        highest = jnp.max(values, axis=-1, keepdims=True)
        weights = jnp.exp(values - highest)
        weights = weights * (1.0 / jnp.sum(weights, axis=-1, keepdims=True))
        tans = score_tan[at, :]
        moved = weights * tans
        moved = moved - weights * jnp.sum(moved, axis=-1, keepdims=True)
        prob[at, :] = weights
        prob_tan[at, :] = moved
        rnd[at, :] = weights.astype(BF)
        rnd_tan[at, :] = moved.astype(BF)
        return carry

    lax.fori_loop(0, TOK // 32, soft_rows, 0)

    def sum_blocks(term, shape):
        total = jnp.zeros(shape, F32)
        return lax.fori_loop(0, 4, lambda b, held: held + term(b), total)

    def gather_one(t):
        copies = []
        for d in (1, 2, 3):
            copies.append(remote(ga.at[t, z, x], ga.at[t, z, x], xp(d)))
            copies.append(remote(gb.at[t, x, z], gb.at[t, x, z], zp(d)))
        return copies

    def gather_two(t):
        copies = []
        for d in (1, 2, 3):
            copies.append(remote(ga.at[t, z], ga.at[t, z], zp(d)))
            copies.append(remote(gb.at[t, x], gb.at[t, x], xp(d)))
        return copies

    value_terms = sum_blocks(
        lambda b: dot(gkv[b, 2 * HS : 4 * HS], rnd[:, keys_of(b)], NT), (2 * HS, TOK)
    )
    attn = value_terms[:HS].astype(BF)
    ga[0, z, x] = attn[:HALF]
    gb[0, x, z] = attn[HALF:]
    g_one = gather_one(0)
    attn_tan = (
        sum_blocks(lambda b: dot(gkv[b, 2 * HS : 3 * HS], rnd_tan[:, keys_of(b)], NT), (HS, TOK))
        + value_terms[HS:]
    ).astype(BF)
    ga[1, z, x] = attn_tan[:HALF]
    gb[1, x, z] = attn_tan[HALF:]
    g_one_tan = gather_one(1)
    arrived(g_one)
    g_two = gather_two(0)
    arrived(g_one_tan)
    g_two_tan = gather_two(1)


    arrived([n_sib] + n_two)

    def turn_own(i, carry):
        nt[s, pl.ds(pl.multiple_of(i * TOK, TOK), TOK), :] = nrm[:, lanes(s * SHARE + i * TOK, TOK)].T
        return carry

    lax.fori_loop(0, SHARE // TOK, turn_own, 0)

    def turn_other(i, carry):
        b = (s + 1 + i // 6) % 4
        k = i % 6
        nt[b, pl.ds(pl.multiple_of(k * TOK, TOK), TOK), :] = nb[b, :, lanes(k * TOK, TOK)].T
        return carry

    lax.fori_loop(0, 18, turn_other, 0)

    own_wa.wait()
    own_wb.wait()
    arrived(w_two)
    arrived(g_two)

    def whole(ref, *at):
        value = ref[at]
        return value.reshape(4 * HALF, value.shape[-1])

    mix_acc[...] = jnp.zeros_like(mix_acc)

    def mix_one(i, carry):
        left, right = whole(ga, 0, i), whole(gb, 0, i)
        mix_acc[0] += dot(left, whole(wa, i), TN) + dot(right, whole(wb, i), TN)
        mix_acc[1] += dot(left, whole(pa, i), TN) + dot(right, whole(pb, i), TN)
        return carry

    lax.fori_loop(0, 4, mix_one, 0)
    mix_out[0] = mix_acc[0].astype(BF)
    m_one = remote(mix_out.at[0], mix_in.at[0], partner)
    arrived(g_two_tan)

    def mix_two(i, carry):
        mix_acc[1] += dot(whole(ga, 1, i), whole(wa, i), TN) + dot(whole(gb, 1, i), whole(wb, i), TN)
        return carry

    lax.fori_loop(0, 4, mix_two, 0)
    mix_out[1] = mix_acc[1].astype(BF)
    m_two = remote(mix_out.at[1], mix_in.at[1], partner)

    s_base = (
        (lax.broadcasted_iota(jnp.int32, (128, COLS), 0) + s * SHARE) * WIDE
        + lax.broadcasted_iota(jnp.int32, (128, COLS), 1)
        + fs * COLS
    ) * jnp.int32(MIX[0]) + seeded

    def sign_rows(i, carry):
        bit = sign_bit(s_base + i * jnp.int32(wrap(128 * WIDE * MIX[0])))
        sgn[pl.ds(pl.multiple_of(i * 128, 128), 128), :] = jnp.where(
            bit == 0, F32(math.sqrt(D)), F32(-math.sqrt(D))
        )
        return carry

    lax.fori_loop(0, SHARE // 128, sign_rows, 0)

    tgt_load.wait()
    arrived([m_one])
    resid = tok[:, lanes(own_cols, PART)].astype(F32) - tgt[...].astype(F32)
    resid = resid + (mix_acc[0] + mix_in[0].astype(F32))
    grads[0] = (resid * (1 / 1024)).astype(BF)

    def back_one(i, carry):
        grad = grads[0]
        sa[0, i] = dot(whole(wa, i), grad, NT).astype(BF).reshape(4, HALF, TOK)
        sb[0, i] = dot(whole(wb, i), grad, NT).astype(BF).reshape(4, HALF, TOK)
        back_acc[0, i] = dot(whole(pa, i), grad, NT)
        back_acc[1, i] = dot(whole(pb, i), grad, NT)
        return carry

    lax.fori_loop(0, 4, back_one, 0)

    def scatter_one(t):
        copies = []
        for d in (1, 2, 3):
            copies.append(remote(sa.at[t, (z + d) % 4], ra1.at[t, d - 1], zp(d)))
            copies.append(remote(sb.at[t, (x + d) % 4], rb1.at[t, d - 1], xp(d)))
        return copies

    def total_of(own, others):
        total = own.astype(F32)
        for other in others:
            total = total + other.astype(F32)
        return total

    def scatter_two(t):
        sa2[t] = total_of(sa[t, z], [ra1[t, k] for k in range(3)]).astype(BF)
        sb2[t] = total_of(sb[t, x], [rb1[t, k] for k in range(3)]).astype(BF)
        copies = []
        for d in (1, 2, 3):
            copies.append(remote(sa2.at[t, (x + d) % 4], ra2.at[t, d - 1], xp(d)))
            copies.append(remote(sb2.at[t, (z + d) % 4], rb2.at[t, d - 1], zp(d)))
        return copies

    def scattered(t):
        first = total_of(sa2[t, x], [ra2[t, k] for k in range(3)])
        second = total_of(sb2[t, z], [rb2[t, k] for k in range(3)])
        return jnp.concatenate([first.astype(BF), second.astype(BF)], axis=0)

    r_one = scatter_one(0)
    arrived([m_two])
    grads[1] = ((mix_acc[1] + mix_in[1].astype(F32)) * (1 / 1024)).astype(BF)

    def back_two(i, carry):
        grad = grads[1]
        sa[1, i] = (dot(whole(wa, i), grad, NT) + back_acc[0, i]).astype(BF).reshape(4, HALF, TOK)
        sb[1, i] = (dot(whole(wb, i), grad, NT) + back_acc[1, i]).astype(BF).reshape(4, HALF, TOK)
        return carry

    lax.fori_loop(0, 4, back_two, 0)
    r_one_tan = scatter_one(1)

    def out_terms(i, carry):
        one, two = grads[0], grads[1]
        ha[i] = (
            (dot(whole(ga, 1, i), one, NN) + dot(whole(ga, 0, i), two, NN))
            .astype(BF).reshape(4, HALF, PART)
        )
        hb[i] = (
            (dot(whole(gb, 1, i), one, NN) + dot(whole(gb, 0, i), two, NN))
            .astype(BF).reshape(4, HALF, PART)
        )
        return carry

    lax.fori_loop(0, 4, out_terms, 0)
    o_core = []
    for k in range(2):
        o_core.append(remote(ha.at[:, 2 * k + 1 - c], ca.at[k], sib))
        o_core.append(remote(hb.at[2 * k + 1 - c], cb.at[k], sib))
    arrived(r_one)
    r_two = scatter_two(0)

    arrived(o_core)
    far = 1 - yh
    xa[...] = total_of(ha[:, 2 * far + c], [ca[far]]).astype(BF)
    xb[...] = total_of(hb[2 * far + c], [cb[far]]).astype(BF)
    o_crs = [remote(xa, ya, crs), remote(xb, yb, crs)]

    arrived(r_one_tan)
    r_two_tan = scatter_two(1)

    arrived(r_two)
    g = scattered(0)

    def pull_block(b, carry):
        score[:, keys_of(b)] = dot(g, gkv[b, 2 * HS : 3 * HS], TN)
        return carry

    lax.fori_loop(0, 4, pull_block, 0)
    arrived(o_crs)
    fa[...] = total_of(ha[:, s], [ca[yh], ya[...]]).astype(BF)
    fb[...] = total_of(hb[s], [cb[yh], yb[...]]).astype(BF)
    o_fin = []
    for d in (1, 2, 3):
        other = (z + d) % 4
        o_fin.append(remote(fa.at[other], oa.at[z], fin(d)))
        o_fin.append(remote(fb.at[other], ob.at[z], fin(d)))
    o_far = [
        remote(fa.at[z], oa.at[z], fin(0), begin=False),
        remote(fb.at[z], ob.at[z], fin(0), begin=False),
    ]
    near = local_count[0]
    o_near = [
        pltpu.make_async_copy(fa.at[z], oa.at[z], local.at[near]),
        pltpu.make_async_copy(fb.at[z], ob.at[z], local.at[near + 1]),
    ]

    @pl.when(x != s)
    def _():
        for copy in o_far:
            copy.start()

    @pl.when(x == s)
    def _():
        for copy in o_near:
            copy.start()

    arrived(r_two_tan)
    g_tan = scattered(1)
    g_both = jnp.concatenate([g_tan, g], axis=0)

    def pull_block_tan(b, carry):
        score_tan[:, keys_of(b)] = dot(g_both, gkv[b, 2 * HS : 4 * HS], TN)
        return carry

    lax.fori_loop(0, 4, pull_block_tan, 0)
    rnd_q, rnd_q_tan = prob, prob_tan

    def soft_back(i, carry):
        at = pl.ds(pl.multiple_of(i * 32, 32), 32)
        weights, moved = prob[at, :], prob_tan[at, :]
        pulled, pulled_tan = score[at, :], score_tan[at, :]
        base = jnp.sum(weights * pulled, axis=-1, keepdims=True)
        base_tan = jnp.sum(moved * pulled + weights * pulled_tan, axis=-1, keepdims=True)
        less = pulled - base
        score[at, :] = weights * less
        score_tan[at, :] = moved * less + weights * (pulled_tan - base_tan)
        return carry

    lax.fori_loop(0, TOK // 32, soft_back, 0)

    def cot_block(b, held):
        at = keys_of(b)
        slope, slope_tan = score[:, at].astype(BF), score_tan[:, at].astype(BF)
        ck[b, 0:HS] = ((dot(q, slope_tan, NN) + dot(q_tan, slope, NN)) * root).astype(BF)
        ck[b, HS : 2 * HS] = (dot(g, rnd_tan[:, at], NN) + dot(g_tan, rnd[:, at], NN)).astype(BF)
        return held + dot(gkv[b, 0:HS], slope_tan, NT) + dot(gkv[b, HS : 2 * HS], slope, NT)

    cot_query = lax.fori_loop(0, 4, cot_block, jnp.zeros((HS, TOK), F32)) * root
    c_core = [remote(ck.at[2 * k + 1 - c], cr.at[k], sib) for k in range(2)]
    cot[s, 0:HS] = rotate(cot_query.astype(BF).astype(F32), -sin).astype(BF)
    arrived(c_core)
    cx[...] = total_of(ck[2 * far + c], [cr[far]]).astype(BF)
    c_crs = remote(cx, cy, crs)

    arrived(o_fin)

    @pl.when(x != s)
    def _():
        for copy in o_far:
            copy.wait_recv()
            copy.wait_send()

    @pl.when(x == s)
    def _():
        for copy in o_near:
            copy.wait()

    e_base = (
        lax.broadcasted_iota(jnp.int32, (HALF, PART), 0) * D
        + lax.broadcasted_iota(jnp.int32, (HALF, PART), 1)
        + (D * WIDE + fs * HS * D + s * SHARE)
    ) * jnp.int32(MIX[0]) + seeded
    scale = math.sqrt(INNER)
    for half, ref in enumerate((oa, ob)):
        for k in range(4):
            bit = sign_bit(e_base + jnp.int32(wrap((half * HALF * D + k * PART) * MIX[0])))
            oo[half * HALF : (half + 1) * HALF, k * PART : (k + 1) * PART] = ref[k].astype(
                F32
            ) * jnp.where(bit == 0, F32(scale), F32(-scale))

    arrived([c_crs])
    both = total_of(ck[s], [cr[yh], cy[...]])
    cot[s, HS : 2 * HS] = rotate(both[:HS].astype(BF).astype(F32), -sin).astype(BF)
    cot[s, 2 * HS : 3 * HS] = both[HS:].astype(BF)
    t_crs = remote(cot.at[s], cot.at[s], crs)
    t_sib = remote(cot.at[s], cot.at[s], sib)

    def share_rows(i):
        return pl.ds(pl.multiple_of(i * TOK, TOK), TOK)

    def first_term(i, carry):
        oq[share_rows(i), :] = dot(nt[s, share_rows(i), :], cot[s], NT)
        return carry

    lax.fori_loop(0, SHARE // TOK, first_term, 0)
    arrived([t_sib])

    def second_term(i, carry):
        oq[share_rows(i), :] += dot(nt[s_sib, share_rows(i), :], cot[s_sib], NT)
        return carry

    lax.fori_loop(0, SHARE // TOK, second_term, 0)
    arrived([t_crs])
    t_rel = remote(cot.at[s_crs], cot.at[s_crs], sib)

    def third_term(i, carry):
        oq[share_rows(i), :] += dot(nt[s_crs, share_rows(i), :], cot[s_crs], NT)
        return carry

    lax.fori_loop(0, SHARE // TOK, third_term, 0)
    arrived([t_rel])

    def last_term(i, carry):
        at = share_rows(i)
        oq[at, :] = (oq[at, :] + dot(nt[s_crd, at, :], cot[s_crd], NT)) * sgn[at, :]
        return carry

    lax.fori_loop(0, SHARE // TOK, last_term, 0)
    for copy in sent:
        copy.wait_send()


def tables():
    rate = 10000.0 ** (-2.0 * np.arange(ROT // 2) / ROT)
    rate = np.concatenate([rate, rate])[:, None]
    within = np.arange(TOK)[None, :] * rate
    blocks = np.arange(4)[:, None, None] * float(TOK) * rate[None] + np.zeros((1, 1, TOK))
    tab_t = np.stack([np.cos(within), np.sin(within)]).astype(np.float32)
    tab_b = np.stack([np.cos(blocks), np.sin(blocks)], axis=1).astype(np.float32)
    return tab_t, tab_b


def per_device(tokens, target, norm_gain, qkv_weight, out_weight, probe_seed, block_order):
    tab_t, tab_b = tables()
    anywhere = pl.BlockSpec(memory_space=pl.ANY)
    vmem = pl.BlockSpec(memory_space=pltpu.VMEM)
    smem = pl.BlockSpec(memory_space=pltpu.SMEM)
    v = pltpu.VMEM
    scratch = [
        v((TOK, D), BF), v((TOK, PART), BF), v((D, COLS), BF), v((TOK, D), BF), v((2, TOK, 384), F32),
        v((4, TOK, SHARE), BF), v((4, SHARE, TOK), BF), v((4, 4 * HS + 16, TOK), BF),
        v((4, HALF, SHARE), BF), v((4, 4, HALF, PART), BF),
        v((4, 4, HALF, PART), BF), v((4, 4, HALF, PART), BF),
        v((4, 4, HALF, PART), BF), v((4, 4, HALF, PART), BF),
        v((2, 4, 4, HALF, TOK), BF), v((2, 4, 4, HALF, TOK), BF),
        v((TOK, 1024), F32), v((TOK, 1024), F32), v((TOK, 1024), F32), v((TOK, 1024), F32),
        v((TOK, 1024), BF), v((TOK, 1024), BF),
        v((2, TOK, PART), F32), v((2, TOK, PART), BF), v((2, TOK, PART), BF), v((2, TOK, PART), BF),
        v((2, 4, 4 * HALF, TOK), F32),
        v((2, 4, 4, HALF, TOK), BF), v((2, 4, 4, HALF, TOK), BF),
        v((2, 3, 4, HALF, TOK), BF), v((2, 3, 4, HALF, TOK), BF),
        v((2, 4, HALF, TOK), BF), v((2, 4, HALF, TOK), BF),
        v((2, 3, HALF, TOK), BF), v((2, 3, HALF, TOK), BF),
        v((4, 4, HALF, PART), BF), v((4, 4, HALF, PART), BF),
        v((2, 4, HALF, PART), BF), v((2, 4, HALF, PART), BF),
        v((4, HALF, PART), BF), v((4, HALF, PART), BF), v((4, HALF, PART), BF), v((4, HALF, PART), BF),
        v((4, HALF, PART), BF), v((4, HALF, PART), BF), v((4, HALF, PART), BF), v((4, HALF, PART), BF),
        v((4, 2 * HS, TOK), BF), v((2, 2 * HS, TOK), BF), v((2 * HS, TOK), BF), v((2 * HS, TOK), BF),
        v((4, 3 * HS, TOK), BF), v((SHARE, COLS), F32),
        pltpu.SemaphoreType.DMA((N_REMOTE,)), pltpu.SemaphoreType.DMA((N_REMOTE,)),
        pltpu.SemaphoreType.DMA((N_LOCAL,)),
    ]
    return pl.pallas_call(
        kernel,
        out_shape=(
            jax.ShapeDtypeStruct((SHARE, COLS), F32),
            jax.ShapeDtypeStruct((HS, SHARE), F32),
        ),
        in_specs=[anywhere, anywhere, vmem, anywhere, anywhere, smem, smem, vmem, vmem],
        out_specs=(vmem, vmem),
        scratch_shapes=scratch,
        compiler_params=pltpu.CompilerParams(
            collective_id=0, has_side_effects=True, vmem_limit_bytes=60 * 2**20
        ),
    )(
        tokens, target, norm_gain.reshape(1, D), qkv_weight, out_weight, probe_seed, block_order,
        jnp.asarray(tab_t), jnp.asarray(tab_b),
    )


def solution(mesh):
    placed = (P("seq", None), P("seq", None), P(), P(None, "fsdp"), P("fsdp", None), P(), P("seq"))
    return jax.shard_map(
        per_device,
        mesh=mesh,
        in_specs=placed,
        out_specs=(P("seq", "fsdp"), P("fsdp", "seq")),
        check_vma=False,
    )
```

time: 611 us -> 117 us (0.19)
  waiting for transfers between devices: 470 us -> 0 us
  Pallas kernels: 0 us -> 104 us
  matrix products: 47.7 us -> 0 us
  blocking collectives: 36.8 us -> 0 us
  other arithmetic: 30.3 us -> 0 us
  between operations: 16.4 us -> 1.94 us
    psum x1 -> x0, waiting for transfers between devices: 349 us -> none  [per_device(): mixed, mixed_tan = lax.psum((mixed_part, mixed_tan_part), 'fsdp')]
    reduce_scatter x4 -> x0, waiting for transfers between devices: 121 us -> none  [the longest x1 47.5 us: per_device(): lax.psum_scatter(jnp.dot(normed.T, cot_rounded, preferred_element_type=jn...]
    pallas_call x0 -> x1, Pallas kernels: none -> 104 us  [per_device(): pl.pallas_call(kernel, out_shape=(jax.ShapeDtypeStruct((SHARE, COLS), F32...]
    dot_general x26 -> x0, matrix products: 47.7 us -> none  [the longest x1 7.33 us: per_device(): qkv_tan = jnp.dot(normed, qkv_probe, preferred_element_type=jnp.float32)]
    all_gather x4 -> x0, blocking collectives: 31 us -> none  [the longest x1 8.43 us: per_device(): lax.all_gather(own_parts[1], 'seq', axis=0, tiled=True)]
    convert_element_type x7 -> x0, other arithmetic: 17.7 us -> none  [the longest x2 9.14 us: probe_signs(): return (1 - 2 * chosen).astype(jnp.float32)]
  transfers between devices with their start and end apart: 5 -> 0, of which waited for: 5 -> 0; matrix products, arithmetic and copies ran while one was open for 5% -> 0% of each run, Pallas kernels for 0% -> 0%
where the time goes in v1:
time: 117 us; the launch traced here: 116 us
  Pallas kernels  104 us (89%)
  local copies, waits for them, and re-layouts  10 us (9%)
  between operations  1.94 us (2%)
    pallas_call x1, Pallas kernels, per_device(): pl.pallas_call(kernel, out_shape=(jax.ShapeDtypeStruct((SHARE, COLS), F32...  104 us
    unnamed x4, local copies, waits for them, and re-layouts  7.09 us
    pallas_call x1, local copies, waits for them, and re-layouts, per_device(): pl.pallas_call(kernel, out_shape=(jax.ShapeDtypeStruct((SHARE, COLS), F32...  2.95 us

profile of v1, /device:TPU:1, one launch (start us, length us, event | category | flops | bytes accessed | tf_op | source)
XLA Modules:
  0.0 115.7 jit_solution(17164751401598155238)
XLA Ops:
  1.9 6.3 %copy.11.wq_in = bf16[6144,288]{1,0:T(8,128)(2,1)} copy(bf16[6144,288]{0,1:T(8,128)(2,1)} %param.12) | data formatting | bytes 7077888 | tf_op args[3]
  8.2 103.7 %shard_map.104 = (f32[1536,288]{1,0:T(8,128)}, f32[96,1536]{1,0:T(8,128)}) custom-call(bf16[256,6144]{1,0:T(8,128)(2,1)} %tok_in.1, bf16[256,6144]{1,0:T(8,128)(2,1)} %tgt_in.1, f32[1,6144]{1,0:T(1,128)} %bitcast.1, bf16[6144,288]{1,0:T(8,128)(2,1)} %copy.11.wq_in, bf16[96,6144]{1,0:T(8,128)(2,1)} %wo_in.1, s32[1]{0:T(128)S(6)} %copy.14.seed, ...), custom_call_target="tpu_custom_call" | custom-call | tf_op jit(solution)/shard_map/pallas_call | solution.py:703
  111.9 0.0 copy-start
  111.9 2.9 %copy.12 = f32[1536,288]{0,1:T(8,128)} copy(f32[1536,288]{1,0:T(8,128)} %get-tuple-element.2) | data formatting | bytes 3538944 | tf_op jit(solution)/shard_map/pallas_call | solution.py:703
  114.9 0.0 copy-done
  114.9 0.8 copy.16
Async XLA Ops:
  111.9 3.0 %copy-start = (f32[96,1536]{1,0:T(8,128)S(1)}, f32[96,1536]{1,0:T(8,128)}, u32[]{:S(2)}) copy-start(f32[96,1536]{1,0:T(8,128)} %get-tuple-element.7) | copy-start | bytes 1769476

commit v2 on v1

--- a/solution.py
+++ b/solution.py
@@ -22,6 +22,7 @@
 SHARE = 1536
 PART = 384
 HALF = 48
+STEP = 768
 MIX = (-1640531535, -2048144789, -1028477387)
 N_REMOTE = 136
 N_LOCAL = 16
@@ -56,7 +57,7 @@
     tok_in, tgt_in, gain, wq_in, wo_in, seed, block, tab_t, tab_b,
     oq, oo,
     tok, tgt, wq, nrm, acc,
-    nb, nt, gkv, ta, tb, wa, wb, pa, pb, ga, gb,
+    nb, gkv, ta, tb, wa, wb, pa, pb, ga, gb,
     score, score_tan, prob, prob_tan, rnd, rnd_tan,
     mix_acc, mix_out, mix_in, grads, back_acc,
     sa, sb, ra1, rb1, sa2, sb2, ra2, rb2,
@@ -195,20 +196,20 @@
     seeded = seed[0]
     q_probe = float(np.float32(1 / math.sqrt(D)).astype(jnp.bfloat16))
     o_probe = float(np.float32(1 / math.sqrt(INNER)).astype(jnp.bfloat16))
-    q_rows = lax.broadcasted_iota(jnp.int32, (TOK, COLS), 0)
-    q_cols = lax.broadcasted_iota(jnp.int32, (TOK, COLS), 1)
+    q_rows = lax.broadcasted_iota(jnp.int32, (COLS, STEP), 1)
+    q_cols = lax.broadcasted_iota(jnp.int32, (COLS, STEP), 0)
     q_base = (q_rows * WIDE + q_cols + fs * COLS) * jnp.int32(MIX[0]) + seeded
 
     def project(i, carry):
-        at = pl.ds(pl.multiple_of(i * TOK, TOK), TOK)
-        bit = sign_bit(q_base + i * jnp.int32(wrap(TOK * WIDE * MIX[0])))
+        at = pl.ds(pl.multiple_of(i * STEP, STEP), STEP)
+        bit = sign_bit(q_base + i * jnp.int32(wrap(STEP * WIDE * MIX[0])))
         probe = jnp.where(bit == 0, F32(q_probe), F32(-q_probe)).astype(BF)
-        left = nrm[:, pl.ds(pl.multiple_of(i * TOK, TOK), TOK)]
-        acc[0, :, pl.ds(0, COLS)] += dot(left, wq[at, :], NN)
-        acc[1, :, pl.ds(0, COLS)] += dot(left, probe, NN)
-        return carry
-
-    lax.fori_loop(0, D // TOK, project, 0)
+        right = nrm[:, at]
+        acc[0] += dot(wq[:, at], right, NT)
+        acc[1] += dot(probe, right, NT)
+        return carry
+
+    lax.fori_loop(0, D // STEP, project, 0)
 
     number = block[0]
     cos_b = jnp.zeros((ROT, TOK), F32)
@@ -229,7 +230,7 @@
 
     fields = []
     for k in range(2):
-        turned = acc[k].T
+        turned = acc[k]
         fields.append(
             (
                 rotate(turned[0:HS], sin).astype(BF),
@@ -371,23 +372,6 @@
     arrived(g_one_tan)
     g_two_tan = gather_two(1)
 
-
-    arrived([n_sib] + n_two)
-
-    def turn_own(i, carry):
-        nt[s, pl.ds(pl.multiple_of(i * TOK, TOK), TOK), :] = nrm[:, lanes(s * SHARE + i * TOK, TOK)].T
-        return carry
-
-    lax.fori_loop(0, SHARE // TOK, turn_own, 0)
-
-    def turn_other(i, carry):
-        b = (s + 1 + i // 6) % 4
-        k = i % 6
-        nt[b, pl.ds(pl.multiple_of(k * TOK, TOK), TOK), :] = nb[b, :, lanes(k * TOK, TOK)].T
-        return carry
-
-    lax.fori_loop(0, 18, turn_other, 0)
-
     own_wa.wait()
     own_wb.wait()
     arrived(w_two)
@@ -419,19 +403,17 @@
     m_two = remote(mix_out.at[1], mix_in.at[1], partner)
 
     s_base = (
-        (lax.broadcasted_iota(jnp.int32, (128, COLS), 0) + s * SHARE) * WIDE
-        + lax.broadcasted_iota(jnp.int32, (128, COLS), 1)
+        (lax.broadcasted_iota(jnp.int32, (COLS, TOK), 1) + s * SHARE) * WIDE
+        + lax.broadcasted_iota(jnp.int32, (COLS, TOK), 0)
         + fs * COLS
     ) * jnp.int32(MIX[0]) + seeded
 
-    def sign_rows(i, carry):
-        bit = sign_bit(s_base + i * jnp.int32(wrap(128 * WIDE * MIX[0])))
-        sgn[pl.ds(pl.multiple_of(i * 128, 128), 128), :] = jnp.where(
-            bit == 0, F32(math.sqrt(D)), F32(-math.sqrt(D))
-        )
-        return carry
-
-    lax.fori_loop(0, SHARE // 128, sign_rows, 0)
+    def sign_cols(i, carry):
+        bit = sign_bit(s_base + i * jnp.int32(wrap(TOK * WIDE * MIX[0])))
+        sgn[:, lanes(i * TOK, TOK)] = jnp.where(bit == 0, F32(math.sqrt(D)), F32(-math.sqrt(D)))
+        return carry
+
+    lax.fori_loop(0, SHARE // TOK, sign_cols, 0)
 
     tgt_load.wait()
     arrived([m_one])
@@ -563,7 +545,6 @@
         return carry
 
     lax.fori_loop(0, 4, pull_block_tan, 0)
-    rnd_q, rnd_q_tan = prob, prob_tan
 
     def soft_back(i, carry):
         at = pl.ds(pl.multiple_of(i * 32, 32), 32)
@@ -625,34 +606,32 @@
     t_crs = remote(cot.at[s], cot.at[s], crs)
     t_sib = remote(cot.at[s], cot.at[s], sib)
 
-    def share_rows(i):
-        return pl.ds(pl.multiple_of(i * TOK, TOK), TOK)
+    arrived([n_sib] + n_two)
 
     def first_term(i, carry):
-        oq[share_rows(i), :] = dot(nt[s, share_rows(i), :], cot[s], NT)
+        oq[:, lanes(i * TOK, TOK)] = dot(cot[s], nrm[:, lanes(s * SHARE + i * TOK, TOK)], NN)
         return carry
 
     lax.fori_loop(0, SHARE // TOK, first_term, 0)
     arrived([t_sib])
 
-    def second_term(i, carry):
-        oq[share_rows(i), :] += dot(nt[s_sib, share_rows(i), :], cot[s_sib], NT)
-        return carry
-
-    lax.fori_loop(0, SHARE // TOK, second_term, 0)
+    def next_term(b):
+        def term(i, carry):
+            at = lanes(i * TOK, TOK)
+            oq[:, at] += dot(cot[b], nb[b, :, at], NN)
+            return carry
+
+        lax.fori_loop(0, SHARE // TOK, term, 0)
+
+    next_term(s_sib)
     arrived([t_crs])
     t_rel = remote(cot.at[s_crs], cot.at[s_crs], sib)
-
-    def third_term(i, carry):
-        oq[share_rows(i), :] += dot(nt[s_crs, share_rows(i), :], cot[s_crs], NT)
-        return carry
-
-    lax.fori_loop(0, SHARE // TOK, third_term, 0)
+    next_term(s_crs)
     arrived([t_rel])
 
     def last_term(i, carry):
-        at = share_rows(i)
-        oq[at, :] = (oq[at, :] + dot(nt[s_crd, at, :], cot[s_crd], NT)) * sgn[at, :]
+        at = lanes(i * TOK, TOK)
+        oq[:, at] = (oq[:, at] + dot(cot[s_crd], nb[s_crd, :, at], NN)) * sgn[:, at]
         return carry
 
     lax.fori_loop(0, SHARE // TOK, last_term, 0)
@@ -677,8 +656,8 @@
     smem = pl.BlockSpec(memory_space=pltpu.SMEM)
     v = pltpu.VMEM
     scratch = [
-        v((TOK, D), BF), v((TOK, PART), BF), v((D, COLS), BF), v((TOK, D), BF), v((2, TOK, 384), F32),
-        v((4, TOK, SHARE), BF), v((4, SHARE, TOK), BF), v((4, 4 * HS + 16, TOK), BF),
+        v((TOK, D), BF), v((TOK, PART), BF), v((COLS, D), BF), v((TOK, D), BF), v((2, COLS, TOK), F32),
+        v((4, TOK, SHARE), BF), v((4, 4 * HS + 16, TOK), BF),
         v((4, HALF, SHARE), BF), v((4, 4, HALF, PART), BF),
         v((4, 4, HALF, PART), BF), v((4, 4, HALF, PART), BF),
         v((4, 4, HALF, PART), BF), v((4, 4, HALF, PART), BF),
@@ -696,14 +675,14 @@
         v((4, HALF, PART), BF), v((4, HALF, PART), BF), v((4, HALF, PART), BF), v((4, HALF, PART), BF),
         v((4, HALF, PART), BF), v((4, HALF, PART), BF), v((4, HALF, PART), BF), v((4, HALF, PART), BF),
         v((4, 2 * HS, TOK), BF), v((2, 2 * HS, TOK), BF), v((2 * HS, TOK), BF), v((2 * HS, TOK), BF),
-        v((4, 3 * HS, TOK), BF), v((SHARE, COLS), F32),
+        v((4, 3 * HS, TOK), BF), v((COLS, SHARE), F32),
         pltpu.SemaphoreType.DMA((N_REMOTE,)), pltpu.SemaphoreType.DMA((N_REMOTE,)),
         pltpu.SemaphoreType.DMA((N_LOCAL,)),
     ]
-    return pl.pallas_call(
+    product, out_curv = pl.pallas_call(
         kernel,
         out_shape=(
-            jax.ShapeDtypeStruct((SHARE, COLS), F32),
+            jax.ShapeDtypeStruct((COLS, SHARE), F32),
             jax.ShapeDtypeStruct((HS, SHARE), F32),
         ),
         in_specs=[anywhere, anywhere, vmem, anywhere, anywhere, smem, smem, vmem, vmem],
@@ -713,9 +692,10 @@
             collective_id=0, has_side_effects=True, vmem_limit_bytes=60 * 2**20
         ),
     )(
-        tokens, target, norm_gain.reshape(1, D), qkv_weight, out_weight, probe_seed, block_order,
+        tokens, target, norm_gain.reshape(1, D), qkv_weight.T, out_weight, probe_seed, block_order,
         jnp.asarray(tab_t), jnp.asarray(tab_b),
     )
+    return product.T, out_curv
 
 
 def solution(mesh):

time: 117 us -> 105 us (0.90)
  local copies, waits for them, and re-layouts: 10 us -> 3.68 us
  Pallas kernels: 104 us -> 98.4 us
    pallas_call x1, Pallas kernels: 104 us -> 98.4 us  [per_device(): pl.pallas_call(kernel, out_shape=(jax.ShapeDtypeStruct((COLS, SHARE), F32...]
    unnamed x4, local copies, waits for them, and re-layouts: 7.09 us -> 3.68 us
    pallas_call x1 -> x0, local copies, waits for them, and re-layouts: 2.95 us -> none  [per_device(): pl.pallas_call(kernel, out_shape=(jax.ShapeDtypeStruct((SHARE, COLS), F32...]
where the time goes in v2:
time: 105 us; the launch traced here: 104 us
  Pallas kernels  98.4 us (94%)
  local copies, waits for them, and re-layouts  3.68 us (4%)
  between operations  1.94 us (2%)
    pallas_call x1, Pallas kernels, per_device(): pl.pallas_call(kernel, out_shape=(jax.ShapeDtypeStruct((COLS, SHARE), F32...  98.4 us
    unnamed x4, local copies, waits for them, and re-layouts  3.68 us

profile of v2, /device:TPU:1, one launch (start us, length us, event | category | flops | bytes accessed | tf_op | source)
XLA Modules:
  0.0 104.0 jit_solution(10488936120363901958)
XLA Ops:
  1.9 98.4 %shard_map.104 = (f32[288,1536]{1,0:T(8,128)}, f32[96,1536]{1,0:T(8,128)}) custom-call(bf16[256,6144]{1,0:T(8,128)(2,1)} %tok_in.1, bf16[256,6144]{1,0:T(8,128)(2,1)} %tgt_in.1, f32[1,6144]{1,0:T(1,128)} %bitcast.5, bf16[288,6144]{1,0:T(8,128)(2,1)} %bitcast.3, bf16[96,6144]{1,0:T(8,128)(2,1)} %wo_in.1, s32[1]{0:T(128)S(6)} %copy.13.seed, s32[1]{0:T(128)S(6)} %copy.14.block, ...), custom_call_target="tpu_custom_call" | custom-call | tf_op jit(solution)/shard_map/pallas_call | solution.py:682
  100.3 0.0 copy-start
  100.4 2.9 %copy.15 = f32[1536,288]{0,1:T(8,128)} copy(f32[1536,288]{0,1:T(8,128)} %bitcast.4) | data formatting | bytes 3538944
  103.2 0.0 copy-done
  103.2 0.8 copy.16
Async XLA Ops:
  100.3 2.9 %copy-start = (f32[96,1536]{1,0:T(8,128)S(1)}, f32[96,1536]{1,0:T(8,128)}, u32[]{:S(2)}) copy-start(f32[96,1536]{1,0:T(8,128)} %get-tuple-element.9) | copy-start | bytes 1769476

commit v3 on v2

--- a/solution.py
+++ b/solution.py
@@ -22,6 +22,7 @@
 SHARE = 1536
 PART = 384
 HALF = 48
+KEYS = 2 * HS + 16
 STEP = 768
 MIX = (-1640531535, -2048144789, -1028477387)
 N_REMOTE = 136
@@ -57,12 +58,13 @@
     tok_in, tgt_in, gain, wq_in, wo_in, seed, block, tab_t, tab_b,
     oq, oo,
     tok, tgt, wq, nrm, acc,
-    nb, gkv, ta, tb, wa, wb, pa, pb, ga, gb,
+    stat, nb, gkv,
+    wt, ww, pa, pb, ga, gb,
     score, score_tan, prob, prob_tan, rnd, rnd_tan,
     mix_acc, mix_out, mix_in, grads, back_acc,
     sa, sb, ra1, rb1, sa2, sb2, ra2, rb2,
     ha, hb, ca, cb, xa, xb, ya, yb, fa, fb, oa, ob,
-    ck, cr, cx, cy, cot, sgn,
+    cv, cvr, cvs, cvf, ck, ckr, cks, ckf, cot, sgn, part,
     send, recv, local,
 ):
     fs = lax.axis_index("fsdp")
@@ -131,9 +133,13 @@
     tok_load = stay(tok_in, tok)
     wq_load = stay(wq_in, wq)
     tgt_load = stay(tgt_in.at[:, lanes(own_cols, PART)], tgt)
-    own_ta = stay(wo_in.at[pl.ds(0, HALF), lanes(x * SHARE, SHARE)], ta.at[x])
-    own_tb = [
-        stay(wo_in.at[pl.ds(HALF, HALF), lanes((k * 4 + z) * PART, PART)], tb.at[z, k])
+    first, second = jnp.where(c == 0, x, z), jnp.where(c == 0, z, x)
+
+    def column(a, k):
+        return jnp.where(c == 0, a * 4 + k, k * 4 + a) * PART
+
+    own_w = [
+        stay(wo_in.at[rows(c * HALF, HALF), lanes(column(first, k), PART)], wt.at[first, k])
         for k in range(4)
     ]
 
@@ -153,100 +159,140 @@
         for d in range(4):
             greet(fin(d))
 
+    tok_load.wait()
+
+    def norm_sums(i, carry):
+        at = rows(i * 16, 16)
+        totals = [jnp.zeros((16, 128), F32) for _ in range(2)]
+        for k in range(D // 128):
+            totals[k % 2] += tok[at, k * 128 : (k + 1) * 128].astype(F32)
+        stat[0, at, :] = totals[0] + totals[1]
+        return carry
+
+    lax.fori_loop(0, TOK // 16, norm_sums, 0)
+    average = jnp.sum(stat[0], axis=-1, keepdims=True) * (1 / D)
+    stat[0] = jnp.broadcast_to(average, (TOK, 128))
+
+    def norm_squares(i, carry):
+        at = rows(i * 16, 16)
+        middle = stat[0, at, :]
+        totals = [jnp.zeros((16, 128), F32) for _ in range(2)]
+        for k in range(D // 128):
+            centred = tok[at, k * 128 : (k + 1) * 128].astype(F32) - middle
+            totals[k % 2] += centred * centred
+        stat[1, at, :] = totals[0] + totals[1]
+        return carry
+
+    lax.fori_loop(0, TOK // 16, norm_squares, 0)
+    spread = jnp.sum(stat[1], axis=-1, keepdims=True) * (1 / D)
+    stat[1] = jnp.broadcast_to(lax.rsqrt(spread + 1e-05), (TOK, 128))
+
     pl.semaphore_wait(barrier, jnp.where(x != s, 14, 10))
+
+    def along_first(d):
+        return device(
+            jnp.where(c == 0, (x + d) % 4, x), yl, jnp.where(c == 0, z, (z + d) % 4), s
+        )
+
+    def along_second(d):
+        return device(
+            jnp.where(c == 0, x, (x + d) % 4), yl, jnp.where(c == 0, (z + d) % 4, z), s
+        )
 
     w_one = []
     for d in (1, 2, 3):
-        other = (x + d) % 4
-        w_one.append(
-            remote(wo_in.at[pl.ds(0, HALF), lanes(other * SHARE, SHARE)], ta.at[x], xp(d))
-        )
-        other = (z + d) % 4
         for k in range(4):
             w_one.append(
                 remote(
-                    wo_in.at[pl.ds(HALF, HALF), lanes((k * 4 + other) * PART, PART)],
-                    tb.at[z, k], zp(d),
+                    wo_in.at[rows(c * HALF, HALF), lanes(column((first + d) % 4, k), PART)],
+                    wt.at[first, k], along_first(d),
                 )
             )
 
-    tok_load.wait()
-
     def norm_rows(i, carry):
         at = rows(i * 16, 16)
-        values = tok[at, :].astype(F32)
-        centred = values - jnp.mean(values, axis=-1, keepdims=True)
-        spread = jnp.mean(centred * centred, axis=-1, keepdims=True)
-        nrm[at, :] = (centred * lax.rsqrt(spread + 1e-05) * gain[...]).astype(BF)
+        middle, factor = stat[0, at, :], stat[1, at, :]
+        for k in range(D // 128):
+            cols = slice(k * 128, (k + 1) * 128)
+            nrm[at, cols] = ((tok[at, cols].astype(F32) - middle) * factor * gain[:, cols]).astype(BF)
         return carry
 
     lax.fori_loop(0, TOK // 16, norm_rows, 0)
 
     piece = jnp.where(c == 0, z * 4 + x, x * 4 + z) * 16
-    n_sib = remote(nrm.at[:, lanes(s_sib * SHARE, SHARE)], nb.at[s], sib)
     n_crs = remote(
         nrm.at[rows(piece, 16), lanes(s_crs * SHARE, SHARE)], nb.at[s, rows(piece, 16)], crs
     )
     n_crd = remote(
         nrm.at[rows(piece, 16), lanes(s_crd * SHARE, SHARE)], nb.at[s, rows(piece, 16)], crd
     )
+    n_sib = remote(nrm.at[:, lanes(s_sib * SHARE, SHARE)], nb.at[s], sib)
 
     wq_load.wait()
     acc[...] = jnp.zeros_like(acc)
     seeded = seed[0]
     q_probe = float(np.float32(1 / math.sqrt(D)).astype(jnp.bfloat16))
     o_probe = float(np.float32(1 / math.sqrt(INNER)).astype(jnp.bfloat16))
-    q_rows = lax.broadcasted_iota(jnp.int32, (COLS, STEP), 1)
-    q_cols = lax.broadcasted_iota(jnp.int32, (COLS, STEP), 0)
-    q_base = (q_rows * WIDE + q_cols + fs * COLS) * jnp.int32(MIX[0]) + seeded
-
-    def project(i, carry):
-        at = pl.ds(pl.multiple_of(i * STEP, STEP), STEP)
-        bit = sign_bit(q_base + i * jnp.int32(wrap(STEP * WIDE * MIX[0])))
-        probe = jnp.where(bit == 0, F32(q_probe), F32(-q_probe)).astype(BF)
-        right = nrm[:, at]
-        acc[0] += dot(wq[:, at], right, NT)
-        acc[1] += dot(probe, right, NT)
-        return carry
-
-    lax.fori_loop(0, D // STEP, project, 0)
+
+    def project(start, size):
+        q_rows = lax.broadcasted_iota(jnp.int32, (size, STEP), 1)
+        q_cols = lax.broadcasted_iota(jnp.int32, (size, STEP), 0)
+        q_base = (q_rows * WIDE + q_cols + (fs * COLS + start)) * jnp.int32(MIX[0]) + seeded
+        to = pl.ds(start, size)
+
+        def step(i, carry):
+            at = pl.ds(pl.multiple_of(i * STEP, STEP), STEP)
+            bit = sign_bit(q_base + i * jnp.int32(wrap(STEP * WIDE * MIX[0])))
+            probe = jnp.where(bit == 0, F32(q_probe), F32(-q_probe)).astype(BF)
+            both = dot(jnp.concatenate([wq[to, at], probe], axis=0), nrm[:, at], NT)
+            acc[0, to] += both[:size]
+            acc[1, to] += both[size:]
+            return carry
+
+        lax.fori_loop(0, D // STEP, step, 0)
+
+    project(HS, 2 * HS)
 
     number = block[0]
-    cos_b = jnp.zeros((ROT, TOK), F32)
-    sin_b = jnp.zeros((ROT, TOK), F32)
-    for k in range(4):
-        here = jnp.full((ROT, TOK), number, jnp.int32) == k
-        cos_b = jnp.where(here, tab_b[k, 0], cos_b)
-        sin_b = jnp.where(here, tab_b[k, 1], sin_b)
-    cos = cos_b * tab_t[0] - sin_b * tab_t[1]
-    sin = sin_b * tab_t[0] + cos_b * tab_t[1]
     low = lax.broadcasted_iota(jnp.int32, (ROT, TOK), 0) < ROT // 2
-    sin = jnp.where(low, -sin, sin)
-
-    def rotate(field, turn):
+
+    def trig(here):
+        cos_b = jnp.zeros((ROT, TOK), F32)
+        sin_b = jnp.zeros((ROT, TOK), F32)
+        for k in range(4):
+            cos_b = jnp.where(here == k, tab_b[k, 0], cos_b)
+            sin_b = jnp.where(here == k, tab_b[k, 1], sin_b)
+        cos = cos_b * tab_t[0] - sin_b * tab_t[1]
+        sin = sin_b * tab_t[0] + cos_b * tab_t[1]
+        return cos, jnp.where(low, -sin, sin)
+
+    own_trig = trig(jnp.full((ROT, TOK), number, jnp.int32))
+
+    def rotate(field, turns, sign=1.0):
+        cos, sin = turns
         head = field[:ROT]
         swapped = pltpu.roll(head, ROT // 2, 0)
-        return jnp.concatenate([head * cos + swapped * turn, field[ROT:]], axis=0)
-
-    fields = []
+        return jnp.concatenate([head * cos + swapped * (sin * sign), field[ROT:]], axis=0)
+
     for k in range(2):
-        turned = acc[k]
-        fields.append(
-            (
-                rotate(turned[0:HS], sin).astype(BF),
-                rotate(turned[HS : 2 * HS], sin).astype(BF),
-                turned[2 * HS : 3 * HS].astype(BF),
-            )
-        )
-    q, q_tan = fields[0][0], fields[1][0]
+        gkv[s, k * HS : (k + 1) * HS] = rotate(acc[k, HS : 2 * HS], own_trig).astype(BF)
+    gkv[s, KEYS - 16 : KEYS] = jnp.full((16, TOK), number, jnp.int32).astype(F32).astype(BF)
+    k_part, v_part = pl.ds(0, KEYS), pl.ds(KEYS, 2 * HS)
+
+    def spread_kv(slot, part, to):
+        return remote(gkv.at[slot, part], gkv.at[slot, part], to)
+
+    k_crs = spread_kv(s, k_part, crs)
+    k_sib = spread_kv(s, k_part, sib)
+    for k in range(2):
+        gkv[s, KEYS + k * HS : KEYS + (k + 1) * HS] = acc[k, 2 * HS : 3 * HS].astype(BF)
+    v_crs = spread_kv(s, v_part, crs)
+    v_sib = spread_kv(s, v_part, sib)
+
+    project(0, HS)
+    q = rotate(acc[0, :HS], own_trig).astype(BF)
+    q_tan = rotate(acc[1, :HS], own_trig).astype(BF)
     q_both = jnp.concatenate([q_tan, q], axis=0)
-    gkv[s, 0:HS] = fields[0][1]
-    gkv[s, HS : 2 * HS] = fields[1][1]
-    gkv[s, 2 * HS : 3 * HS] = fields[0][2]
-    gkv[s, 3 * HS : 4 * HS] = fields[1][2]
-    gkv[s, 4 * HS : 4 * HS + 16] = jnp.full((16, TOK), number, jnp.int32).astype(F32).astype(BF)
-    kv_crs = remote(gkv.at[s], gkv.at[s], crs)
-    kv_sib = remote(gkv.at[s], gkv.at[s], sib)
 
     b0 = (1 - yh) * 2
     b1 = b0 + 1
@@ -258,17 +304,13 @@
         n_one.append(remote(at0, at0, xp(d)))
         n_one.append(remote(at1, at1, zp(d)))
 
-    for copy in [own_ta] + own_tb:
+    for copy in own_w:
         copy.wait()
     arrived(w_one)
     w_two = []
     for d in (1, 2, 3):
-        other = (z + d) % 4
-        w_two.append(remote(ta.at[:, :, lanes(other * PART, PART)], wa.at[z], zp(d)))
-        other = (x + d) % 4
-        w_two.append(remote(tb.at[:, other], wb.at[x], xp(d)))
-    own_wa = stay(ta.at[:, :, lanes(z * PART, PART)], wa.at[z])
-    own_wb = stay(tb.at[:, x], wb.at[x])
+        w_two.append(remote(wt.at[:, (second + d) % 4], ww.at[c, second], along_second(d)))
+    own_ww = stay(wt.at[:, second], ww.at[c, second])
 
     o_rows = lax.broadcasted_iota(jnp.int32, (HALF, PART), 0)
     o_lanes = lax.broadcasted_iota(jnp.int32, (HALF, PART), 1)
@@ -286,18 +328,15 @@
 
     lax.fori_loop(0, 4, probe_piece, 0)
 
-    arrived([kv_crs])
-    kv_rel = remote(gkv.at[s_crs], gkv.at[s_crs], sib)
-
-    arrived(n_one)
-    n_two = []
-    for d in (1, 2, 3):
-        at0 = nb.at[b0, rows(z * 64, 64)]
-        at1 = nb.at[b1, rows(x * 64, 64)]
-        n_two.append(remote(at0, at0, zp(d)))
-        n_two.append(remote(at1, at1, xp(d)))
-
-    arrived([kv_sib, kv_rel])
+    arrived([k_crs])
+    k_rel = spread_kv(s_crs, k_part, sib)
+    arrived([v_crs])
+    v_rel = spread_kv(s_crs, v_part, sib)
+    own_ww.wait()
+    arrived(w_two)
+    w_sib = remote(ww.at[c], ww.at[c], sib)
+
+    arrived([k_sib, k_rel])
     root = 1 / math.sqrt(HS)
 
     def keys_of(b):
@@ -311,7 +350,7 @@
     lax.fori_loop(0, 4, score_block, 0)
     along = lax.broadcasted_iota(jnp.int32, (1, TOK), 1).astype(F32)
     key_pos = jnp.concatenate(
-        [gkv[b, 4 * HS : 4 * HS + 16].astype(F32)[0:1] * float(TOK) + along for b in range(4)], axis=1
+        [gkv[b, KEYS - 16 : KEYS].astype(F32)[0:1] * float(TOK) + along for b in range(4)], axis=1
     )
     number_f = jnp.full((32, 1), number, jnp.int32).astype(F32)
     down = lax.broadcasted_iota(jnp.int32, (32, 1), 0)
@@ -353,15 +392,16 @@
             copies.append(remote(gb.at[t, x], gb.at[t, x], xp(d)))
         return copies
 
+    arrived([v_sib, v_rel])
     value_terms = sum_blocks(
-        lambda b: dot(gkv[b, 2 * HS : 4 * HS], rnd[:, keys_of(b)], NT), (2 * HS, TOK)
+        lambda b: dot(gkv[b, KEYS : KEYS + 2 * HS], rnd[:, keys_of(b)], NT), (2 * HS, TOK)
     )
     attn = value_terms[:HS].astype(BF)
     ga[0, z, x] = attn[:HALF]
     gb[0, x, z] = attn[HALF:]
     g_one = gather_one(0)
     attn_tan = (
-        sum_blocks(lambda b: dot(gkv[b, 2 * HS : 3 * HS], rnd_tan[:, keys_of(b)], NT), (HS, TOK))
+        sum_blocks(lambda b: dot(gkv[b, KEYS : KEYS + HS], rnd_tan[:, keys_of(b)], NT), (HS, TOK))
         + value_terms[HS:]
     ).astype(BF)
     ga[1, z, x] = attn_tan[:HALF]
@@ -372,9 +412,8 @@
     arrived(g_one_tan)
     g_two_tan = gather_two(1)
 
-    own_wa.wait()
-    own_wb.wait()
-    arrived(w_two)
+    arrived([w_sib])
+    wa, wb = ww.at[0], ww.at[1]
     arrived(g_two)
 
     def whole(ref, *at):
@@ -504,10 +543,78 @@
     g = scattered(0)
 
     def pull_block(b, carry):
-        score[:, keys_of(b)] = dot(g, gkv[b, 2 * HS : 3 * HS], TN)
+        score[:, keys_of(b)] = dot(g, gkv[b, KEYS : KEYS + HS], TN)
         return carry
 
     lax.fori_loop(0, 4, pull_block, 0)
+    arrived(r_two_tan)
+    arrived(n_one)
+    n_two = []
+    for d in (1, 2, 3):
+        at0 = nb.at[b0, rows(z * 64, 64)]
+        at1 = nb.at[b1, rows(x * 64, 64)]
+        n_two.append(remote(at0, at0, zp(d)))
+        n_two.append(remote(at1, at1, xp(d)))
+    g_tan = scattered(1)
+    g_both = jnp.concatenate([g_tan, g], axis=0)
+
+    def value_block(b, carry):
+        at = keys_of(b)
+        cv[b] = (dot(g, rnd_tan[:, at], NN) + dot(g_tan, rnd[:, at], NN)).astype(BF)
+        return carry
+
+    lax.fori_loop(0, 4, value_block, 0)
+    v_core = [remote(cv.at[2 * k + 1 - c], cvr.at[k], sib) for k in range(2)]
+
+    def pull_block_tan(b, carry):
+        score_tan[:, keys_of(b)] = dot(g_both, gkv[b, KEYS : KEYS + 2 * HS], TN)
+        return carry
+
+    lax.fori_loop(0, 4, pull_block_tan, 0)
+
+    def chip_sums(own, other, kept):
+        for k in range(2):
+            kept[k] = total_of(own[2 * k + c], [other[k]]).astype(BF)
+
+    arrived(v_core)
+    chip_sums(cv, cvr, cvs)
+    v_far = remote(cvs, cvf, crs)
+
+    def soft_back(i, carry):
+        at = pl.ds(pl.multiple_of(i * 32, 32), 32)
+        weights, moved = prob[at, :], prob_tan[at, :]
+        pulled, pulled_tan = score[at, :], score_tan[at, :]
+        base = jnp.sum(weights * pulled, axis=-1, keepdims=True)
+        base_tan = jnp.sum(moved * pulled + weights * pulled_tan, axis=-1, keepdims=True)
+        less = pulled - base
+        score[at, :] = weights * less
+        score_tan[at, :] = moved * less + weights * (pulled_tan - base_tan)
+        return carry
+
+    lax.fori_loop(0, TOK // 32, soft_back, 0)
+
+    def key_block(b, carry):
+        at = keys_of(b)
+        slope, slope_tan = score[:, at].astype(BF), score_tan[:, at].astype(BF)
+        ck[b] = ((dot(q, slope_tan, NN) + dot(q_tan, slope, NN)) * root).astype(BF)
+        return carry
+
+    lax.fori_loop(0, 4, key_block, 0)
+
+    k_core = [remote(ck.at[2 * k + 1 - c], ckr.at[k], sib) for k in range(2)]
+
+    def query_block(b, held):
+        at = keys_of(b)
+        slope, slope_tan = score[:, at].astype(BF), score_tan[:, at].astype(BF)
+        return held + dot(gkv[b, 0:HS], slope_tan, NT) + dot(gkv[b, HS : 2 * HS], slope, NT)
+
+    cot_query = lax.fori_loop(0, 4, query_block, jnp.zeros((HS, TOK), F32)) * root
+    cot[s, 0:HS] = rotate(cot_query.astype(BF).astype(F32), own_trig, -1.0).astype(BF)
+    q_far = remote(cot.at[s, pl.ds(0, HS)], cot.at[s, pl.ds(0, HS)], crs)
+    arrived(k_core)
+    chip_sums(ck, ckr, cks)
+    k_far = remote(cks, ckf, crs)
+
     arrived(o_crs)
     fa[...] = total_of(ha[:, s], [ca[yh], ya[...]]).astype(BF)
     fb[...] = total_of(hb[s], [cb[yh], yb[...]]).astype(BF)
@@ -536,43 +643,29 @@
         for copy in o_near:
             copy.start()
 
-    arrived(r_two_tan)
-    g_tan = scattered(1)
-    g_both = jnp.concatenate([g_tan, g], axis=0)
-
-    def pull_block_tan(b, carry):
-        score_tan[:, keys_of(b)] = dot(g_both, gkv[b, 2 * HS : 4 * HS], TN)
-        return carry
-
-    lax.fori_loop(0, 4, pull_block_tan, 0)
-
-    def soft_back(i, carry):
-        at = pl.ds(pl.multiple_of(i * 32, 32), 32)
-        weights, moved = prob[at, :], prob_tan[at, :]
-        pulled, pulled_tan = score[at, :], score_tan[at, :]
-        base = jnp.sum(weights * pulled, axis=-1, keepdims=True)
-        base_tan = jnp.sum(moved * pulled + weights * pulled_tan, axis=-1, keepdims=True)
-        less = pulled - base
-        score[at, :] = weights * less
-        score_tan[at, :] = moved * less + weights * (pulled_tan - base_tan)
-        return carry
-
-    lax.fori_loop(0, TOK // 32, soft_back, 0)
-
-    def cot_block(b, held):
-        at = keys_of(b)
-        slope, slope_tan = score[:, at].astype(BF), score_tan[:, at].astype(BF)
-        ck[b, 0:HS] = ((dot(q, slope_tan, NN) + dot(q_tan, slope, NN)) * root).astype(BF)
-        ck[b, HS : 2 * HS] = (dot(g, rnd_tan[:, at], NN) + dot(g_tan, rnd[:, at], NN)).astype(BF)
-        return held + dot(gkv[b, 0:HS], slope_tan, NT) + dot(gkv[b, HS : 2 * HS], slope, NT)
-
-    cot_query = lax.fori_loop(0, 4, cot_block, jnp.zeros((HS, TOK), F32)) * root
-    c_core = [remote(ck.at[2 * k + 1 - c], cr.at[k], sib) for k in range(2)]
-    cot[s, 0:HS] = rotate(cot_query.astype(BF).astype(F32), -sin).astype(BF)
-    arrived(c_core)
-    cx[...] = total_of(ck[2 * far + c], [cr[far]]).astype(BF)
-    c_crs = remote(cx, cy, crs)
-
+    arrived([v_far])
+    for k in range(2):
+        cot[2 * k + c, 2 * HS : 3 * HS] = total_of(cvs[k], [cvf[k]]).astype(BF)
+    turns = [
+        trig(jnp.broadcast_to(gkv[2 * k + c, KEYS - 16 : KEYS].astype(F32)[0:1], (ROT, TOK)))
+        for k in range(2)
+    ]
+    arrived([k_far])
+    for k in range(2):
+        both = total_of(cks[k], [ckf[k]]).astype(BF).astype(F32)
+        cot[2 * k + c, HS : 2 * HS] = rotate(both, turns[k], -1.0).astype(BF)
+    arrived([q_far])
+    t_sib = [remote(cot.at[2 * k + c], cot.at[2 * k + c], sib) for k in range(2)]
+    arrived([n_sib] + n_two)
+
+    def first_terms(i, carry):
+        at = lanes(i * TOK, TOK)
+        part[:, at] = dot(cot[s], nrm[:, lanes(s * SHARE + i * TOK, TOK)], NN) + dot(
+            cot[s_crs], nb[s_crs, :, at], NN
+        )
+        return carry
+
+    lax.fori_loop(0, SHARE // TOK, first_terms, 0)
     arrived(o_fin)
 
     @pl.when(x != s)
@@ -595,46 +688,21 @@
     for half, ref in enumerate((oa, ob)):
         for k in range(4):
             bit = sign_bit(e_base + jnp.int32(wrap((half * HALF * D + k * PART) * MIX[0])))
-            oo[half * HALF : (half + 1) * HALF, k * PART : (k + 1) * PART] = ref[k].astype(
-                F32
-            ) * jnp.where(bit == 0, F32(scale), F32(-scale))
-
-    arrived([c_crs])
-    both = total_of(ck[s], [cr[yh], cy[...]])
-    cot[s, HS : 2 * HS] = rotate(both[:HS].astype(BF).astype(F32), -sin).astype(BF)
-    cot[s, 2 * HS : 3 * HS] = both[HS:].astype(BF)
-    t_crs = remote(cot.at[s], cot.at[s], crs)
-    t_sib = remote(cot.at[s], cot.at[s], sib)
-
-    arrived([n_sib] + n_two)
-
-    def first_term(i, carry):
-        oq[:, lanes(i * TOK, TOK)] = dot(cot[s], nrm[:, lanes(s * SHARE + i * TOK, TOK)], NN)
-        return carry
-
-    lax.fori_loop(0, SHARE // TOK, first_term, 0)
-    arrived([t_sib])
-
-    def next_term(b):
-        def term(i, carry):
-            at = lanes(i * TOK, TOK)
-            oq[:, at] += dot(cot[b], nb[b, :, at], NN)
-            return carry
-
-        lax.fori_loop(0, SHARE // TOK, term, 0)
-
-    next_term(s_sib)
-    arrived([t_crs])
-    t_rel = remote(cot.at[s_crs], cot.at[s_crs], sib)
-    next_term(s_crs)
-    arrived([t_rel])
-
-    def last_term(i, carry):
+            oo[half * HALF : (half + 1) * HALF, k * PART : (k + 1) * PART] = (
+                ref[k].astype(F32) * jnp.where(bit == 0, F32(scale), F32(-scale))
+            ).astype(BF)
+
+
+    arrived(t_sib)
+
+    def last_terms(i, carry):
         at = lanes(i * TOK, TOK)
-        oq[:, at] = (oq[:, at] + dot(cot[s_crd], nb[s_crd, :, at], NN)) * sgn[:, at]
-        return carry
-
-    lax.fori_loop(0, SHARE // TOK, last_term, 0)
+        total = part[:, at] + (dot(cot[s_sib], nb[s_sib, :, at], NN) + dot(cot[s_crd], nb[s_crd, :, at], NN))
+        oq[:, at] = (total * sgn[:, at]).astype(BF)
+        return carry
+
+    lax.fori_loop(0, SHARE // TOK, last_terms, 0)
+
     for copy in sent:
         copy.wait_send()
 
@@ -657,9 +725,8 @@
     v = pltpu.VMEM
     scratch = [
         v((TOK, D), BF), v((TOK, PART), BF), v((COLS, D), BF), v((TOK, D), BF), v((2, COLS, TOK), F32),
-        v((4, TOK, SHARE), BF), v((4, 4 * HS + 16, TOK), BF),
-        v((4, HALF, SHARE), BF), v((4, 4, HALF, PART), BF),
-        v((4, 4, HALF, PART), BF), v((4, 4, HALF, PART), BF),
+        v((2, TOK, 128), F32), v((4, TOK, SHARE), BF), v((4, 4 * HS + 16, TOK), BF),
+        v((4, 4, HALF, PART), BF), v((2, 4, 4, HALF, PART), BF),
         v((4, 4, HALF, PART), BF), v((4, 4, HALF, PART), BF),
         v((2, 4, 4, HALF, TOK), BF), v((2, 4, 4, HALF, TOK), BF),
         v((TOK, 1024), F32), v((TOK, 1024), F32), v((TOK, 1024), F32), v((TOK, 1024), F32),
@@ -674,16 +741,17 @@
         v((2, 4, HALF, PART), BF), v((2, 4, HALF, PART), BF),
         v((4, HALF, PART), BF), v((4, HALF, PART), BF), v((4, HALF, PART), BF), v((4, HALF, PART), BF),
         v((4, HALF, PART), BF), v((4, HALF, PART), BF), v((4, HALF, PART), BF), v((4, HALF, PART), BF),
-        v((4, 2 * HS, TOK), BF), v((2, 2 * HS, TOK), BF), v((2 * HS, TOK), BF), v((2 * HS, TOK), BF),
-        v((4, 3 * HS, TOK), BF), v((COLS, SHARE), F32),
+        v((4, HS, TOK), BF), v((2, HS, TOK), BF), v((2, HS, TOK), BF), v((2, HS, TOK), BF),
+        v((4, HS, TOK), BF), v((2, HS, TOK), BF), v((2, HS, TOK), BF), v((2, HS, TOK), BF),
+        v((4, 3 * HS, TOK), BF), v((COLS, SHARE), F32), v((COLS, SHARE), F32),
         pltpu.SemaphoreType.DMA((N_REMOTE,)), pltpu.SemaphoreType.DMA((N_REMOTE,)),
         pltpu.SemaphoreType.DMA((N_LOCAL,)),
     ]
     product, out_curv = pl.pallas_call(
         kernel,
         out_shape=(
-            jax.ShapeDtypeStruct((COLS, SHARE), F32),
-            jax.ShapeDtypeStruct((HS, SHARE), F32),
+            jax.ShapeDtypeStruct((COLS, SHARE), BF),
+            jax.ShapeDtypeStruct((HS, SHARE), BF),
         ),
         in_specs=[anywhere, anywhere, vmem, anywhere, anywhere, smem, smem, vmem, vmem],
         out_specs=(vmem, vmem),
@@ -695,7 +763,7 @@
         tokens, target, norm_gain.reshape(1, D), qkv_weight.T, out_weight, probe_seed, block_order,
         jnp.asarray(tab_t), jnp.asarray(tab_b),
     )
-    return product.T, out_curv
+    return product.astype(F32).T, out_curv.astype(F32)
 
 
 def solution(mesh):

time: 105 us -> 94.9 us (0.904)
  the two profiles are of different devices: /device:TPU:1 before, /device:TPU:7 now
where the time goes in v3:
time: 94.9 us; the launch traced here: 94.7 us
  Pallas kernels  88.4 us (93%)
  other arithmetic  4.41 us (5%)
  between operations  1.93 us (2%)
    pallas_call x1, Pallas kernels, per_device(): pl.pallas_call(kernel, out_shape=(jax.ShapeDtypeStruct((COLS, SHARE), BF)...  88.4 us
    transpose x1, other arithmetic, per_device(): return (product.astype(F32).T, out_curv.astype(F32))  2.59 us

profile of v3, /device:TPU:7, one launch (start us, length us, event | category | flops | bytes accessed | tf_op | source)
XLA Modules:
  0.0 94.7 jit_solution(14788706917440554504)
XLA Ops:
  1.9 88.4 %shard_map.104 = (bf16[288,1536]{1,0:T(8,128)(2,1)}, bf16[96,1536]{1,0:T(8,128)(2,1)}) custom-call(bf16[256,6144]{1,0:T(8,128)(2,1)} %tok_in.1, bf16[256,6144]{1,0:T(8,128)(2,1)} %tgt_in.1, f32[1,6144]{1,0:T(1,128)} %bitcast.5, bf16[288,6144]{1,0:T(8,128)(2,1)} %bitcast.4, bf16[96,6144]{1,0:T(8,128)(2,1)} %wo_in.1, s32[1]{0:T(128)S(6)} %copy.11.seed, ...), custom_call_target="tpu_custom_call" | custom-call | tf_op jit(solution)/shard_map/pallas_call | solution.py:750
  90.3 2.6 %convert_bitcast_fusion = f32[1536,288]{0,1:T(8,128)} fusion(bf16[288,1536]{1,0:T(8,128)(2,1)} %get-tuple-element.4), kind=kLoop, calls=%fused_computation | loop fusion | flops 442368 | bytes 2654208 | tf_op jit(solution)/shard_map/transpose | solution.py:766
  92.9 1.8 %convert_element_type.4 = f32[96,1536]{1,0:T(8,128)} convert(bf16[96,1536]{1,0:T(8,128)(2,1)} %get-tuple-element.5) | non-fusion elementwise | flops 147456 | bytes 884736 | tf_op jit(solution)/shard_map/convert_element_type | solution.py:766

commit v4 on v3

--- a/solution.py
+++ b/solution.py
@@ -22,10 +22,11 @@
 SHARE = 1536
 PART = 384
 HALF = 48
+SPAN = 128
 KEYS = 2 * HS + 16
 STEP = 768
 MIX = (-1640531535, -2048144789, -1028477387)
-N_REMOTE = 136
+N_REMOTE = 168
 N_LOCAL = 16
 
 
@@ -60,7 +61,7 @@
     tok, tgt, wq, nrm, acc,
     stat, nb, gkv,
     wt, ww, pa, pb, ga, gb,
-    score, score_tan, prob, prob_tan, rnd, rnd_tan,
+    score, score_tan, prob, prob_tan, rnd, rnd_tan, slope, slope_tan, cv_acc, ck_acc,
     mix_acc, mix_out, mix_in, grads, back_acc,
     sa, sb, ra1, rb1, sa2, sb2, ra2, rb2,
     ha, hb, ca, cb, xa, xb, ya, yb, fa, fb, oa, ob,
@@ -342,12 +343,19 @@
     def keys_of(b):
         return lanes(b * TOK, TOK)
 
-    def score_block(b, carry):
-        score[:, keys_of(b)] = dot(q, gkv[b, 0:HS], TN) * root
-        score_tan[:, keys_of(b)] = dot(q_both, gkv[b, 0 : 2 * HS], TN) * root
-        return carry
-
-    lax.fori_loop(0, 4, score_block, 0)
+    def span(h):
+        return slice(h * SPAN, (h + 1) * SPAN)
+
+    def score_blocks(h):
+        left, left_both = q[:, span(h)], q_both[:, span(h)]
+
+        def score_block(b, carry):
+            score[span(h), keys_of(b)] = dot(left, gkv[b, 0:HS], TN) * root
+            score_tan[span(h), keys_of(b)] = dot(left_both, gkv[b, 0 : 2 * HS], TN) * root
+            return carry
+
+        lax.fori_loop(0, 4, score_block, 0)
+
     along = lax.broadcasted_iota(jnp.int32, (1, TOK), 1).astype(F32)
     key_pos = jnp.concatenate(
         [gkv[b, KEYS - 16 : KEYS].astype(F32)[0:1] * float(TOK) + along for b in range(4)], axis=1
@@ -372,49 +380,65 @@
         rnd_tan[at, :] = moved.astype(BF)
         return carry
 
-    lax.fori_loop(0, TOK // 32, soft_rows, 0)
+    def soft(h):
+        lax.fori_loop(h * SPAN // 32, (h + 1) * SPAN // 32, soft_rows, 0)
+
 
     def sum_blocks(term, shape):
         total = jnp.zeros(shape, F32)
         return lax.fori_loop(0, 4, lambda b, held: held + term(b), total)
 
-    def gather_one(t):
+    def gather_one(h, t):
         copies = []
         for d in (1, 2, 3):
-            copies.append(remote(ga.at[t, z, x], ga.at[t, z, x], xp(d)))
-            copies.append(remote(gb.at[t, x, z], gb.at[t, x, z], zp(d)))
+            copies.append(remote(ga.at[h, t, z, x], ga.at[h, t, z, x], xp(d)))
+            copies.append(remote(gb.at[h, t, x, z], gb.at[h, t, x, z], zp(d)))
         return copies
 
-    def gather_two(t):
+    def gather_two(h, t):
         copies = []
         for d in (1, 2, 3):
-            copies.append(remote(ga.at[t, z], ga.at[t, z], zp(d)))
-            copies.append(remote(gb.at[t, x], gb.at[t, x], xp(d)))
+            copies.append(remote(ga.at[h, t, z], ga.at[h, t, z], zp(d)))
+            copies.append(remote(gb.at[h, t, x], gb.at[h, t, x], xp(d)))
         return copies
 
+    def attn_products(h):
+        terms = sum_blocks(
+            lambda b: dot(gkv[b, KEYS : KEYS + 2 * HS], rnd[span(h), keys_of(b)], NT), (2 * HS, SPAN)
+        )
+        attn = terms[:HS].astype(BF)
+        ga[h, 0, z, x] = attn[:HALF]
+        gb[h, 0, x, z] = attn[HALF:]
+        one = gather_one(h, 0)
+        attn_tan = (
+            sum_blocks(
+                lambda b: dot(gkv[b, KEYS : KEYS + HS], rnd_tan[span(h), keys_of(b)], NT), (HS, SPAN)
+            )
+            + terms[HS:]
+        ).astype(BF)
+        ga[h, 1, z, x] = attn_tan[:HALF]
+        gb[h, 1, x, z] = attn_tan[HALF:]
+        return one, gather_one(h, 1)
+
+    score_blocks(0)
+    soft(0)
     arrived([v_sib, v_rel])
-    value_terms = sum_blocks(
-        lambda b: dot(gkv[b, KEYS : KEYS + 2 * HS], rnd[:, keys_of(b)], NT), (2 * HS, TOK)
-    )
-    attn = value_terms[:HS].astype(BF)
-    ga[0, z, x] = attn[:HALF]
-    gb[0, x, z] = attn[HALF:]
-    g_one = gather_one(0)
-    attn_tan = (
-        sum_blocks(lambda b: dot(gkv[b, KEYS : KEYS + HS], rnd_tan[:, keys_of(b)], NT), (HS, TOK))
-        + value_terms[HS:]
-    ).astype(BF)
-    ga[1, z, x] = attn_tan[:HALF]
-    gb[1, x, z] = attn_tan[HALF:]
-    g_one_tan = gather_one(1)
-    arrived(g_one)
-    g_two = gather_two(0)
-    arrived(g_one_tan)
-    g_two_tan = gather_two(1)
+    g_one = [attn_products(0)]
+    score_blocks(1)
+    soft(1)
+
+    g_two = []
+    for h in range(2):
+        if h == 1:
+            g_one.append(attn_products(1))
+        pair = []
+        for t in range(2):
+            arrived(g_one[h][t])
+            pair.append(gather_two(h, t))
+        g_two.append(pair)
 
     arrived([w_sib])
     wa, wb = ww.at[0], ww.at[1]
-    arrived(g_two)
 
     def whole(ref, *at):
         value = ref[at]
@@ -422,24 +446,33 @@
 
     mix_acc[...] = jnp.zeros_like(mix_acc)
 
-    def mix_one(i, carry):
-        left, right = whole(ga, 0, i), whole(gb, 0, i)
-        mix_acc[0] += dot(left, whole(wa, i), TN) + dot(right, whole(wb, i), TN)
-        mix_acc[1] += dot(left, whole(pa, i), TN) + dot(right, whole(pb, i), TN)
-        return carry
-
-    lax.fori_loop(0, 4, mix_one, 0)
-    mix_out[0] = mix_acc[0].astype(BF)
-    m_one = remote(mix_out.at[0], mix_in.at[0], partner)
-    arrived(g_two_tan)
-
-    def mix_two(i, carry):
-        mix_acc[1] += dot(whole(ga, 1, i), whole(wa, i), TN) + dot(whole(gb, 1, i), whole(wb, i), TN)
-        return carry
-
-    lax.fori_loop(0, 4, mix_two, 0)
-    mix_out[1] = mix_acc[1].astype(BF)
-    m_two = remote(mix_out.at[1], mix_in.at[1], partner)
+    def mix_one(h):
+        def step(i, carry):
+            left, right = whole(ga, h, 0, i), whole(gb, h, 0, i)
+            mix_acc[h, 0] += dot(left, whole(wa, i), TN) + dot(right, whole(wb, i), TN)
+            mix_acc[h, 1] += dot(left, whole(pa, i), TN) + dot(right, whole(pb, i), TN)
+            return carry
+
+        arrived(g_two[h][0])
+        lax.fori_loop(0, 4, step, 0)
+        mix_out[h, 0] = mix_acc[h, 0].astype(BF)
+        return remote(mix_out.at[h, 0], mix_in.at[h, 0], partner)
+
+    def mix_two(h):
+        def step(i, carry):
+            mix_acc[h, 1] += dot(whole(ga, h, 1, i), whole(wa, i), TN) + dot(
+                whole(gb, h, 1, i), whole(wb, i), TN
+            )
+            return carry
+
+        arrived(g_two[h][1])
+        lax.fori_loop(0, 4, step, 0)
+        mix_out[h, 1] = mix_acc[h, 1].astype(BF)
+        return remote(mix_out.at[h, 1], mix_in.at[h, 1], partner)
+
+    m_one = [mix_one(0)]
+    m_two = [mix_two(0)]
+    m_one.append(mix_one(1))
 
     s_base = (
         (lax.broadcasted_iota(jnp.int32, (COLS, TOK), 1) + s * SHARE) * WIDE
@@ -455,27 +488,54 @@
     lax.fori_loop(0, SHARE // TOK, sign_cols, 0)
 
     tgt_load.wait()
-    arrived([m_one])
-    resid = tok[:, lanes(own_cols, PART)].astype(F32) - tgt[...].astype(F32)
-    resid = resid + (mix_acc[0] + mix_in[0].astype(F32))
-    grads[0] = (resid * (1 / 1024)).astype(BF)
-
-    def back_one(i, carry):
-        grad = grads[0]
-        sa[0, i] = dot(whole(wa, i), grad, NT).astype(BF).reshape(4, HALF, TOK)
-        sb[0, i] = dot(whole(wb, i), grad, NT).astype(BF).reshape(4, HALF, TOK)
-        back_acc[0, i] = dot(whole(pa, i), grad, NT)
-        back_acc[1, i] = dot(whole(pb, i), grad, NT)
-        return carry
-
-    lax.fori_loop(0, 4, back_one, 0)
-
-    def scatter_one(t):
+
+    def scatter_one(h, t):
         copies = []
         for d in (1, 2, 3):
-            copies.append(remote(sa.at[t, (z + d) % 4], ra1.at[t, d - 1], zp(d)))
-            copies.append(remote(sb.at[t, (x + d) % 4], rb1.at[t, d - 1], xp(d)))
+            copies.append(remote(sa.at[h, t, (z + d) % 4], ra1.at[h, t, d - 1], zp(d)))
+            copies.append(remote(sb.at[h, t, (x + d) % 4], rb1.at[h, t, d - 1], xp(d)))
         return copies
+
+    def back_one(h):
+        arrived([m_one[h]])
+        resid = tok[span(h), lanes(own_cols, PART)].astype(F32) - tgt[span(h), :].astype(F32)
+        resid = resid + (mix_acc[h, 0] + mix_in[h, 0].astype(F32))
+        grads[0, span(h)] = (resid * (1 / 1024)).astype(BF)
+
+        def step(i, carry):
+            grad = grads[0, span(h)]
+            sa[h, 0, i] = dot(whole(wa, i), grad, NT).astype(BF).reshape(4, HALF, SPAN)
+            sb[h, 0, i] = dot(whole(wb, i), grad, NT).astype(BF).reshape(4, HALF, SPAN)
+            return carry
+
+        lax.fori_loop(0, 4, step, 0)
+        copies = scatter_one(h, 0)
+
+        def probe_step(i, carry):
+            grad = grads[0, span(h)]
+            back_acc[h, 0, i] = dot(whole(pa, i), grad, NT)
+            back_acc[h, 1, i] = dot(whole(pb, i), grad, NT)
+            return carry
+
+        lax.fori_loop(0, 4, probe_step, 0)
+        return copies
+
+    def back_two(h):
+        arrived([m_two[h]])
+        grads[1, span(h)] = ((mix_acc[h, 1] + mix_in[h, 1].astype(F32)) * (1 / 1024)).astype(BF)
+
+        def step(i, carry):
+            grad = grads[1, span(h)]
+            sa[h, 1, i] = (
+                (dot(whole(wa, i), grad, NT) + back_acc[h, 0, i]).astype(BF).reshape(4, HALF, SPAN)
+            )
+            sb[h, 1, i] = (
+                (dot(whole(wb, i), grad, NT) + back_acc[h, 1, i]).astype(BF).reshape(4, HALF, SPAN)
+            )
+            return carry
+
+        lax.fori_loop(0, 4, step, 0)
+        return scatter_one(h, 1)
 
     def total_of(own, others):
         total = own.astype(F32)
@@ -483,43 +543,39 @@
             total = total + other.astype(F32)
         return total
 
-    def scatter_two(t):
-        sa2[t] = total_of(sa[t, z], [ra1[t, k] for k in range(3)]).astype(BF)
-        sb2[t] = total_of(sb[t, x], [rb1[t, k] for k in range(3)]).astype(BF)
+    def scatter_two(h, t):
+        sa2[h, t] = total_of(sa[h, t, z], [ra1[h, t, k] for k in range(3)]).astype(BF)
+        sb2[h, t] = total_of(sb[h, t, x], [rb1[h, t, k] for k in range(3)]).astype(BF)
         copies = []
         for d in (1, 2, 3):
-            copies.append(remote(sa2.at[t, (x + d) % 4], ra2.at[t, d - 1], xp(d)))
-            copies.append(remote(sb2.at[t, (z + d) % 4], rb2.at[t, d - 1], zp(d)))
+            copies.append(remote(sa2.at[h, t, (x + d) % 4], ra2.at[h, t, d - 1], xp(d)))
+            copies.append(remote(sb2.at[h, t, (z + d) % 4], rb2.at[h, t, d - 1], zp(d)))
         return copies
 
-    def scattered(t):
-        first = total_of(sa2[t, x], [ra2[t, k] for k in range(3)])
-        second = total_of(sb2[t, z], [rb2[t, k] for k in range(3)])
+    def scattered(h, t):
+        first = total_of(sa2[h, t, x], [ra2[h, t, k] for k in range(3)])
+        second = total_of(sb2[h, t, z], [rb2[h, t, k] for k in range(3)])
         return jnp.concatenate([first.astype(BF), second.astype(BF)], axis=0)
 
-    r_one = scatter_one(0)
-    arrived([m_two])
-    grads[1] = ((mix_acc[1] + mix_in[1].astype(F32)) * (1 / 1024)).astype(BF)
-
-    def back_two(i, carry):
-        grad = grads[1]
-        sa[1, i] = (dot(whole(wa, i), grad, NT) + back_acc[0, i]).astype(BF).reshape(4, HALF, TOK)
-        sb[1, i] = (dot(whole(wb, i), grad, NT) + back_acc[1, i]).astype(BF).reshape(4, HALF, TOK)
-        return carry
-
-    lax.fori_loop(0, 4, back_two, 0)
-    r_one_tan = scatter_one(1)
+    r_one = [[back_one(0)], []]
+    r_one[0].append(back_two(0))
+    m_two.append(mix_two(1))
+    r_one[1].append(back_one(1))
+    r_two = [[], []]
+    arrived(r_one[0][0])
+    r_two[0].append(scatter_two(0, 0))
+    r_one[1].append(back_two(1))
+    arrived(r_one[0][1])
+    r_two[0].append(scatter_two(0, 1))
 
     def out_terms(i, carry):
-        one, two = grads[0], grads[1]
-        ha[i] = (
-            (dot(whole(ga, 1, i), one, NN) + dot(whole(ga, 0, i), two, NN))
-            .astype(BF).reshape(4, HALF, PART)
-        )
-        hb[i] = (
-            (dot(whole(gb, 1, i), one, NN) + dot(whole(gb, 0, i), two, NN))
-            .astype(BF).reshape(4, HALF, PART)
-        )
+        both = grads[...].reshape(2 * TOK, PART)
+
+        def joined(ref):
+            return jnp.concatenate([whole(ref, h, t, i) for t in (1, 0) for h in (0, 1)], axis=1)
+
+        ha[i] = dot(joined(ga), both, NN).astype(BF).reshape(4, HALF, PART)
+        hb[i] = dot(joined(gb), both, NN).astype(BF).reshape(4, HALF, PART)
         return carry
 
     lax.fori_loop(0, 4, out_terms, 0)
@@ -527,27 +583,73 @@
     for k in range(2):
         o_core.append(remote(ha.at[:, 2 * k + 1 - c], ca.at[k], sib))
         o_core.append(remote(hb.at[2 * k + 1 - c], cb.at[k], sib))
-    arrived(r_one)
-    r_two = scatter_two(0)
-
+    arrived(r_one[1][0])
+    r_two[1].append(scatter_two(1, 0))
     arrived(o_core)
     far = 1 - yh
     xa[...] = total_of(ha[:, 2 * far + c], [ca[far]]).astype(BF)
     xb[...] = total_of(hb[2 * far + c], [cb[far]]).astype(BF)
     o_crs = [remote(xa, ya, crs), remote(xb, yb, crs)]
 
-    arrived(r_one_tan)
-    r_two_tan = scatter_two(1)
-
-    arrived(r_two)
-    g = scattered(0)
-
-    def pull_block(b, carry):
-        score[:, keys_of(b)] = dot(g, gkv[b, KEYS : KEYS + HS], TN)
-        return carry
-
-    lax.fori_loop(0, 4, pull_block, 0)
-    arrived(r_two_tan)
+    cv_acc[...] = jnp.zeros_like(cv_acc)
+    ck_acc[...] = jnp.zeros_like(ck_acc)
+
+    def soft_back(i, carry):
+        at = pl.ds(pl.multiple_of(i * 32, 32), 32)
+        weights, moved = prob[at, :], prob_tan[at, :]
+        pulled, pulled_tan = score[at, :], score_tan[at, :]
+        base = jnp.sum(weights * pulled, axis=-1, keepdims=True)
+        base_tan = jnp.sum(moved * pulled + weights * pulled_tan, axis=-1, keepdims=True)
+        less = pulled - base
+        slope[at, :] = (weights * less).astype(BF)
+        slope_tan[at, :] = (moved * less + weights * (pulled_tan - base_tan)).astype(BF)
+        return carry
+
+    def value_terms(h, g, g_tan):
+        def step(b, carry):
+            at = keys_of(b)
+            cv_acc[b] += dot(g, rnd_tan[span(h), at], NN) + dot(g_tan, rnd[span(h), at], NN)
+            return carry
+
+        lax.fori_loop(0, 4, step, 0)
+
+    def slopes(h, g, g_tan):
+        g_both = jnp.concatenate([g_tan, g], axis=0)
+
+        def step(b, carry):
+            at = keys_of(b)
+            score[span(h), at] = dot(g, gkv[b, KEYS : KEYS + HS], TN)
+            score_tan[span(h), at] = dot(g_both, gkv[b, KEYS : KEYS + 2 * HS], TN)
+            return carry
+
+        lax.fori_loop(0, 4, step, 0)
+        lax.fori_loop(h * SPAN // 32, (h + 1) * SPAN // 32, soft_back, 0)
+
+    def key_terms(h):
+        left, left_tan = q[:, span(h)], q_tan[:, span(h)]
+
+        def step(b, carry):
+            at = keys_of(b)
+            ck_acc[b] += dot(left, slope_tan[span(h), at], NN) + dot(left_tan, slope[span(h), at], NN)
+            return carry
+
+        lax.fori_loop(0, 4, step, 0)
+
+    def chip_sums(own, other, kept):
+        for k in range(2):
+            kept[k] = total_of(own[2 * k + c], [other[k]]).astype(BF)
+
+    arrived(r_two[0][0])
+    arrived(r_two[0][1])
+    g_first, g_first_tan = scattered(0, 0), scattered(0, 1)
+    value_terms(0, g_first, g_first_tan)
+    arrived(r_one[1][1])
+    r_two[1].append(scatter_two(1, 1))
+    slopes(0, g_first, g_first_tan)
+    key_terms(0)
+
+    arrived(r_two[1][0])
+    arrived(r_two[1][1])
     arrived(n_one)
     n_two = []
     for d in (1, 2, 3):
@@ -555,58 +657,22 @@
         at1 = nb.at[b1, rows(x * 64, 64)]
         n_two.append(remote(at0, at0, zp(d)))
         n_two.append(remote(at1, at1, xp(d)))
-    g_tan = scattered(1)
-    g_both = jnp.concatenate([g_tan, g], axis=0)
-
-    def value_block(b, carry):
-        at = keys_of(b)
-        cv[b] = (dot(g, rnd_tan[:, at], NN) + dot(g_tan, rnd[:, at], NN)).astype(BF)
-        return carry
-
-    lax.fori_loop(0, 4, value_block, 0)
+    g_second, g_second_tan = scattered(1, 0), scattered(1, 1)
+    value_terms(1, g_second, g_second_tan)
+    cv[...] = cv_acc[...].astype(BF)
     v_core = [remote(cv.at[2 * k + 1 - c], cvr.at[k], sib) for k in range(2)]
-
-    def pull_block_tan(b, carry):
-        score_tan[:, keys_of(b)] = dot(g_both, gkv[b, KEYS : KEYS + 2 * HS], TN)
-        return carry
-
-    lax.fori_loop(0, 4, pull_block_tan, 0)
-
-    def chip_sums(own, other, kept):
-        for k in range(2):
-            kept[k] = total_of(own[2 * k + c], [other[k]]).astype(BF)
-
+    slopes(1, g_second, g_second_tan)
     arrived(v_core)
     chip_sums(cv, cvr, cvs)
     v_far = remote(cvs, cvf, crs)
-
-    def soft_back(i, carry):
-        at = pl.ds(pl.multiple_of(i * 32, 32), 32)
-        weights, moved = prob[at, :], prob_tan[at, :]
-        pulled, pulled_tan = score[at, :], score_tan[at, :]
-        base = jnp.sum(weights * pulled, axis=-1, keepdims=True)
-        base_tan = jnp.sum(moved * pulled + weights * pulled_tan, axis=-1, keepdims=True)
-        less = pulled - base
-        score[at, :] = weights * less
-        score_tan[at, :] = moved * less + weights * (pulled_tan - base_tan)
-        return carry
-
-    lax.fori_loop(0, TOK // 32, soft_back, 0)
-
-    def key_block(b, carry):
-        at = keys_of(b)
-        slope, slope_tan = score[:, at].astype(BF), score_tan[:, at].astype(BF)
-        ck[b] = ((dot(q, slope_tan, NN) + dot(q_tan, slope, NN)) * root).astype(BF)
-        return carry
-
-    lax.fori_loop(0, 4, key_block, 0)
+    key_terms(1)
+    ck[...] = (ck_acc[...] * root).astype(BF)
 
     k_core = [remote(ck.at[2 * k + 1 - c], ckr.at[k], sib) for k in range(2)]
 
     def query_block(b, held):
         at = keys_of(b)
-        slope, slope_tan = score[:, at].astype(BF), score_tan[:, at].astype(BF)
-        return held + dot(gkv[b, 0:HS], slope_tan, NT) + dot(gkv[b, HS : 2 * HS], slope, NT)
+        return held + dot(gkv[b, 0:HS], slope_tan[:, at], NT) + dot(gkv[b, HS : 2 * HS], slope[:, at], NT)
 
     cot_query = lax.fori_loop(0, 4, query_block, jnp.zeros((HS, TOK), F32)) * root
     cot[s, 0:HS] = rotate(cot_query.astype(BF).astype(F32), own_trig, -1.0).astype(BF)
@@ -707,6 +773,11 @@
         copy.wait_send()
 
 
+def widen(product_in, out_in, product, out):
+    product[...] = product_in[...].astype(F32)
+    out[...] = out_in[...].astype(F32)
+
+
 def tables():
     rate = 10000.0 ** (-2.0 * np.arange(ROT // 2) / ROT)
     rate = np.concatenate([rate, rate])[:, None]
@@ -728,15 +799,16 @@
         v((2, TOK, 128), F32), v((4, TOK, SHARE), BF), v((4, 4 * HS + 16, TOK), BF),
         v((4, 4, HALF, PART), BF), v((2, 4, 4, HALF, PART), BF),
         v((4, 4, HALF, PART), BF), v((4, 4, HALF, PART), BF),
-        v((2, 4, 4, HALF, TOK), BF), v((2, 4, 4, HALF, TOK), BF),
+        v((2, 2, 4, 4, HALF, SPAN), BF), v((2, 2, 4, 4, HALF, SPAN), BF),
         v((TOK, 1024), F32), v((TOK, 1024), F32), v((TOK, 1024), F32), v((TOK, 1024), F32),
-        v((TOK, 1024), BF), v((TOK, 1024), BF),
-        v((2, TOK, PART), F32), v((2, TOK, PART), BF), v((2, TOK, PART), BF), v((2, TOK, PART), BF),
-        v((2, 4, 4 * HALF, TOK), F32),
-        v((2, 4, 4, HALF, TOK), BF), v((2, 4, 4, HALF, TOK), BF),
-        v((2, 3, 4, HALF, TOK), BF), v((2, 3, 4, HALF, TOK), BF),
-        v((2, 4, HALF, TOK), BF), v((2, 4, HALF, TOK), BF),
-        v((2, 3, HALF, TOK), BF), v((2, 3, HALF, TOK), BF),
+        v((TOK, 1024), BF), v((TOK, 1024), BF), v((TOK, 1024), BF), v((TOK, 1024), BF),
+        v((4, HS, TOK), F32), v((4, HS, TOK), F32),
+        v((2, 2, SPAN, PART), F32), v((2, 2, SPAN, PART), BF), v((2, 2, SPAN, PART), BF), v((2, TOK, PART), BF),
+        v((2, 2, 4, 4 * HALF, SPAN), F32),
+        v((2, 2, 4, 4, HALF, SPAN), BF), v((2, 2, 4, 4, HALF, SPAN), BF),
+        v((2, 2, 3, 4, HALF, SPAN), BF), v((2, 2, 3, 4, HALF, SPAN), BF),
+        v((2, 2, 4, HALF, SPAN), BF), v((2, 2, 4, HALF, SPAN), BF),
+        v((2, 2, 3, HALF, SPAN), BF), v((2, 2, 3, HALF, SPAN), BF),
         v((4, 4, HALF, PART), BF), v((4, 4, HALF, PART), BF),
         v((2, 4, HALF, PART), BF), v((2, 4, HALF, PART), BF),
         v((4, HALF, PART), BF), v((4, HALF, PART), BF), v((4, HALF, PART), BF), v((4, HALF, PART), BF),
@@ -763,7 +835,17 @@
         tokens, target, norm_gain.reshape(1, D), qkv_weight.T, out_weight, probe_seed, block_order,
         jnp.asarray(tab_t), jnp.asarray(tab_b),
     )
-    return product.astype(F32).T, out_curv.astype(F32)
+    product, out_curv = pl.pallas_call(
+        widen,
+        grid=(3,),
+        out_shape=(
+            jax.ShapeDtypeStruct((COLS, SHARE), F32),
+            jax.ShapeDtypeStruct((HS, SHARE), F32),
+        ),
+        in_specs=[pl.BlockSpec((COLS, SHARE // 3), lambda i: (0, i)), pl.BlockSpec((HS, SHARE // 3), lambda i: (0, i))],
+        out_specs=(pl.BlockSpec((COLS, SHARE // 3), lambda i: (0, i)), pl.BlockSpec((HS, SHARE // 3), lambda i: (0, i))),
+    )(product, out_curv)
+    return product.T, out_curv
 
 
 def solution(mesh):

time: 94.9 us -> 91.3 us (0.962)
  the two profiles are of different devices: /device:TPU:7 before, /device:TPU:4 now
where the time goes in v4:
time: 91.3 us; the launch traced here: 91.1 us
  Pallas kernels  89.2 us (98%)
  between operations  1.93 us (2%)
    pallas_call x1, Pallas kernels, per_device(): pl.pallas_call(kernel, out_shape=(jax.ShapeDtypeStruct((COLS, SHARE), BF)...  85.9 us
    pallas_call x1, Pallas kernels, per_device(): pl.pallas_call(widen, grid=(3,), out_shape=(jax.ShapeDtypeStruct((COLS, S...  3.28 us

profile of v4, /device:TPU:4, one launch (start us, length us, event | category | flops | bytes accessed | tf_op | source)
XLA Modules:
  0.0 91.1 jit_solution(4104379634903277541)
XLA Ops:
  1.9 85.9 %shard_map.104 = (bf16[288,1536]{1,0:T(8,128)(2,1)}, bf16[96,1536]{1,0:T(8,128)(2,1)}) custom-call(bf16[256,6144]{1,0:T(8,128)(2,1)} %tok_in.1, bf16[256,6144]{1,0:T(8,128)(2,1)} %tgt_in.1, f32[1,6144]{1,0:T(1,128)} %bitcast.4, bf16[288,6144]{1,0:T(8,128)(2,1)} %bitcast.3, bf16[96,6144]{1,0:T(8,128)(2,1)} %wo_in.1, s32[1]{0:T(128)S(6)} %copy.11.seed, ...), custom_call_target="tpu_custom_call" | custom-call | tf_op jit(solution)/shard_map/pallas_call | solution.py:822
  87.8 3.3 %shard_map.105 = (f32[288,1536]{1,0:T(8,128)}, f32[96,1536]{1,0:T(8,128)}) custom-call(bf16[288,1536]{1,0:T(8,128)(2,1)} %get-tuple-element.6.product_in, bf16[96,1536]{1,0:T(8,128)(2,1)} %get-tuple-element.7.out_in), custom_call_target="tpu_custom_call" | custom-call | tf_op jit(solution)/shard_map/pallas_call | solution.py:838

commit v5 on v3

--- a/solution.py
+++ b/solution.py
@@ -22,11 +22,12 @@
 SHARE = 1536
 PART = 384
 HALF = 48
+SPAN = 128
 KEYS = 2 * HS + 16
 STEP = 768
 MIX = (-1640531535, -2048144789, -1028477387)
-N_REMOTE = 136
-N_LOCAL = 16
+N_REMOTE = 120
+N_LOCAL = 24
 
 
 def wrap(value):
@@ -55,14 +56,14 @@
 
 
 def kernel(
-    tok_in, tgt_in, gain, wq_in, wo_in, seed, block, tab_t, tab_b,
-    oq, oo,
-    tok, tgt, wq, nrm, acc,
+    tok_in, tgt_in, gain_in, wq_in, wo_in, seed, block, tab_t_in, tab_b_in,
+    oq_out, oo_out,
+    oq, oo, gain, tab_t, tab_b, tok, tgt, wq, nrm, acc,
     stat, nb, gkv,
-    wt, ww, pa, pb, ga, gb,
-    score, score_tan, prob, prob_tan, rnd, rnd_tan,
-    mix_acc, mix_out, mix_in, grads, back_acc,
-    sa, sb, ra1, rb1, sa2, sb2, ra2, rb2,
+    wt, ww, pp, wpt, ga, gb,
+    qq, qk, gg, score, prob, prob_tan, rnd, slope, cv_acc, ck_acc, cq_acc,
+    mix_acc, mix_out, mix_in, grads, grad, turn, resid,
+    sab, ra1, rb1, sa2, sb2, ra2, rb2,
     ha, hb, ca, cb, xa, xb, ya, yb, fa, fb, oa, ob,
     cv, cvr, cvs, cvf, ck, ckr, cks, ckf, cot, sgn, part,
     send, recv, local,
@@ -120,6 +121,11 @@
         copy.start()
         return copy
 
+    def nearby(src, dst):
+        i = local_count[0]
+        local_count[0] += 1
+        return pltpu.make_async_copy(src, dst, local.at[i])
+
     def arrived(copies):
         for copy in copies:
             copy.wait_recv()
@@ -130,8 +136,8 @@
     def rows(start, size):
         return pl.ds(pl.multiple_of(start, 16), size)
 
-    tok_load = stay(tok_in, tok)
-    wq_load = stay(wq_in, wq)
+    tok_loads = [stay(tok_in.at[pl.ds(k * 64, 64)], tok.at[pl.ds(k * 64, 64)]) for k in range(4)]
+    tab_loads = [stay(gain_in, gain), stay(tab_t_in, tab_t), stay(tab_b_in, tab_b)]
     tgt_load = stay(tgt_in.at[:, lanes(own_cols, PART)], tgt)
     first, second = jnp.where(c == 0, x, z), jnp.where(c == 0, z, x)
 
@@ -159,7 +165,6 @@
         for d in range(4):
             greet(fin(d))
 
-    tok_load.wait()
 
     def norm_sums(i, carry):
         at = rows(i * 16, 16)
@@ -169,7 +174,10 @@
         stat[0, at, :] = totals[0] + totals[1]
         return carry
 
-    lax.fori_loop(0, TOK // 16, norm_sums, 0)
+    for k in range(4):
+        tok_loads[k].wait()
+        lax.fori_loop(k * 4, (k + 1) * 4, norm_sums, 0, unroll=2)
+    wq_load = stay(wq_in, wq)
     average = jnp.sum(stat[0], axis=-1, keepdims=True) * (1 / D)
     stat[0] = jnp.broadcast_to(average, (TOK, 128))
 
@@ -183,7 +191,7 @@
         stat[1, at, :] = totals[0] + totals[1]
         return carry
 
-    lax.fori_loop(0, TOK // 16, norm_squares, 0)
+    lax.fori_loop(0, TOK // 16, norm_squares, 0, unroll=2)
     spread = jnp.sum(stat[1], axis=-1, keepdims=True) * (1 / D)
     stat[1] = jnp.broadcast_to(lax.rsqrt(spread + 1e-05), (TOK, 128))
 
@@ -209,6 +217,9 @@
                 )
             )
 
+    for copy in tab_loads:
+        copy.wait()
+
     def norm_rows(i, carry):
         at = rows(i * 16, 16)
         middle, factor = stat[0, at, :], stat[1, at, :]
@@ -289,10 +300,21 @@
     v_crs = spread_kv(s, v_part, crs)
     v_sib = spread_kv(s, v_part, sib)
 
+    def span(h):
+        return slice(h * SPAN, (h + 1) * SPAN)
+
+    tgt_load.wait()
     project(0, HS)
     q = rotate(acc[0, :HS], own_trig).astype(BF)
     q_tan = rotate(acc[1, :HS], own_trig).astype(BF)
-    q_both = jnp.concatenate([q_tan, q], axis=0)
+    for h in range(2):
+        one, two = q[:, span(h)], q_tan[:, span(h)]
+        qq[h] = jnp.concatenate(
+            [jnp.concatenate([one, two], axis=1), jnp.concatenate([jnp.zeros_like(one), one], axis=1)],
+            axis=0,
+        ).astype(F32).T.astype(BF)
+        qk[h] = jnp.concatenate([one, two], axis=1)
+    resid[...] = (tok[:, lanes(own_cols, PART)].astype(F32) - tgt[...].astype(F32)).T
 
     b0 = (1 - yh) * 2
     b1 = b0 + 1
@@ -321,20 +343,28 @@
             first = ((k * 2 + yl) * 4 + i) * HS
             second = ((i * 2 + yl) * 4 + k) * HS + HALF
             bit = sign_bit(o_base + first * jnp.int32(wrap(D * MIX[0])))
-            pa[i, k] = jnp.where(bit == 0, F32(o_probe), F32(-o_probe)).astype(BF)
+            pp[0, i, k] = jnp.where(bit == 0, F32(o_probe), F32(-o_probe)).astype(BF)
             bit = sign_bit(o_base + second * jnp.int32(wrap(D * MIX[0])))
-            pb[i, k] = jnp.where(bit == 0, F32(o_probe), F32(-o_probe)).astype(BF)
+            pp[1, i, k] = jnp.where(bit == 0, F32(o_probe), F32(-o_probe)).astype(BF)
         return carry
 
     lax.fori_loop(0, 4, probe_piece, 0)
+
+    def turned(source, start):
+        def turn(i, carry):
+            for a in range(2):
+                value = source[a, i].reshape(4 * HALF, PART).astype(F32)
+                wpt[a, i, start : start + PART] = value.T.astype(BF)
+            return carry
+
+        lax.fori_loop(0, 4, turn, 0)
+
+    turned(pp, PART)
 
     arrived([k_crs])
     k_rel = spread_kv(s_crs, k_part, sib)
     arrived([v_crs])
     v_rel = spread_kv(s_crs, v_part, sib)
-    own_ww.wait()
-    arrived(w_two)
-    w_sib = remote(ww.at[c], ww.at[c], sib)
 
     arrived([k_sib, k_rel])
     root = 1 / math.sqrt(HS)
@@ -342,12 +372,13 @@
     def keys_of(b):
         return lanes(b * TOK, TOK)
 
-    def score_block(b, carry):
-        score[:, keys_of(b)] = dot(q, gkv[b, 0:HS], TN) * root
-        score_tan[:, keys_of(b)] = dot(q_both, gkv[b, 0 : 2 * HS], TN) * root
-        return carry
-
-    lax.fori_loop(0, 4, score_block, 0)
+    def pulls(left, part, h):
+        def pull(b, carry):
+            score[h, :, keys_of(b)] = dot(left[h], gkv[b, part], NN)
+            return carry
+
+        lax.fori_loop(0, 4, pull, 0, unroll=2)
+
     along = lax.broadcasted_iota(jnp.int32, (1, TOK), 1).astype(F32)
     key_pos = jnp.concatenate(
         [gkv[b, KEYS - 16 : KEYS].astype(F32)[0:1] * float(TOK) + along for b in range(4)], axis=1
@@ -355,91 +386,82 @@
     number_f = jnp.full((32, 1), number, jnp.int32).astype(F32)
     down = lax.broadcasted_iota(jnp.int32, (32, 1), 0)
 
-    def soft_rows(i, carry):
-        at = pl.ds(pl.multiple_of(i * 32, 32), 32)
-        query_pos = number_f * float(TOK) + (down + i * 32).astype(F32)
-        allowed = key_pos <= query_pos
-        values = jnp.where(allowed, score[at, :], -1e30)
-        highest = jnp.max(values, axis=-1, keepdims=True)
-        weights = jnp.exp(values - highest)
-        weights = weights * (1.0 / jnp.sum(weights, axis=-1, keepdims=True))
-        tans = score_tan[at, :]
-        moved = weights * tans
-        moved = moved - weights * jnp.sum(moved, axis=-1, keepdims=True)
-        prob[at, :] = weights
-        prob_tan[at, :] = moved
-        rnd[at, :] = weights.astype(BF)
-        rnd_tan[at, :] = moved.astype(BF)
-        return carry
-
-    lax.fori_loop(0, TOK // 32, soft_rows, 0)
-
-    def sum_blocks(term, shape):
-        total = jnp.zeros(shape, F32)
-        return lax.fori_loop(0, 4, lambda b, held: held + term(b), total)
-
-    def gather_one(t):
+    def soft(h):
+        def soft_rows(i, carry):
+            at = pl.ds(pl.multiple_of(h * SPAN + i * 32, 32), 32)
+            low, high = pl.ds(pl.multiple_of(i * 32, 32), 32), pl.ds(pl.multiple_of(SPAN + i * 32, 32), 32)
+            query_pos = number_f * float(TOK) + (down + (h * SPAN + i * 32)).astype(F32)
+            allowed = key_pos <= query_pos
+            values = jnp.where(allowed, score[h, low, :] * root, -1e30)
+            highest = jnp.max(values, axis=-1, keepdims=True)
+            weights = jnp.exp(values - highest)
+            weights = weights * (1.0 / jnp.sum(weights, axis=-1, keepdims=True))
+            moved = weights * (score[h, high, :] * root)
+            moved = moved - weights * jnp.sum(moved, axis=-1, keepdims=True)
+            prob[at, :] = weights
+            prob_tan[at, :] = moved
+            rnd[h, high, :] = weights.astype(BF)
+            rnd[h, low, :] = moved.astype(BF)
+            return carry
+
+        lax.fori_loop(0, SPAN // 32, soft_rows, 0, unroll=2)
+
+    def joint(part, ref, h):
+        def term(b, held):
+            return held + dot(gkv[b, part], ref[h, :, keys_of(b)], NT)
+
+        return lax.fori_loop(0, 4, term, jnp.zeros((2 * HS, 2 * SPAN), F32))
+
+    def attn_products(h):
+        terms = joint(v_part, rnd, h)
+        both = jnp.concatenate([terms[:HS, SPAN:], terms[:HS, :SPAN] + terms[HS:, SPAN:]], axis=1)
+        both = both.astype(BF)
+        ga[h, z, x] = both[:HALF]
+        gb[h, x, z] = both[HALF:]
         copies = []
         for d in (1, 2, 3):
-            copies.append(remote(ga.at[t, z, x], ga.at[t, z, x], xp(d)))
-            copies.append(remote(gb.at[t, x, z], gb.at[t, x, z], zp(d)))
+            copies.append(remote(ga.at[h, z, x], ga.at[h, z, x], xp(d)))
+            copies.append(remote(gb.at[h, x, z], gb.at[h, x, z], zp(d)))
         return copies
 
-    def gather_two(t):
+    def gather_two(h):
         copies = []
         for d in (1, 2, 3):
-            copies.append(remote(ga.at[t, z], ga.at[t, z], zp(d)))
-            copies.append(remote(gb.at[t, x], gb.at[t, x], xp(d)))
+            copies.append(remote(ga.at[h, z], ga.at[h, z], zp(d)))
+            copies.append(remote(gb.at[h, x], gb.at[h, x], xp(d)))
         return copies
 
+    pulls(qq, pl.ds(0, 2 * HS), 0)
+    soft(0)
     arrived([v_sib, v_rel])
-    value_terms = sum_blocks(
-        lambda b: dot(gkv[b, KEYS : KEYS + 2 * HS], rnd[:, keys_of(b)], NT), (2 * HS, TOK)
-    )
-    attn = value_terms[:HS].astype(BF)
-    ga[0, z, x] = attn[:HALF]
-    gb[0, x, z] = attn[HALF:]
-    g_one = gather_one(0)
-    attn_tan = (
-        sum_blocks(lambda b: dot(gkv[b, KEYS : KEYS + HS], rnd_tan[:, keys_of(b)], NT), (HS, TOK))
-        + value_terms[HS:]
-    ).astype(BF)
-    ga[1, z, x] = attn_tan[:HALF]
-    gb[1, x, z] = attn_tan[HALF:]
-    g_one_tan = gather_one(1)
-    arrived(g_one)
-    g_two = gather_two(0)
-    arrived(g_one_tan)
-    g_two_tan = gather_two(1)
+    g_one = [attn_products(0)]
+    pulls(qq, pl.ds(0, 2 * HS), 1)
+    own_ww.wait()
+    arrived(w_two)
+    w_sib = remote(ww.at[c], ww.at[c], sib)
+    soft(1)
+
+    arrived(g_one[0])
+    g_two = [gather_two(0)]
+    g_one.append(attn_products(1))
 
     arrived([w_sib])
-    wa, wb = ww.at[0], ww.at[1]
-    arrived(g_two)
-
-    def whole(ref, *at):
-        value = ref[at]
-        return value.reshape(4 * HALF, value.shape[-1])
-
-    mix_acc[...] = jnp.zeros_like(mix_acc)
-
-    def mix_one(i, carry):
-        left, right = whole(ga, 0, i), whole(gb, 0, i)
-        mix_acc[0] += dot(left, whole(wa, i), TN) + dot(right, whole(wb, i), TN)
-        mix_acc[1] += dot(left, whole(pa, i), TN) + dot(right, whole(pb, i), TN)
-        return carry
-
-    lax.fori_loop(0, 4, mix_one, 0)
-    mix_out[0] = mix_acc[0].astype(BF)
-    m_one = remote(mix_out.at[0], mix_in.at[0], partner)
-    arrived(g_two_tan)
-
-    def mix_two(i, carry):
-        mix_acc[1] += dot(whole(ga, 1, i), whole(wa, i), TN) + dot(whole(gb, 1, i), whole(wb, i), TN)
-        return carry
-
-    lax.fori_loop(0, 4, mix_two, 0)
-    mix_out[1] = mix_acc[1].astype(BF)
-    m_two = remote(mix_out.at[1], mix_in.at[1], partner)
+    turned(ww, 0)
+    arrived(g_one[1])
+    g_two.append(gather_two(1))
+
+    def mix(h):
+        arrived(g_two[h])
+        total = jnp.zeros((2 * PART, 2 * SPAN), F32)
+        for a, ref in enumerate((ga, gb)):
+            for i in range(4):
+                total = total + dot(wpt[a, i], ref[h, i].reshape(4 * HALF, 2 * SPAN), NN)
+        mix_acc[h, :, 0:SPAN] = total[:PART, :SPAN]
+        mix_acc[h, :, SPAN:] = total[:PART, SPAN:] + total[PART:, :SPAN]
+        mix_out[h] = mix_acc[h].astype(BF)
+        return remote(mix_out.at[h], mix_in.at[h], partner)
+
+    m_both = [mix(0)]
 
     s_base = (
         (lax.broadcasted_iota(jnp.int32, (COLS, TOK), 1) + s * SHARE) * WIDE
@@ -454,27 +476,25 @@
 
     lax.fori_loop(0, SHARE // TOK, sign_cols, 0)
 
-    tgt_load.wait()
-    arrived([m_one])
-    resid = tok[:, lanes(own_cols, PART)].astype(F32) - tgt[...].astype(F32)
-    resid = resid + (mix_acc[0] + mix_in[0].astype(F32))
-    grads[0] = (resid * (1 / 1024)).astype(BF)
-
-    def back_one(i, carry):
-        grad = grads[0]
-        sa[0, i] = dot(whole(wa, i), grad, NT).astype(BF).reshape(4, HALF, TOK)
-        sb[0, i] = dot(whole(wb, i), grad, NT).astype(BF).reshape(4, HALF, TOK)
-        back_acc[0, i] = dot(whole(pa, i), grad, NT)
-        back_acc[1, i] = dot(whole(pb, i), grad, NT)
-        return carry
-
-    lax.fori_loop(0, 4, back_one, 0)
-
-    def scatter_one(t):
+    def back(h):
+        arrived([m_both[h]])
+        grads[h] = mix_acc[h] + mix_in[h].astype(F32)
+        grads[h, :, 0:SPAN] += resid[:, span(h)]
+        grad[h] = (grads[h] * (1 / 1024)).astype(BF)
+
+        def step(a, carry):
+            for i in range(4):
+                first = dot(ww[a, i].reshape(4 * HALF, PART), grad[h], NN)
+                second = dot(pp[a, i].reshape(4 * HALF, PART), grad[h, :, 0:SPAN], NN)
+                sab[h, a, i, :, :, 0:SPAN] = first[:, :SPAN].astype(BF).reshape(4, HALF, SPAN)
+                sab[h, a, i, :, :, SPAN:] = (first[:, SPAN:] + second).astype(BF).reshape(4, HALF, SPAN)
+            return carry
+
+        lax.fori_loop(0, 2, step, 0)
         copies = []
         for d in (1, 2, 3):
-            copies.append(remote(sa.at[t, (z + d) % 4], ra1.at[t, d - 1], zp(d)))
-            copies.append(remote(sb.at[t, (x + d) % 4], rb1.at[t, d - 1], xp(d)))
+            copies.append(remote(sab.at[h, 0, (z + d) % 4], ra1.at[h, d - 1], zp(d)))
+            copies.append(remote(sab.at[h, 1, (x + d) % 4], rb1.at[h, d - 1], xp(d)))
         return copies
 
     def total_of(own, others):
@@ -483,43 +503,38 @@
             total = total + other.astype(F32)
         return total
 
-    def scatter_two(t):
-        sa2[t] = total_of(sa[t, z], [ra1[t, k] for k in range(3)]).astype(BF)
-        sb2[t] = total_of(sb[t, x], [rb1[t, k] for k in range(3)]).astype(BF)
+    def scatter_two(h):
+        arrived(r_one[h])
+        sa2[h] = total_of(sab[h, 0, z], [ra1[h, k] for k in range(3)]).astype(BF)
+        sb2[h] = total_of(sab[h, 1, x], [rb1[h, k] for k in range(3)]).astype(BF)
         copies = []
         for d in (1, 2, 3):
-            copies.append(remote(sa2.at[t, (x + d) % 4], ra2.at[t, d - 1], xp(d)))
-            copies.append(remote(sb2.at[t, (z + d) % 4], rb2.at[t, d - 1], zp(d)))
+            copies.append(remote(sa2.at[h, (x + d) % 4], ra2.at[h, d - 1], xp(d)))
+            copies.append(remote(sb2.at[h, (z + d) % 4], rb2.at[h, d - 1], zp(d)))
         return copies
 
-    def scattered(t):
-        first = total_of(sa2[t, x], [ra2[t, k] for k in range(3)])
-        second = total_of(sb2[t, z], [rb2[t, k] for k in range(3)])
+    def scattered(h):
+        arrived(r_two[h])
+        first = total_of(sa2[h, x], [ra2[h, k] for k in range(3)])
+        second = total_of(sb2[h, z], [rb2[h, k] for k in range(3)])
         return jnp.concatenate([first.astype(BF), second.astype(BF)], axis=0)
 
-    r_one = scatter_one(0)
-    arrived([m_two])
-    grads[1] = ((mix_acc[1] + mix_in[1].astype(F32)) * (1 / 1024)).astype(BF)
-
-    def back_two(i, carry):
-        grad = grads[1]
-        sa[1, i] = (dot(whole(wa, i), grad, NT) + back_acc[0, i]).astype(BF).reshape(4, HALF, TOK)
-        sb[1, i] = (dot(whole(wb, i), grad, NT) + back_acc[1, i]).astype(BF).reshape(4, HALF, TOK)
-        return carry
-
-    lax.fori_loop(0, 4, back_two, 0)
-    r_one_tan = scatter_one(1)
+    r_one = [back(0)]
+    m_both.append(mix(1))
+    r_one.append(back(1))
+    r_two = [scatter_two(0)]
+
+    for h in range(2):
+        for k in range(2):
+            at = slice((2 * h + k) * SPAN, (2 * h + k + 1) * SPAN)
+            turn[at] = grad[h, :, (1 - k) * SPAN : (2 - k) * SPAN].astype(F32).T.astype(BF)
 
     def out_terms(i, carry):
-        one, two = grads[0], grads[1]
-        ha[i] = (
-            (dot(whole(ga, 1, i), one, NN) + dot(whole(ga, 0, i), two, NN))
-            .astype(BF).reshape(4, HALF, PART)
-        )
-        hb[i] = (
-            (dot(whole(gb, 1, i), one, NN) + dot(whole(gb, 0, i), two, NN))
-            .astype(BF).reshape(4, HALF, PART)
-        )
+        def joined(ref):
+            return jnp.concatenate([ref[h, i].reshape(4 * HALF, 2 * SPAN) for h in range(2)], axis=1)
+
+        ha[i] = dot(joined(ga), turn[...], NN).astype(BF).reshape(4, HALF, PART)
+        hb[i] = dot(joined(gb), turn[...], NN).astype(BF).reshape(4, HALF, PART)
         return carry
 
     lax.fori_loop(0, 4, out_terms, 0)
@@ -527,93 +542,67 @@
     for k in range(2):
         o_core.append(remote(ha.at[:, 2 * k + 1 - c], ca.at[k], sib))
         o_core.append(remote(hb.at[2 * k + 1 - c], cb.at[k], sib))
-    arrived(r_one)
-    r_two = scatter_two(0)
-
     arrived(o_core)
     far = 1 - yh
     xa[...] = total_of(ha[:, 2 * far + c], [ca[far]]).astype(BF)
     xb[...] = total_of(hb[2 * far + c], [cb[far]]).astype(BF)
     o_crs = [remote(xa, ya, crs), remote(xb, yb, crs)]
 
-    arrived(r_one_tan)
-    r_two_tan = scatter_two(1)
-
-    arrived(r_two)
-    g = scattered(0)
-
-    def pull_block(b, carry):
-        score[:, keys_of(b)] = dot(g, gkv[b, KEYS : KEYS + HS], TN)
-        return carry
-
-    lax.fori_loop(0, 4, pull_block, 0)
-    arrived(r_two_tan)
-    arrived(n_one)
-    n_two = []
-    for d in (1, 2, 3):
-        at0 = nb.at[b0, rows(z * 64, 64)]
-        at1 = nb.at[b1, rows(x * 64, 64)]
-        n_two.append(remote(at0, at0, zp(d)))
-        n_two.append(remote(at1, at1, xp(d)))
-    g_tan = scattered(1)
-    g_both = jnp.concatenate([g_tan, g], axis=0)
-
-    def value_block(b, carry):
-        at = keys_of(b)
-        cv[b] = (dot(g, rnd_tan[:, at], NN) + dot(g_tan, rnd[:, at], NN)).astype(BF)
-        return carry
-
-    lax.fori_loop(0, 4, value_block, 0)
-    v_core = [remote(cv.at[2 * k + 1 - c], cvr.at[k], sib) for k in range(2)]
-
-    def pull_block_tan(b, carry):
-        score_tan[:, keys_of(b)] = dot(g_both, gkv[b, KEYS : KEYS + 2 * HS], TN)
-        return carry
-
-    lax.fori_loop(0, 4, pull_block_tan, 0)
+    cv_acc[...] = jnp.zeros_like(cv_acc)
+    ck_acc[...] = jnp.zeros_like(ck_acc)
+
+    def soft_back(h):
+        def rows_back(i, carry):
+            at = pl.ds(pl.multiple_of(h * SPAN + i * 32, 32), 32)
+            low, high = pl.ds(pl.multiple_of(i * 32, 32), 32), pl.ds(pl.multiple_of(SPAN + i * 32, 32), 32)
+            weights, moved = prob[at, :], prob_tan[at, :]
+            pulled, pulled_tan = score[h, low, :], score[h, high, :]
+            base = jnp.sum(weights * pulled, axis=-1, keepdims=True)
+            base_tan = jnp.sum(moved * pulled + weights * pulled_tan, axis=-1, keepdims=True)
+            less = pulled - base
+            slope[h, high, :] = (weights * less).astype(BF)
+            slope[h, low, :] = (moved * less + weights * (pulled_tan - base_tan)).astype(BF)
+            return carry
+
+        lax.fori_loop(0, SPAN // 32, rows_back, 0, unroll=2)
+
+    def value_terms(h, g):
+        def step(b, carry):
+            cv_acc[b] += dot(g, rnd[h, :, keys_of(b)], NN)
+            return carry
+
+        lax.fori_loop(0, 4, step, 0, unroll=2)
+
+    def slopes(h, g):
+        one, two = g[:, :SPAN], g[:, SPAN:]
+        gg[h] = jnp.concatenate(
+            [jnp.concatenate([one, two], axis=1), jnp.concatenate([jnp.zeros_like(one), one], axis=1)],
+            axis=0,
+        ).astype(F32).T.astype(BF)
+        pulls(gg, v_part, h)
+        soft_back(h)
+
+    def key_terms(h):
+        def step(b, carry):
+            ck_acc[b] += dot(qk[h], slope[h, :, keys_of(b)], NN)
+            return carry
+
+        lax.fori_loop(0, 4, step, 0, unroll=2)
+
+    def query_terms(h):
+        terms = joint(pl.ds(0, 2 * HS), slope, h)
+        cq_acc[:, span(h)] = terms[:HS, :SPAN] + terms[HS:, SPAN:]
 
     def chip_sums(own, other, kept):
         for k in range(2):
             kept[k] = total_of(own[2 * k + c], [other[k]]).astype(BF)
 
-    arrived(v_core)
-    chip_sums(cv, cvr, cvs)
-    v_far = remote(cvs, cvf, crs)
-
-    def soft_back(i, carry):
-        at = pl.ds(pl.multiple_of(i * 32, 32), 32)
-        weights, moved = prob[at, :], prob_tan[at, :]
-        pulled, pulled_tan = score[at, :], score_tan[at, :]
-        base = jnp.sum(weights * pulled, axis=-1, keepdims=True)
-        base_tan = jnp.sum(moved * pulled + weights * pulled_tan, axis=-1, keepdims=True)
-        less = pulled - base
-        score[at, :] = weights * less
-        score_tan[at, :] = moved * less + weights * (pulled_tan - base_tan)
-        return carry
-
-    lax.fori_loop(0, TOK // 32, soft_back, 0)
-
-    def key_block(b, carry):
-        at = keys_of(b)
-        slope, slope_tan = score[:, at].astype(BF), score_tan[:, at].astype(BF)
-        ck[b] = ((dot(q, slope_tan, NN) + dot(q_tan, slope, NN)) * root).astype(BF)
-        return carry
-
-    lax.fori_loop(0, 4, key_block, 0)
-
-    k_core = [remote(ck.at[2 * k + 1 - c], ckr.at[k], sib) for k in range(2)]
-
-    def query_block(b, held):
-        at = keys_of(b)
-        slope, slope_tan = score[:, at].astype(BF), score_tan[:, at].astype(BF)
-        return held + dot(gkv[b, 0:HS], slope_tan, NT) + dot(gkv[b, HS : 2 * HS], slope, NT)
-
-    cot_query = lax.fori_loop(0, 4, query_block, jnp.zeros((HS, TOK), F32)) * root
-    cot[s, 0:HS] = rotate(cot_query.astype(BF).astype(F32), own_trig, -1.0).astype(BF)
-    q_far = remote(cot.at[s, pl.ds(0, HS)], cot.at[s, pl.ds(0, HS)], crs)
-    arrived(k_core)
-    chip_sums(ck, ckr, cks)
-    k_far = remote(cks, ckf, crs)
+    g_first = scattered(0)
+    value_terms(0, g_first)
+    r_two.append(scatter_two(1))
+    slopes(0, g_first)
+    key_terms(0)
+    query_terms(0)
 
     arrived(o_crs)
     fa[...] = total_of(ha[:, s], [ca[yh], ya[...]]).astype(BF)
@@ -627,11 +616,7 @@
         remote(fa.at[z], oa.at[z], fin(0), begin=False),
         remote(fb.at[z], ob.at[z], fin(0), begin=False),
     ]
-    near = local_count[0]
-    o_near = [
-        pltpu.make_async_copy(fa.at[z], oa.at[z], local.at[near]),
-        pltpu.make_async_copy(fb.at[z], ob.at[z], local.at[near + 1]),
-    ]
+    o_near = [nearby(fa.at[z], oa.at[z]), nearby(fb.at[z], ob.at[z])]
 
     @pl.when(x != s)
     def _():
@@ -642,6 +627,34 @@
     def _():
         for copy in o_near:
             copy.start()
+
+    g_second = scattered(1)
+    arrived(n_one)
+    n_two = []
+    for d in (1, 2, 3):
+        at0 = nb.at[b0, rows(z * 64, 64)]
+        at1 = nb.at[b1, rows(x * 64, 64)]
+        n_two.append(remote(at0, at0, zp(d)))
+        n_two.append(remote(at1, at1, xp(d)))
+    value_terms(1, g_second)
+    cv[...] = cv_acc[...].astype(BF)
+    v_core = [remote(cv.at[2 * k + 1 - c], cvr.at[k], sib) for k in range(2)]
+    slopes(1, g_second)
+    arrived(v_core)
+    chip_sums(cv, cvr, cvs)
+    v_far = remote(cvs, cvf, crs)
+    key_terms(1)
+    ck[...] = (ck_acc[...] * root).astype(BF)
+
+    k_core = [remote(ck.at[2 * k + 1 - c], ckr.at[k], sib) for k in range(2)]
+
+    query_terms(1)
+    cot_query = cq_acc[...] * root
+    cot[s, 0:HS] = rotate(cot_query.astype(BF).astype(F32), own_trig, -1.0).astype(BF)
+    q_far = remote(cot.at[s, pl.ds(0, HS)], cot.at[s, pl.ds(0, HS)], crs)
+    arrived(k_core)
+    chip_sums(ck, ckr, cks)
+    k_far = remote(cks, ckf, crs)
 
     arrived([v_far])
     for k in range(2):
@@ -701,10 +714,32 @@
         oq[:, at] = (total * sgn[:, at]).astype(BF)
         return carry
 
-    lax.fori_loop(0, SHARE // TOK, last_terms, 0)
+    leaving = [stay(oo, oo_out)]
+    for k in range(2):
+        lax.fori_loop(k * 3, k * 3 + 3, last_terms, 0)
+        cols = pl.ds(k * SHARE // 2, SHARE // 2)
+        leaving.append(stay(oq.at[:, cols], oq_out.at[:, cols]))
+    for copy in leaving:
+        copy.wait()
 
     for copy in sent:
         copy.wait_send()
+
+
+def widen(product_in, out_in, product, out, narrow, narrow_out, wide, wide_out, loads, stores):
+    thirds = [pl.ds(k * SHARE // 3, SHARE // 3) for k in range(3)]
+    parts = [(product_in.at[:, at], narrow.at[k], wide.at[k], product.at[:, at]) for k, at in enumerate(thirds)]
+    parts.append((out_in, narrow_out, wide_out, out))
+    arrive = [pltpu.make_async_copy(part[0], part[1], loads.at[k]) for k, part in enumerate(parts)]
+    leave = [pltpu.make_async_copy(part[2], part[3], stores.at[k]) for k, part in enumerate(parts)]
+    for copy in arrive:
+        copy.start()
+    for k, part in enumerate(parts):
+        arrive[k].wait()
+        part[2][...] = part[1][...].astype(F32)
+        leave[k].start()
+    for copy in leave:
+        copy.wait()
 
 
 def tables():
@@ -720,23 +755,25 @@
 def per_device(tokens, target, norm_gain, qkv_weight, out_weight, probe_seed, block_order):
     tab_t, tab_b = tables()
     anywhere = pl.BlockSpec(memory_space=pl.ANY)
-    vmem = pl.BlockSpec(memory_space=pltpu.VMEM)
     smem = pl.BlockSpec(memory_space=pltpu.SMEM)
     v = pltpu.VMEM
     scratch = [
+        v((COLS, SHARE), BF), v((HS, SHARE), BF), v((1, D), F32), v((2, ROT, TOK), F32), v((4, 2, ROT, TOK), F32),
         v((TOK, D), BF), v((TOK, PART), BF), v((COLS, D), BF), v((TOK, D), BF), v((2, COLS, TOK), F32),
         v((2, TOK, 128), F32), v((4, TOK, SHARE), BF), v((4, 4 * HS + 16, TOK), BF),
-        v((4, 4, HALF, PART), BF), v((2, 4, 4, HALF, PART), BF),
-        v((4, 4, HALF, PART), BF), v((4, 4, HALF, PART), BF),
-        v((2, 4, 4, HALF, TOK), BF), v((2, 4, 4, HALF, TOK), BF),
-        v((TOK, 1024), F32), v((TOK, 1024), F32), v((TOK, 1024), F32), v((TOK, 1024), F32),
-        v((TOK, 1024), BF), v((TOK, 1024), BF),
-        v((2, TOK, PART), F32), v((2, TOK, PART), BF), v((2, TOK, PART), BF), v((2, TOK, PART), BF),
-        v((2, 4, 4 * HALF, TOK), F32),
-        v((2, 4, 4, HALF, TOK), BF), v((2, 4, 4, HALF, TOK), BF),
-        v((2, 3, 4, HALF, TOK), BF), v((2, 3, 4, HALF, TOK), BF),
-        v((2, 4, HALF, TOK), BF), v((2, 4, HALF, TOK), BF),
-        v((2, 3, HALF, TOK), BF), v((2, 3, HALF, TOK), BF),
+        v((4, 4, HALF, PART), BF), v((2, 4, 4, HALF, PART), BF), v((2, 4, 4, HALF, PART), BF),
+        v((2, 4, 2 * PART, 4 * HALF), BF),
+        v((2, 4, 4, HALF, 2 * SPAN), BF), v((2, 4, 4, HALF, 2 * SPAN), BF),
+        v((2, 2 * SPAN, 2 * HS), BF), v((2, HS, 2 * SPAN), BF), v((2, 2 * SPAN, 2 * HS), BF),
+        v((2, 2 * SPAN, 1024), F32), v((TOK, 1024), F32), v((TOK, 1024), F32),
+        v((2, 2 * SPAN, 1024), BF), v((2, 2 * SPAN, 1024), BF),
+        v((4, HS, TOK), F32), v((4, HS, TOK), F32), v((HS, TOK), F32),
+        v((2, PART, 2 * SPAN), F32), v((2, PART, 2 * SPAN), BF), v((2, PART, 2 * SPAN), BF),
+        v((2, PART, 2 * SPAN), F32), v((2, PART, 2 * SPAN), BF), v((4 * SPAN, PART), BF), v((PART, TOK), F32),
+        v((2, 2, 4, 4, HALF, 2 * SPAN), BF),
+        v((2, 3, 4, HALF, 2 * SPAN), BF), v((2, 3, 4, HALF, 2 * SPAN), BF),
+        v((2, 4, HALF, 2 * SPAN), BF), v((2, 4, HALF, 2 * SPAN), BF),
+        v((2, 3, HALF, 2 * SPAN), BF), v((2, 3, HALF, 2 * SPAN), BF),
         v((4, 4, HALF, PART), BF), v((4, 4, HALF, PART), BF),
         v((2, 4, HALF, PART), BF), v((2, 4, HALF, PART), BF),
         v((4, HALF, PART), BF), v((4, HALF, PART), BF), v((4, HALF, PART), BF), v((4, HALF, PART), BF),
@@ -753,8 +790,8 @@
             jax.ShapeDtypeStruct((COLS, SHARE), BF),
             jax.ShapeDtypeStruct((HS, SHARE), BF),
         ),
-        in_specs=[anywhere, anywhere, vmem, anywhere, anywhere, smem, smem, vmem, vmem],
-        out_specs=(vmem, vmem),
+        in_specs=[anywhere, anywhere, anywhere, anywhere, anywhere, smem, smem, anywhere, anywhere],
+        out_specs=(anywhere, anywhere),
         scratch_shapes=scratch,
         compiler_params=pltpu.CompilerParams(
             collective_id=0, has_side_effects=True, vmem_limit_bytes=60 * 2**20
@@ -763,7 +800,21 @@
         tokens, target, norm_gain.reshape(1, D), qkv_weight.T, out_weight, probe_seed, block_order,
         jnp.asarray(tab_t), jnp.asarray(tab_b),
     )
-    return product.astype(F32).T, out_curv.astype(F32)
+    product, out_curv = pl.pallas_call(
+        widen,
+        out_shape=(
+            jax.ShapeDtypeStruct((COLS, SHARE), F32),
+            jax.ShapeDtypeStruct((HS, SHARE), F32),
+        ),
+        in_specs=[anywhere, anywhere],
+        out_specs=(anywhere, anywhere),
+        scratch_shapes=[
+            v((3, COLS, SHARE // 3), BF), v((HS, SHARE), BF),
+            v((3, COLS, SHARE // 3), F32), v((HS, SHARE), F32),
+            pltpu.SemaphoreType.DMA((4,)), pltpu.SemaphoreType.DMA((4,)),
+        ],
+    )(product, out_curv)
+    return product.T, out_curv
 
 
 def solution(mesh):

time: 94.9 us -> 86.8 us (0.915)
  the two profiles are of different devices: /device:TPU:7 before, /device:TPU:0 now
where the time goes in v5:
time: 86.8 us; the launch traced here: 86.6 us
  Pallas kernels  84.7 us (98%)
  between operations  1.93 us (2%)
    pallas_call x1, Pallas kernels, per_device(): pl.pallas_call(kernel, out_shape=(jax.ShapeDtypeStruct((COLS, SHARE), BF)...  82.2 us
    pallas_call x1, Pallas kernels, per_device(): pl.pallas_call(widen, out_shape=(jax.ShapeDtypeStruct((COLS, SHARE), F32)...  2.47 us

profile of v5, /device:TPU:0, one launch (start us, length us, event | category | flops | bytes accessed | tf_op | source)
XLA Modules:
  0.0 86.6 jit_solution(9813269267564000214)
XLA Ops:
  1.9 82.2 %shard_map.104 = (bf16[288,1536]{1,0:T(8,128)(2,1)}, bf16[96,1536]{1,0:T(8,128)(2,1)}) custom-call(bf16[256,6144]{1,0:T(8,128)(2,1)} %tok_in.1, bf16[256,6144]{1,0:T(8,128)(2,1)} %tgt_in.1, f32[1,6144]{1,0:T(1,128)} %bitcast.4, bf16[288,6144]{1,0:T(8,128)(2,1)} %bitcast.3, bf16[96,6144]{1,0:T(8,128)(2,1)} %wo_in.1, s32[1]{0:T(128)S(6)} %copy.11.seed, ...), custom_call_target="tpu_custom_call" | custom-call | tf_op jit(solution)/shard_map/pallas_call | solution.py:787
  84.1 2.5 %shard_map.105 = (f32[288,1536]{1,0:T(8,128)}, f32[96,1536]{1,0:T(8,128)}) custom-call(bf16[288,1536]{1,0:T(8,128)(2,1)} %get-tuple-element.6.product_in, bf16[96,1536]{1,0:T(8,128)(2,1)} %get-tuple-element.7.out_in), custom_call_target="tpu_custom_call" | custom-call | tf_op jit(solution)/shard_map/pallas_call | solution.py:803

commit v6 on v5

--- a/solution.py
+++ b/solution.py
@@ -26,8 +26,8 @@
 KEYS = 2 * HS + 16
 STEP = 768
 MIX = (-1640531535, -2048144789, -1028477387)
-N_REMOTE = 120
-N_LOCAL = 24
+N_REMOTE = 40
+N_LOCAL = 25
 
 
 def wrap(value):
@@ -55,17 +55,28 @@
 TN = ((0,), (0,))
 
 
+class Group:
+    def __init__(self, size, send, recv):
+        self.size, self.send, self.recv = size, send, recv
+
+    def wait_recv(self):
+        pltpu.make_async_copy(self.size, self.size, self.recv).wait()
+
+    def wait_send(self):
+        pltpu.make_async_copy(self.size, self.size, self.send).wait()
+
+
 def kernel(
-    tok_in, tgt_in, gain_in, wq_in, wo_in, seed, block, tab_t_in, tab_b_in,
+    tok_in, tgt_in, gain_in, wq_in, wo_in, seed_in, block_in, tab_t_in, tab_b_in,
     oq_out, oo_out,
-    oq, oo, gain, tab_t, tab_b, tok, tgt, wq, nrm, acc,
+    seed, block, oq, oo, gain, tab_t, tab_b, tok, tgt, wq, nrm, acc,
     stat, nb, gkv,
     wt, ww, pp, wpt, ga, gb,
     qq, qk, gg, score, prob, prob_tan, rnd, slope, cv_acc, ck_acc, cq_acc,
     mix_acc, mix_out, mix_in, grads, grad, turn, resid,
     sab, ra1, rb1, sa2, sb2, ra2, rb2,
     ha, hb, ca, cb, xa, xb, ya, yb, fa, fb, oa, ob,
-    cv, cvr, cvs, cvf, ck, ckr, cks, ckf, cot, sgn, part,
+    cv, cvr, cvs, cvf, ck, ckr, cks, ckf, cot, sgn, acc_q, out_acc,
     send, recv, local,
 ):
     fs = lax.axis_index("fsdp")
@@ -100,17 +111,21 @@
     count = [0]
     sent = []
 
-    def remote(src, dst, to, begin=True):
+    def group(size):
         i = count[0]
         count[0] += 1
+        sent.append(Group(size, send.at[i], recv.at[i]))
+        return sent[-1]
+
+    def remote(src, dst, to, within=None, begin=True):
+        held = within or group(dst)
         copy = pltpu.make_async_remote_copy(
-            src_ref=src, dst_ref=dst, send_sem=send.at[i], recv_sem=recv.at[i],
+            src_ref=src, dst_ref=dst, send_sem=held.send, recv_sem=held.recv,
             device_id=to, device_id_type=MESH,
         )
         if begin:
             copy.start()
-            sent.append(copy)
-        return copy
+        return copy if not begin else held
 
     local_count = [0]
 
@@ -137,7 +152,7 @@
         return pl.ds(pl.multiple_of(start, 16), size)
 
     tok_loads = [stay(tok_in.at[pl.ds(k * 64, 64)], tok.at[pl.ds(k * 64, 64)]) for k in range(4)]
-    tab_loads = [stay(gain_in, gain), stay(tab_t_in, tab_t), stay(tab_b_in, tab_b)]
+    tab_loads = [stay(seed_in, seed), stay(block_in, block), stay(gain_in, gain), stay(tab_t_in, tab_t), stay(tab_b_in, tab_b)]
     tgt_load = stay(tgt_in.at[:, lanes(own_cols, PART)], tgt)
     first, second = jnp.where(c == 0, x, z), jnp.where(c == 0, z, x)
 
@@ -207,14 +222,12 @@
             jnp.where(c == 0, x, (x + d) % 4), yl, jnp.where(c == 0, (z + d) % 4, z), s
         )
 
-    w_one = []
+    w_one = group(wt.at[pl.ds(0, 3)])
     for d in (1, 2, 3):
         for k in range(4):
-            w_one.append(
-                remote(
-                    wo_in.at[rows(c * HALF, HALF), lanes(column((first + d) % 4, k), PART)],
-                    wt.at[first, k], along_first(d),
-                )
+            remote(
+                wo_in.at[rows(c * HALF, HALF), lanes(column((first + d) % 4, k), PART)],
+                wt.at[first, k], along_first(d), w_one,
             )
 
     for copy in tab_loads:
@@ -231,11 +244,12 @@
     lax.fori_loop(0, TOK // 16, norm_rows, 0)
 
     piece = jnp.where(c == 0, z * 4 + x, x * 4 + z) * 16
-    n_crs = remote(
-        nrm.at[rows(piece, 16), lanes(s_crs * SHARE, SHARE)], nb.at[s, rows(piece, 16)], crs
+    n_far = group(nb.at[0, pl.ds(0, 32)])
+    remote(
+        nrm.at[rows(piece, 16), lanes(s_crs * SHARE, SHARE)], nb.at[s, rows(piece, 16)], crs, n_far
     )
-    n_crd = remote(
-        nrm.at[rows(piece, 16), lanes(s_crd * SHARE, SHARE)], nb.at[s, rows(piece, 16)], crd
+    remote(
+        nrm.at[rows(piece, 16), lanes(s_crd * SHARE, SHARE)], nb.at[s, rows(piece, 16)], crd, n_far
     )
     n_sib = remote(nrm.at[:, lanes(s_sib * SHARE, SHARE)], nb.at[s], sib)
 
@@ -318,20 +332,20 @@
 
     b0 = (1 - yh) * 2
     b1 = b0 + 1
-    arrived([n_crs, n_crd])
-    n_one = []
+    arrived([n_far])
+    n_one = group(nb.at[0, pl.ds(0, 96)])
     for d in (1, 2, 3):
         at0 = nb.at[b0, rows((z * 4 + x) * 16, 16)]
         at1 = nb.at[b1, rows((x * 4 + z) * 16, 16)]
-        n_one.append(remote(at0, at0, xp(d)))
-        n_one.append(remote(at1, at1, zp(d)))
+        remote(at0, at0, xp(d), n_one)
+        remote(at1, at1, zp(d), n_one)
 
     for copy in own_w:
         copy.wait()
-    arrived(w_one)
-    w_two = []
+    arrived([w_one])
+    w_two = group(ww.at[0, pl.ds(0, 3)])
     for d in (1, 2, 3):
-        w_two.append(remote(wt.at[:, (second + d) % 4], ww.at[c, second], along_second(d)))
+        remote(wt.at[:, (second + d) % 4], ww.at[c, second], along_second(d), w_two)
     own_ww = stay(wt.at[:, second], ww.at[c, second])
 
     o_rows = lax.broadcasted_iota(jnp.int32, (HALF, PART), 0)
@@ -360,6 +374,15 @@
         lax.fori_loop(0, 4, turn, 0)
 
     turned(pp, PART)
+
+    def spread_normed(cols):
+        held = group(nb.at[pl.ds(0, 2), pl.ds(0, 192), cols])
+        for d in (1, 2, 3):
+            at0 = nb.at[b0, rows(z * 64, 64), cols]
+            at1 = nb.at[b1, rows(x * 64, 64), cols]
+            remote(at0, at0, zp(d), held)
+            remote(at1, at1, xp(d), held)
+        return held
 
     arrived([k_crs])
     k_rel = spread_kv(s_crs, k_part, sib)
@@ -418,18 +441,18 @@
         both = both.astype(BF)
         ga[h, z, x] = both[:HALF]
         gb[h, x, z] = both[HALF:]
-        copies = []
+        held = group(ra1.at[0, pl.ds(0, 3), pl.ds(0, 2)])
         for d in (1, 2, 3):
-            copies.append(remote(ga.at[h, z, x], ga.at[h, z, x], xp(d)))
-            copies.append(remote(gb.at[h, x, z], gb.at[h, x, z], zp(d)))
-        return copies
+            remote(ga.at[h, z, x], ga.at[h, z, x], xp(d), held)
+            remote(gb.at[h, x, z], gb.at[h, x, z], zp(d), held)
+        return held
 
     def gather_two(h):
-        copies = []
+        held = group(ra1)
         for d in (1, 2, 3):
-            copies.append(remote(ga.at[h, z], ga.at[h, z], zp(d)))
-            copies.append(remote(gb.at[h, x], gb.at[h, x], xp(d)))
-        return copies
+            remote(ga.at[h, z], ga.at[h, z], zp(d), held)
+            remote(gb.at[h, x], gb.at[h, x], xp(d), held)
+        return held
 
     pulls(qq, pl.ds(0, 2 * HS), 0)
     soft(0)
@@ -437,21 +460,23 @@
     g_one = [attn_products(0)]
     pulls(qq, pl.ds(0, 2 * HS), 1)
     own_ww.wait()
-    arrived(w_two)
+    arrived([w_two])
     w_sib = remote(ww.at[c], ww.at[c], sib)
     soft(1)
 
-    arrived(g_one[0])
+    g_one.append(attn_products(1))
+
+    arrived([g_one[0]])
     g_two = [gather_two(0)]
-    g_one.append(attn_products(1))
-
     arrived([w_sib])
     turned(ww, 0)
-    arrived(g_one[1])
+    arrived([g_one[1]])
     g_two.append(gather_two(1))
+    arrived([n_one])
+    n_two = [spread_normed(pl.ds(0, SHARE // 2))]
 
     def mix(h):
-        arrived(g_two[h])
+        arrived([g_two[h]])
         total = jnp.zeros((2 * PART, 2 * SPAN), F32)
         for a, ref in enumerate((ga, gb)):
             for i in range(4):
@@ -461,7 +486,7 @@
         mix_out[h] = mix_acc[h].astype(BF)
         return remote(mix_out.at[h], mix_in.at[h], partner)
 
-    m_both = [mix(0)]
+    m_both = [mix(0), mix(1)]
 
     s_base = (
         (lax.broadcasted_iota(jnp.int32, (COLS, TOK), 1) + s * SHARE) * WIDE
@@ -491,11 +516,11 @@
             return carry
 
         lax.fori_loop(0, 2, step, 0)
-        copies = []
+        held = group(ra1)
         for d in (1, 2, 3):
-            copies.append(remote(sab.at[h, 0, (z + d) % 4], ra1.at[h, d - 1], zp(d)))
-            copies.append(remote(sab.at[h, 1, (x + d) % 4], rb1.at[h, d - 1], xp(d)))
-        return copies
+            remote(sab.at[h, 0, (z + d) % 4], ra1.at[h, d - 1], zp(d), held)
+            remote(sab.at[h, 1, (x + d) % 4], rb1.at[h, d - 1], xp(d), held)
+        return held
 
     def total_of(own, others):
         total = own.astype(F32)
@@ -504,49 +529,56 @@
         return total
 
     def scatter_two(h):
-        arrived(r_one[h])
+        arrived([r_one[h]])
         sa2[h] = total_of(sab[h, 0, z], [ra1[h, k] for k in range(3)]).astype(BF)
         sb2[h] = total_of(sab[h, 1, x], [rb1[h, k] for k in range(3)]).astype(BF)
-        copies = []
+        held = group(ra2)
         for d in (1, 2, 3):
-            copies.append(remote(sa2.at[h, (x + d) % 4], ra2.at[h, d - 1], xp(d)))
-            copies.append(remote(sb2.at[h, (z + d) % 4], rb2.at[h, d - 1], zp(d)))
-        return copies
+            remote(sa2.at[h, (x + d) % 4], ra2.at[h, d - 1], xp(d), held)
+            remote(sb2.at[h, (z + d) % 4], rb2.at[h, d - 1], zp(d), held)
+        return held
 
     def scattered(h):
-        arrived(r_two[h])
+        arrived([r_two[h]])
         first = total_of(sa2[h, x], [ra2[h, k] for k in range(3)])
         second = total_of(sb2[h, z], [rb2[h, k] for k in range(3)])
         return jnp.concatenate([first.astype(BF), second.astype(BF)], axis=0)
 
-    r_one = [back(0)]
-    m_both.append(mix(1))
-    r_one.append(back(1))
-    r_two = [scatter_two(0)]
-
-    for h in range(2):
+    def out_terms(h):
         for k in range(2):
             at = slice((2 * h + k) * SPAN, (2 * h + k + 1) * SPAN)
             turn[at] = grad[h, :, (1 - k) * SPAN : (2 - k) * SPAN].astype(F32).T.astype(BF)
 
-    def out_terms(i, carry):
-        def joined(ref):
-            return jnp.concatenate([ref[h, i].reshape(4 * HALF, 2 * SPAN) for h in range(2)], axis=1)
-
-        ha[i] = dot(joined(ga), turn[...], NN).astype(BF).reshape(4, HALF, PART)
-        hb[i] = dot(joined(gb), turn[...], NN).astype(BF).reshape(4, HALF, PART)
-        return carry
-
-    lax.fori_loop(0, 4, out_terms, 0)
-    o_core = []
-    for k in range(2):
-        o_core.append(remote(ha.at[:, 2 * k + 1 - c], ca.at[k], sib))
-        o_core.append(remote(hb.at[2 * k + 1 - c], cb.at[k], sib))
-    arrived(o_core)
+        def term(i, carry):
+            right = turn[2 * h * SPAN : 2 * (h + 1) * SPAN]
+            for a, (ref, to) in enumerate(((ga, ha), (gb, hb))):
+                total = dot(ref[h, i].reshape(4 * HALF, 2 * SPAN), right, NN)
+                if h == 0:
+                    out_acc[a, i] = total
+                else:
+                    to[i] = (out_acc[a, i] + total).astype(BF).reshape(4, HALF, PART)
+            return carry
+
+        lax.fori_loop(0, 4, term, 0)
+
+    r_one = [back(0)]
+    out_terms(0)
+    r_one.append(back(1))
+    out_terms(1)
+
+    o_core = group(ha)
+    for k in range(2):
+        remote(ha.at[:, 2 * k + 1 - c], ca.at[k], sib, o_core)
+        remote(hb.at[2 * k + 1 - c], cb.at[k], sib, o_core)
+    r_two = [scatter_two(0)]
+
+    arrived([o_core])
     far = 1 - yh
     xa[...] = total_of(ha[:, 2 * far + c], [ca[far]]).astype(BF)
     xb[...] = total_of(hb[2 * far + c], [cb[far]]).astype(BF)
-    o_crs = [remote(xa, ya, crs), remote(xb, yb, crs)]
+    o_crs = group(ca)
+    remote(xa, ya, crs, o_crs)
+    remote(xb, yb, crs, o_crs)
 
     cv_acc[...] = jnp.zeros_like(cv_acc)
     ck_acc[...] = jnp.zeros_like(ck_acc)
@@ -604,17 +636,27 @@
     key_terms(0)
     query_terms(0)
 
-    arrived(o_crs)
+    g_second = scattered(1)
+    n_two.append(spread_normed(pl.ds(SHARE // 2, SHARE // 2)))
+    value_terms(1, g_second)
+    cv[...] = cv_acc[...].astype(BF)
+    v_core = group(cvr)
+    for k in range(2):
+        remote(cv.at[2 * k + 1 - c], cvr.at[k], sib, v_core)
+    arrived([o_crs])
     fa[...] = total_of(ha[:, s], [ca[yh], ya[...]]).astype(BF)
     fb[...] = total_of(hb[s], [cb[yh], yb[...]]).astype(BF)
-    o_fin = []
+    o_fin = group(ca.at[0, pl.ds(0, 3)])
+    o_fin_b = group(ca.at[0, pl.ds(0, 3)])
     for d in (1, 2, 3):
         other = (z + d) % 4
-        o_fin.append(remote(fa.at[other], oa.at[z], fin(d)))
-        o_fin.append(remote(fb.at[other], ob.at[z], fin(d)))
+        remote(fa.at[other], oa.at[z], fin(d), o_fin)
+        remote(fb.at[other], ob.at[z], fin(d), o_fin_b)
+    lone = [Group(fa.at[z], send.at[count[0] + k], recv.at[count[0] + k]) for k in range(2)]
+    count[0] += 2
     o_far = [
-        remote(fa.at[z], oa.at[z], fin(0), begin=False),
-        remote(fb.at[z], ob.at[z], fin(0), begin=False),
+        remote(fa.at[z], oa.at[z], fin(0), lone[0], begin=False),
+        remote(fb.at[z], ob.at[z], fin(0), lone[1], begin=False),
     ]
     o_near = [nearby(fa.at[z], oa.at[z]), nearby(fb.at[z], ob.at[z])]
 
@@ -628,58 +670,74 @@
         for copy in o_near:
             copy.start()
 
-    g_second = scattered(1)
-    arrived(n_one)
-    n_two = []
-    for d in (1, 2, 3):
-        at0 = nb.at[b0, rows(z * 64, 64)]
-        at1 = nb.at[b1, rows(x * 64, 64)]
-        n_two.append(remote(at0, at0, zp(d)))
-        n_two.append(remote(at1, at1, xp(d)))
-    value_terms(1, g_second)
-    cv[...] = cv_acc[...].astype(BF)
-    v_core = [remote(cv.at[2 * k + 1 - c], cvr.at[k], sib) for k in range(2)]
     slopes(1, g_second)
-    arrived(v_core)
+    arrived([v_core])
     chip_sums(cv, cvr, cvs)
     v_far = remote(cvs, cvf, crs)
     key_terms(1)
     ck[...] = (ck_acc[...] * root).astype(BF)
 
-    k_core = [remote(ck.at[2 * k + 1 - c], ckr.at[k], sib) for k in range(2)]
-
+    k_core = group(ckr)
+    for k in range(2):
+        remote(ck.at[2 * k + 1 - c], ckr.at[k], sib, k_core)
     query_terms(1)
-    cot_query = cq_acc[...] * root
-    cot[s, 0:HS] = rotate(cot_query.astype(BF).astype(F32), own_trig, -1.0).astype(BF)
-    q_far = remote(cot.at[s, pl.ds(0, HS)], cot.at[s, pl.ds(0, HS)], crs)
-    arrived(k_core)
+    q_part, k_rows, head_part = pl.ds(0, HS), pl.ds(HS, HS), pl.ds(0, 2 * HS)
+    tail_part = pl.ds(2 * HS, HS)
+    cot[s, q_part] = rotate((cq_acc[...] * root).astype(BF).astype(F32), own_trig, -1.0).astype(BF)
+    arrived([k_core])
     chip_sums(ck, ckr, cks)
     k_far = remote(cks, ckf, crs)
+    q_far = remote(cot.at[s, q_part], cot.at[s, q_part], crs)
 
     arrived([v_far])
     for k in range(2):
-        cot[2 * k + c, 2 * HS : 3 * HS] = total_of(cvs[k], [cvf[k]]).astype(BF)
+        cot[2 * k + c, tail_part] = total_of(cvs[k], [cvf[k]]).astype(BF)
+    t_tail = group(cvr)
+    for k in range(2):
+        remote(cot.at[2 * k + c, tail_part], cot.at[2 * k + c, tail_part], sib, t_tail)
     turns = [
         trig(jnp.broadcast_to(gkv[2 * k + c, KEYS - 16 : KEYS].astype(F32)[0:1], (ROT, TOK)))
         for k in range(2)
     ]
+    arrived([n_sib] + n_two)
+
+    def first_terms(part):
+        def term(i, carry):
+            at = lanes(i * TOK, TOK)
+            acc_q[part, at] = dot(cot[s, part], nrm[:, lanes(s * SHARE + i * TOK, TOK)], NN) + dot(
+                cot[s_crs, part], nb[s_crs, :, at], NN
+            )
+            return carry
+
+        lax.fori_loop(0, SHARE // TOK, term, 0, unroll=2)
+
+    def last_terms(part, start, stop):
+        def term(i, carry):
+            at = lanes(i * TOK, TOK)
+            total = acc_q[part, at] + (
+                dot(cot[s_sib, part], nb[s_sib, :, at], NN) + dot(cot[s_crd, part], nb[s_crd, :, at], NN)
+            )
+            oq[part, at] = (total * sgn[part, at]).astype(BF)
+            return carry
+
+        lax.fori_loop(start, stop, term, 0, unroll=3)
+
+    first_terms(tail_part)
+    arrived([t_tail])
+    last_terms(tail_part, 0, 6)
+    leaving = [stay(oq.at[tail_part], oq_out.at[tail_part])]
+
     arrived([k_far])
     for k in range(2):
         both = total_of(cks[k], [ckf[k]]).astype(BF).astype(F32)
-        cot[2 * k + c, HS : 2 * HS] = rotate(both, turns[k], -1.0).astype(BF)
+        cot[2 * k + c, k_rows] = rotate(both, turns[k], -1.0).astype(BF)
     arrived([q_far])
-    t_sib = [remote(cot.at[2 * k + c], cot.at[2 * k + c], sib) for k in range(2)]
-    arrived([n_sib] + n_two)
-
-    def first_terms(i, carry):
-        at = lanes(i * TOK, TOK)
-        part[:, at] = dot(cot[s], nrm[:, lanes(s * SHARE + i * TOK, TOK)], NN) + dot(
-            cot[s_crs], nb[s_crs, :, at], NN
-        )
-        return carry
-
-    lax.fori_loop(0, SHARE // TOK, first_terms, 0)
-    arrived(o_fin)
+    t_head = group(cot.at[pl.ds(0, 2), head_part])
+    for k in range(2):
+        remote(cot.at[2 * k + c, head_part], cot.at[2 * k + c, head_part], sib, t_head)
+    first_terms(head_part)
+
+    arrived([o_fin, o_fin_b])
 
     @pl.when(x != s)
     def _():
@@ -706,19 +764,12 @@
             ).astype(BF)
 
 
-    arrived(t_sib)
-
-    def last_terms(i, carry):
-        at = lanes(i * TOK, TOK)
-        total = part[:, at] + (dot(cot[s_sib], nb[s_sib, :, at], NN) + dot(cot[s_crd], nb[s_crd, :, at], NN))
-        oq[:, at] = (total * sgn[:, at]).astype(BF)
-        return carry
-
-    leaving = [stay(oo, oo_out)]
-    for k in range(2):
-        lax.fori_loop(k * 3, k * 3 + 3, last_terms, 0)
+    leaving.append(stay(oo, oo_out))
+    arrived([t_head])
+    for k in range(2):
+        last_terms(head_part, k * 3, k * 3 + 3)
         cols = pl.ds(k * SHARE // 2, SHARE // 2)
-        leaving.append(stay(oq.at[:, cols], oq_out.at[:, cols]))
+        leaving.append(stay(oq.at[head_part, cols], oq_out.at[head_part, cols]))
     for copy in leaving:
         copy.wait()
 
@@ -755,9 +806,9 @@
 def per_device(tokens, target, norm_gain, qkv_weight, out_weight, probe_seed, block_order):
     tab_t, tab_b = tables()
     anywhere = pl.BlockSpec(memory_space=pl.ANY)
-    smem = pl.BlockSpec(memory_space=pltpu.SMEM)
     v = pltpu.VMEM
     scratch = [
+        pltpu.SMEM((1,), jnp.int32), pltpu.SMEM((1,), jnp.int32),
         v((COLS, SHARE), BF), v((HS, SHARE), BF), v((1, D), F32), v((2, ROT, TOK), F32), v((4, 2, ROT, TOK), F32),
         v((TOK, D), BF), v((TOK, PART), BF), v((COLS, D), BF), v((TOK, D), BF), v((2, COLS, TOK), F32),
         v((2, TOK, 128), F32), v((4, TOK, SHARE), BF), v((4, 4 * HS + 16, TOK), BF),
@@ -780,7 +831,7 @@
         v((4, HALF, PART), BF), v((4, HALF, PART), BF), v((4, HALF, PART), BF), v((4, HALF, PART), BF),
         v((4, HS, TOK), BF), v((2, HS, TOK), BF), v((2, HS, TOK), BF), v((2, HS, TOK), BF),
         v((4, HS, TOK), BF), v((2, HS, TOK), BF), v((2, HS, TOK), BF), v((2, HS, TOK), BF),
-        v((4, 3 * HS, TOK), BF), v((COLS, SHARE), F32), v((COLS, SHARE), F32),
+        v((4, 3 * HS, TOK), BF), v((COLS, SHARE), F32), v((COLS, SHARE), F32), v((2, 4, 4 * HALF, PART), F32),
         pltpu.SemaphoreType.DMA((N_REMOTE,)), pltpu.SemaphoreType.DMA((N_REMOTE,)),
         pltpu.SemaphoreType.DMA((N_LOCAL,)),
     ]
@@ -790,7 +841,7 @@
             jax.ShapeDtypeStruct((COLS, SHARE), BF),
             jax.ShapeDtypeStruct((HS, SHARE), BF),
         ),
-        in_specs=[anywhere, anywhere, anywhere, anywhere, anywhere, smem, smem, anywhere, anywhere],
+        in_specs=[anywhere] * 9,
         out_specs=(anywhere, anywhere),
         scratch_shapes=scratch,
         compiler_params=pltpu.CompilerParams(

time: 86.8 us -> 82 us (0.945)
  the two profiles are of different devices: /device:TPU:0 before, /device:TPU:25 now
where the time goes in v6:
time: 82 us; the launch traced here: 81.8 us
  Pallas kernels  79.9 us (97%)
  between operations  1.93 us (2%)
    pallas_call x1, Pallas kernels, per_device(): pl.pallas_call(kernel, out_shape=(jax.ShapeDtypeStruct((COLS, SHARE), BF)...  77.4 us
    pallas_call x1, Pallas kernels, per_device(): pl.pallas_call(widen, out_shape=(jax.ShapeDtypeStruct((COLS, SHARE), F32)...  2.47 us

profile of v6, /device:TPU:25, one launch (start us, length us, event | category | flops | bytes accessed | tf_op | source)
XLA Modules:
  0.0 81.8 jit_solution(16803239256627625622)
XLA Ops:
  1.9 77.4 %shard_map.104 = (bf16[288,1536]{1,0:T(8,128)(2,1)}, bf16[96,1536]{1,0:T(8,128)(2,1)}) custom-call(bf16[256,6144]{1,0:T(8,128)(2,1)} %tok_in.1, bf16[256,6144]{1,0:T(8,128)(2,1)} %tgt_in.1, f32[1,6144]{1,0:T(1,128)} %bitcast.4, bf16[288,6144]{1,0:T(8,128)(2,1)} %bitcast.3, bf16[96,6144]{1,0:T(8,128)(2,1)} %wo_in.1, s32[1]{0:T(128)S(6)} %copy.11.seed_in, ...), custom_call_target="tpu_custom_call" | custom-call | tf_op jit(solution)/shard_map/pallas_call | solution.py:838
  79.3 2.5 %shard_map.105 = (f32[288,1536]{1,0:T(8,128)}, f32[96,1536]{1,0:T(8,128)}) custom-call(bf16[288,1536]{1,0:T(8,128)(2,1)} %get-tuple-element.6.product_in, bf16[96,1536]{1,0:T(8,128)(2,1)} %get-tuple-element.7.out_in), custom_call_target="tpu_custom_call" | custom-call | tf_op jit(solution)/shard_map/pallas_call | solution.py:854

commit v7 on v6

--- a/solution.py
+++ b/solution.py
@@ -26,7 +26,7 @@
 KEYS = 2 * HS + 16
 STEP = 768
 MIX = (-1640531535, -2048144789, -1028477387)
-N_REMOTE = 40
+N_REMOTE = 48
 N_LOCAL = 25
 
 
@@ -73,7 +73,7 @@
     stat, nb, gkv,
     wt, ww, pp, wpt, ga, gb,
     qq, qk, gg, score, prob, prob_tan, rnd, slope, cv_acc, ck_acc, cq_acc,
-    mix_acc, mix_out, mix_in, grads, grad, turn, resid,
+    mix_acc, mix_out, mix_in, back_acc, grad, turn, resid,
     sab, ra1, rb1, sa2, sb2, ra2, rb2,
     ha, hb, ca, cb, xa, xb, ya, yb, fa, fb, oa, ob,
     cv, cvr, cvs, cvf, ck, ckr, cks, ckf, cot, sgn, acc_q, out_acc,
@@ -100,8 +100,14 @@
     def zp(d):
         return device(x, yl, (z + d) % 4, s)
 
+    kept = (s + 2 * (x % 2)) % 4
+    alone = (x == s) & (x % 2 == 0)
+
     def fin(d):
-        return device(s, yl, (z + d) % 4, x)
+        return device(kept, yl, (z + d) % 4, x)
+
+    def fin_from(d):
+        return device(s, yl, (z + d) % 4, (x + 2 * (s % 2)) % 4)
 
     partner = device(x, 1 - yl, z, s)
     sib = device(x, yl, z, s_sib)
@@ -175,10 +181,12 @@
     for to in (partner, sib, crs, crd):
         greet(to)
 
-    @pl.when(x != s)
+    for d in (1, 2, 3):
+        greet(fin_from(d))
+
+    @pl.when(jnp.logical_not(alone))
     def _():
-        for d in range(4):
-            greet(fin(d))
+        greet(fin_from(0))
 
 
     def norm_sums(i, carry):
@@ -210,7 +218,7 @@
     spread = jnp.sum(stat[1], axis=-1, keepdims=True) * (1 / D)
     stat[1] = jnp.broadcast_to(lax.rsqrt(spread + 1e-05), (TOK, 128))
 
-    pl.semaphore_wait(barrier, jnp.where(x != s, 14, 10))
+    pl.semaphore_wait(barrier, jnp.where(alone, 13, 14))
 
     def along_first(d):
         return device(
@@ -259,7 +267,7 @@
     q_probe = float(np.float32(1 / math.sqrt(D)).astype(jnp.bfloat16))
     o_probe = float(np.float32(1 / math.sqrt(INNER)).astype(jnp.bfloat16))
 
-    def project(start, size):
+    def project(start, size, steps=(0, D // STEP)):
         q_rows = lax.broadcasted_iota(jnp.int32, (size, STEP), 1)
         q_cols = lax.broadcasted_iota(jnp.int32, (size, STEP), 0)
         q_base = (q_rows * WIDE + q_cols + (fs * COLS + start)) * jnp.int32(MIX[0]) + seeded
@@ -274,7 +282,7 @@
             acc[1, to] += both[size:]
             return carry
 
-        lax.fori_loop(0, D // STEP, step, 0)
+        lax.fori_loop(*steps, step, 0)
 
     project(HS, 2 * HS)
 
@@ -318,7 +326,28 @@
         return slice(h * SPAN, (h + 1) * SPAN)
 
     tgt_load.wait()
-    project(0, HS)
+    project(0, HS, (0, 4))
+
+    for copy in own_w:
+        copy.wait()
+    arrived([w_one])
+    w_two = group(ww.at[0, pl.ds(0, 3)])
+    for d in (1, 2, 3):
+        remote(wt.at[:, (second + d) % 4], ww.at[c, second], along_second(d), w_two)
+    own_ww = stay(wt.at[:, second], ww.at[c, second])
+
+    b0 = (1 - yh) * 2
+    b1 = b0 + 1
+    arrived([n_far])
+    n_one = group(nb.at[0, pl.ds(0, 96)])
+    for d in (1, 2, 3):
+        at0 = nb.at[b0, rows((z * 4 + x) * 16, 16)]
+        at1 = nb.at[b1, rows((x * 4 + z) * 16, 16)]
+        remote(at0, at0, xp(d), n_one)
+        remote(at1, at1, zp(d), n_one)
+
+    project(0, HS, (4, D // STEP))
+
     q = rotate(acc[0, :HS], own_trig).astype(BF)
     q_tan = rotate(acc[1, :HS], own_trig).astype(BF)
     for h in range(2):
@@ -330,24 +359,6 @@
         qk[h] = jnp.concatenate([one, two], axis=1)
     resid[...] = (tok[:, lanes(own_cols, PART)].astype(F32) - tgt[...].astype(F32)).T
 
-    b0 = (1 - yh) * 2
-    b1 = b0 + 1
-    arrived([n_far])
-    n_one = group(nb.at[0, pl.ds(0, 96)])
-    for d in (1, 2, 3):
-        at0 = nb.at[b0, rows((z * 4 + x) * 16, 16)]
-        at1 = nb.at[b1, rows((x * 4 + z) * 16, 16)]
-        remote(at0, at0, xp(d), n_one)
-        remote(at1, at1, zp(d), n_one)
-
-    for copy in own_w:
-        copy.wait()
-    arrived([w_one])
-    w_two = group(ww.at[0, pl.ds(0, 3)])
-    for d in (1, 2, 3):
-        remote(wt.at[:, (second + d) % 4], ww.at[c, second], along_second(d), w_two)
-    own_ww = stay(wt.at[:, second], ww.at[c, second])
-
     o_rows = lax.broadcasted_iota(jnp.int32, (HALF, PART), 0)
     o_lanes = lax.broadcasted_iota(jnp.int32, (HALF, PART), 1)
     o_base = (o_rows * D + o_lanes + (D * WIDE + own_cols)) * jnp.int32(MIX[0]) + seeded
@@ -386,26 +397,17 @@
 
     arrived([k_crs])
     k_rel = spread_kv(s_crs, k_part, sib)
-    arrived([v_crs])
-    v_rel = spread_kv(s_crs, v_part, sib)
-
-    arrived([k_sib, k_rel])
+
     root = 1 / math.sqrt(HS)
 
     def keys_of(b):
         return lanes(b * TOK, TOK)
 
-    def pulls(left, part, h):
-        def pull(b, carry):
+    def pulls(left, part, h, blocks=range(4)):
+        for b in blocks:
             score[h, :, keys_of(b)] = dot(left[h], gkv[b, part], NN)
-            return carry
-
-        lax.fori_loop(0, 4, pull, 0, unroll=2)
 
     along = lax.broadcasted_iota(jnp.int32, (1, TOK), 1).astype(F32)
-    key_pos = jnp.concatenate(
-        [gkv[b, KEYS - 16 : KEYS].astype(F32)[0:1] * float(TOK) + along for b in range(4)], axis=1
-    )
     number_f = jnp.full((32, 1), number, jnp.int32).astype(F32)
     down = lax.broadcasted_iota(jnp.int32, (32, 1), 0)
 
@@ -447,18 +449,33 @@
             remote(gb.at[h, x, z], gb.at[h, x, z], zp(d), held)
         return held
 
+    def side(t):
+        return pl.ds(t * SPAN, SPAN)
+
     def gather_two(h):
-        held = group(ra1)
-        for d in (1, 2, 3):
-            remote(ga.at[h, z], ga.at[h, z], zp(d), held)
-            remote(gb.at[h, x], gb.at[h, x], xp(d), held)
-        return held
-
-    pulls(qq, pl.ds(0, 2 * HS), 0)
+        groups = []
+        for t in range(2):
+            held = group(ra1.at[:, :, :, :, side(t)])
+            for d in (1, 2, 3):
+                at0, at1 = ga.at[h, z, :, :, side(t)], gb.at[h, x, :, :, side(t)]
+                remote(at0, at0, zp(d), held)
+                remote(at1, at1, xp(d), held)
+            groups.append(held)
+        return groups
+
+    pulls(qq, pl.ds(0, 2 * HS), 0, (s, s_crs))
+    pulls(qq, pl.ds(0, 2 * HS), 1, (s, s_crs))
+    arrived([k_sib, k_rel])
+    key_pos = jnp.concatenate(
+        [gkv[b, KEYS - 16 : KEYS].astype(F32)[0:1] * float(TOK) + along for b in range(4)], axis=1
+    )
+    pulls(qq, pl.ds(0, 2 * HS), 0, (s_sib, s_crd))
+    pulls(qq, pl.ds(0, 2 * HS), 1, (s_sib, s_crd))
+    arrived([v_crs])
+    v_rel = spread_kv(s_crs, v_part, sib)
     soft(0)
     arrived([v_sib, v_rel])
     g_one = [attn_products(0)]
-    pulls(qq, pl.ds(0, 2 * HS), 1)
     own_ww.wait()
     arrived([w_two])
     w_sib = remote(ww.at[c], ww.at[c], sib)
@@ -475,19 +492,6 @@
     arrived([n_one])
     n_two = [spread_normed(pl.ds(0, SHARE // 2))]
 
-    def mix(h):
-        arrived([g_two[h]])
-        total = jnp.zeros((2 * PART, 2 * SPAN), F32)
-        for a, ref in enumerate((ga, gb)):
-            for i in range(4):
-                total = total + dot(wpt[a, i], ref[h, i].reshape(4 * HALF, 2 * SPAN), NN)
-        mix_acc[h, :, 0:SPAN] = total[:PART, :SPAN]
-        mix_acc[h, :, SPAN:] = total[:PART, SPAN:] + total[PART:, :SPAN]
-        mix_out[h] = mix_acc[h].astype(BF)
-        return remote(mix_out.at[h], mix_in.at[h], partner)
-
-    m_both = [mix(0), mix(1)]
-
     s_base = (
         (lax.broadcasted_iota(jnp.int32, (COLS, TOK), 1) + s * SHARE) * WIDE
         + lax.broadcasted_iota(jnp.int32, (COLS, TOK), 0)
@@ -501,25 +505,62 @@
 
     lax.fori_loop(0, SHARE // TOK, sign_cols, 0)
 
-    def back(h):
-        arrived([m_both[h]])
-        grads[h] = mix_acc[h] + mix_in[h].astype(F32)
-        grads[h, :, 0:SPAN] += resid[:, span(h)]
-        grad[h] = (grads[h] * (1 / 1024)).astype(BF)
+    def products(h, t, tall):
+        total = jnp.zeros((tall, SPAN), F32)
+        for a, ref in enumerate((ga, gb)):
+            for i in range(4):
+                right = ref[h, i, :, :, t * SPAN : (t + 1) * SPAN].reshape(4 * HALF, SPAN)
+                total = total + dot(wpt[a, i, 0:tall], right, NN)
+        return total
+
+    def trade(h, t):
+        part = side(t)
+        mix_out[h, :, part] = mix_acc[h, :, part].astype(BF)
+        return remote(mix_out.at[h, :, part], mix_in.at[h, :, part], partner)
+
+    def mix(h, t):
+        arrived([g_two[h][t]])
+        if t == 0:
+            total = products(h, 0, 2 * PART)
+            mix_acc[h, :, side(0)] = total[:PART]
+            mix_acc[h, :, side(1)] = total[PART:]
+        else:
+            mix_acc[h, :, side(1)] += products(h, 1, PART)
+        return trade(h, t)
+
+    m_part = {}
+    m_part[0, 0] = mix(0, 0)
+    m_part[0, 1] = mix(0, 1)
+    m_part[1, 0] = mix(1, 0)
+
+    def back(h, t):
+        arrived([m_part[h, t]])
+        part = side(t)
+        total = mix_acc[h, :, part] + mix_in[h, :, part].astype(F32)
+        if t == 0:
+            total = total + resid[:, span(h)]
+        grad[h, :, part] = (total * (1 / 1024)).astype(BF)
 
         def step(a, carry):
+            right = grad[h, :, part]
             for i in range(4):
-                first = dot(ww[a, i].reshape(4 * HALF, PART), grad[h], NN)
-                second = dot(pp[a, i].reshape(4 * HALF, PART), grad[h, :, 0:SPAN], NN)
-                sab[h, a, i, :, :, 0:SPAN] = first[:, :SPAN].astype(BF).reshape(4, HALF, SPAN)
-                sab[h, a, i, :, :, SPAN:] = (first[:, SPAN:] + second).astype(BF).reshape(4, HALF, SPAN)
+                first = dot(ww[a, i].reshape(4 * HALF, PART), right, NN)
+                if t == 0:
+                    back_acc[h, a, i] = dot(pp[a, i].reshape(4 * HALF, PART), right, NN)
+                else:
+                    first = first + back_acc[h, a, i]
+                sab[h, a, i, :, :, part] = first.astype(BF).reshape(4, HALF, SPAN)
             return carry
 
         lax.fori_loop(0, 2, step, 0)
-        held = group(ra1)
+        held = group(ra1.at[:, :, :, :, part])
         for d in (1, 2, 3):
-            remote(sab.at[h, 0, (z + d) % 4], ra1.at[h, d - 1], zp(d), held)
-            remote(sab.at[h, 1, (x + d) % 4], rb1.at[h, d - 1], xp(d), held)
+            remote(
+                sab.at[h, 0, (z + d) % 4, :, :, part], ra1.at[h, d - 1, :, :, part], zp(d), held
+            )
+            remote(
+                sab.at[h, 1, (x + d) % 4, :, :, part], rb1.at[h, d - 1, :, :, part], xp(d), held
+            )
         return held
 
     def total_of(own, others):
@@ -529,7 +570,7 @@
         return total
 
     def scatter_two(h):
-        arrived([r_one[h]])
+        arrived(r_one[h])
         sa2[h] = total_of(sab[h, 0, z], [ra1[h, k] for k in range(3)]).astype(BF)
         sb2[h] = total_of(sab[h, 1, x], [rb1[h, k] for k in range(3)]).astype(BF)
         held = group(ra2)
@@ -561,24 +602,27 @@
 
         lax.fori_loop(0, 4, term, 0)
 
-    r_one = [back(0)]
+    r_one = [[back(0, 0)], []]
+    m_part[1, 1] = mix(1, 1)
+    r_one[0].append(back(0, 1))
     out_terms(0)
-    r_one.append(back(1))
+    r_one[1].append(back(1, 0))
+    r_one[1].append(back(1, 1))
     out_terms(1)
 
     o_core = group(ha)
     for k in range(2):
         remote(ha.at[:, 2 * k + 1 - c], ca.at[k], sib, o_core)
         remote(hb.at[2 * k + 1 - c], cb.at[k], sib, o_core)
-    r_two = [scatter_two(0)]
-
     arrived([o_core])
-    far = 1 - yh
+    near, far = kept // 2, 1 - kept // 2
     xa[...] = total_of(ha[:, 2 * far + c], [ca[far]]).astype(BF)
     xb[...] = total_of(hb[2 * far + c], [cb[far]]).astype(BF)
     o_crs = group(ca)
     remote(xa, ya, crs, o_crs)
     remote(xb, yb, crs, o_crs)
+
+    r_two = [scatter_two(0)]
 
     cv_acc[...] = jnp.zeros_like(cv_acc)
     ck_acc[...] = jnp.zeros_like(ck_acc)
@@ -629,9 +673,9 @@
         for k in range(2):
             kept[k] = total_of(own[2 * k + c], [other[k]]).astype(BF)
 
+    r_two.append(scatter_two(1))
     g_first = scattered(0)
     value_terms(0, g_first)
-    r_two.append(scatter_two(1))
     slopes(0, g_first)
     key_terms(0)
     query_terms(0)
@@ -643,9 +687,28 @@
     v_core = group(cvr)
     for k in range(2):
         remote(cv.at[2 * k + 1 - c], cvr.at[k], sib, v_core)
+    slopes(1, g_second)
+    arrived([v_core])
+    chip_sums(cv, cvr, cvs)
+    v_far = remote(cvs, cvf, crs)
+    key_terms(1)
+    ck[...] = (ck_acc[...] * root).astype(BF)
+
+    k_core = group(ckr)
+    for k in range(2):
+        remote(ck.at[2 * k + 1 - c], ckr.at[k], sib, k_core)
+    query_terms(1)
+    q_part, k_rows, head_part = pl.ds(0, HS), pl.ds(HS, HS), pl.ds(0, 2 * HS)
+    tail_part = pl.ds(2 * HS, HS)
+    cot[s, q_part] = rotate((cq_acc[...] * root).astype(BF).astype(F32), own_trig, -1.0).astype(BF)
+    arrived([k_core])
+    chip_sums(ck, ckr, cks)
+    k_far = remote(cks, ckf, crs)
+    q_far = remote(cot.at[s, q_part], cot.at[s, q_part], crs)
+
     arrived([o_crs])
-    fa[...] = total_of(ha[:, s], [ca[yh], ya[...]]).astype(BF)
-    fb[...] = total_of(hb[s], [cb[yh], yb[...]]).astype(BF)
+    fa[...] = total_of(ha[:, kept], [ca[near], ya[...]]).astype(BF)
+    fb[...] = total_of(hb[kept], [cb[near], yb[...]]).astype(BF)
     o_fin = group(ca.at[0, pl.ds(0, 3)])
     o_fin_b = group(ca.at[0, pl.ds(0, 3)])
     for d in (1, 2, 3):
@@ -660,34 +723,15 @@
     ]
     o_near = [nearby(fa.at[z], oa.at[z]), nearby(fb.at[z], ob.at[z])]
 
-    @pl.when(x != s)
+    @pl.when(jnp.logical_not(alone))
     def _():
         for copy in o_far:
             copy.start()
 
-    @pl.when(x == s)
+    @pl.when(alone)
     def _():
         for copy in o_near:
             copy.start()
-
-    slopes(1, g_second)
-    arrived([v_core])
-    chip_sums(cv, cvr, cvs)
-    v_far = remote(cvs, cvf, crs)
-    key_terms(1)
-    ck[...] = (ck_acc[...] * root).astype(BF)
-
-    k_core = group(ckr)
-    for k in range(2):
-        remote(ck.at[2 * k + 1 - c], ckr.at[k], sib, k_core)
-    query_terms(1)
-    q_part, k_rows, head_part = pl.ds(0, HS), pl.ds(HS, HS), pl.ds(0, 2 * HS)
-    tail_part = pl.ds(2 * HS, HS)
-    cot[s, q_part] = rotate((cq_acc[...] * root).astype(BF).astype(F32), own_trig, -1.0).astype(BF)
-    arrived([k_core])
-    chip_sums(ck, ckr, cks)
-    k_far = remote(cks, ckf, crs)
-    q_far = remote(cot.at[s, q_part], cot.at[s, q_part], crs)
 
     arrived([v_far])
     for k in range(2):
@@ -739,13 +783,13 @@
 
     arrived([o_fin, o_fin_b])
 
-    @pl.when(x != s)
+    @pl.when(jnp.logical_not(alone))
     def _():
         for copy in o_far:
             copy.wait_recv()
             copy.wait_send()
 
-    @pl.when(x == s)
+    @pl.when(alone)
     def _():
         for copy in o_near:
             copy.wait()
@@ -820,7 +864,7 @@
         v((2, 2 * SPAN, 1024), BF), v((2, 2 * SPAN, 1024), BF),
         v((4, HS, TOK), F32), v((4, HS, TOK), F32), v((HS, TOK), F32),
         v((2, PART, 2 * SPAN), F32), v((2, PART, 2 * SPAN), BF), v((2, PART, 2 * SPAN), BF),
-        v((2, PART, 2 * SPAN), F32), v((2, PART, 2 * SPAN), BF), v((4 * SPAN, PART), BF), v((PART, TOK), F32),
+        v((2, 2, 4, 4 * HALF, SPAN), F32), v((2, PART, 2 * SPAN), BF), v((4 * SPAN, PART), BF), v((PART, TOK), F32),
         v((2, 2, 4, 4, HALF, 2 * SPAN), BF),
         v((2, 3, 4, HALF, 2 * SPAN), BF), v((2, 3, 4, HALF, 2 * SPAN), BF),
         v((2, 4, HALF, 2 * SPAN), BF), v((2, 4, HALF, 2 * SPAN), BF),

time: 82 us -> 76 us (0.927)
  the two profiles are of different devices: /device:TPU:25 before, /device:TPU:1 now
where the time goes in v7:
time: 76 us; the launch traced here: 75.8 us
  Pallas kernels  73.9 us (97%)
  between operations  1.93 us (3%)
    pallas_call x1, Pallas kernels, per_device(): pl.pallas_call(kernel, out_shape=(jax.ShapeDtypeStruct((COLS, SHARE), BF)...  71.4 us
    pallas_call x1, Pallas kernels, per_device(): pl.pallas_call(widen, out_shape=(jax.ShapeDtypeStruct((COLS, SHARE), F32)...  2.47 us

profile of v7, /device:TPU:1, one launch (start us, length us, event | category | flops | bytes accessed | tf_op | source)
XLA Modules:
  0.0 75.8 jit_solution(9681007050351451858)
XLA Ops:
  1.9 71.4 %shard_map.104 = (bf16[288,1536]{1,0:T(8,128)(2,1)}, bf16[96,1536]{1,0:T(8,128)(2,1)}) custom-call(bf16[256,6144]{1,0:T(8,128)(2,1)} %tok_in.1, bf16[256,6144]{1,0:T(8,128)(2,1)} %tgt_in.1, f32[1,6144]{1,0:T(1,128)} %bitcast.4, bf16[288,6144]{1,0:T(8,128)(2,1)} %bitcast.3, bf16[96,6144]{1,0:T(8,128)(2,1)} %wo_in.1, s32[1]{0:T(128)S(6)} %copy.11.seed_in, ...), custom_call_target="tpu_custom_call" | custom-call | tf_op jit(solution)/shard_map/pallas_call | solution.py:882
  73.3 2.5 %shard_map.105 = (f32[288,1536]{1,0:T(8,128)}, f32[96,1536]{1,0:T(8,128)}) custom-call(bf16[288,1536]{1,0:T(8,128)(2,1)} %get-tuple-element.6.product_in, bf16[96,1536]{1,0:T(8,128)(2,1)} %get-tuple-element.7.out_in), custom_call_target="tpu_custom_call" | custom-call | tf_op jit(solution)/shard_map/pallas_call | solution.py:898

commit v8 on v7

--- a/solution.py
+++ b/solution.py
@@ -26,7 +26,7 @@
 KEYS = 2 * HS + 16
 STEP = 768
 MIX = (-1640531535, -2048144789, -1028477387)
-N_REMOTE = 48
+N_REMOTE = 52
 N_LOCAL = 25
 
 
@@ -70,10 +70,10 @@
     tok_in, tgt_in, gain_in, wq_in, wo_in, seed_in, block_in, tab_t_in, tab_b_in,
     oq_out, oo_out,
     seed, block, oq, oo, gain, tab_t, tab_b, tok, tgt, wq, nrm, acc,
-    stat, nb, gkv,
+    stat, few, nb, gkv,
     wt, ww, pp, wpt, ga, gb,
-    qq, qk, gg, score, prob, prob_tan, rnd, slope, cv_acc, ck_acc, cq_acc,
-    mix_acc, mix_out, mix_in, back_acc, grad, turn, resid,
+    qq, qk, gg, score, prob, prob_tan, rnd, slope, cv_acc, ck_acc,
+    mix_acc, mix_out, mix_in, back_acc, grad, resid,
     sab, ra1, rb1, sa2, sb2, ra2, rb2,
     ha, hb, ca, cb, xa, xb, ya, yb, fa, fb, oa, ob,
     cv, cvr, cvs, cvf, ck, ckr, cks, ckf, cot, sgn, acc_q, out_acc,
@@ -241,24 +241,29 @@
     for copy in tab_loads:
         copy.wait()
 
-    def norm_rows(i, carry):
-        at = rows(i * 16, 16)
+    def norm_into(to, start, at):
         middle, factor = stat[0, at, :], stat[1, at, :]
         for k in range(D // 128):
             cols = slice(k * 128, (k + 1) * 128)
-            nrm[at, cols] = ((tok[at, cols].astype(F32) - middle) * factor * gain[:, cols]).astype(BF)
+            to[start, cols] = ((tok[at, cols].astype(F32) - middle) * factor * gain[:, cols]).astype(BF)
+
+    def norm_rows(i, carry):
+        norm_into(nrm, rows(i * 16, 16), rows(i * 16, 16))
         return carry
 
-    lax.fori_loop(0, TOK // 16, norm_rows, 0)
-
     piece = jnp.where(c == 0, z * 4 + x, x * 4 + z) * 16
+    norm_into(few, slice(0, 16), rows(piece, 16))
     n_far = group(nb.at[0, pl.ds(0, 32)])
     remote(
-        nrm.at[rows(piece, 16), lanes(s_crs * SHARE, SHARE)], nb.at[s, rows(piece, 16)], crs, n_far
+        few.at[:, lanes(s_crs * SHARE, SHARE)], nb.at[s, rows(piece, 16)], crs, n_far
     )
     remote(
-        nrm.at[rows(piece, 16), lanes(s_crd * SHARE, SHARE)], nb.at[s, rows(piece, 16)], crd, n_far
+        few.at[:, lanes(s_crd * SHARE, SHARE)], nb.at[s, rows(piece, 16)], crd, n_far
     )
+
+
+    lax.fori_loop(0, TOK // 16, norm_rows, 0)
+
     n_sib = remote(nrm.at[:, lanes(s_sib * SHARE, SHARE)], nb.at[s], sib)
 
     wq_load.wait()
@@ -301,8 +306,8 @@
 
     own_trig = trig(jnp.full((ROT, TOK), number, jnp.int32))
 
-    def rotate(field, turns, sign=1.0):
-        cos, sin = turns
+    def rotate(field, turns, sign=1.0, cols=slice(0, TOK)):
+        cos, sin = turns[0][:, cols], turns[1][:, cols]
         head = field[:ROT]
         swapped = pltpu.roll(head, ROT // 2, 0)
         return jnp.concatenate([head * cos + swapped * (sin * sign), field[ROT:]], axis=0)
@@ -321,20 +326,6 @@
         gkv[s, KEYS + k * HS : KEYS + (k + 1) * HS] = acc[k, 2 * HS : 3 * HS].astype(BF)
     v_crs = spread_kv(s, v_part, crs)
     v_sib = spread_kv(s, v_part, sib)
-
-    def span(h):
-        return slice(h * SPAN, (h + 1) * SPAN)
-
-    tgt_load.wait()
-    project(0, HS, (0, 4))
-
-    for copy in own_w:
-        copy.wait()
-    arrived([w_one])
-    w_two = group(ww.at[0, pl.ds(0, 3)])
-    for d in (1, 2, 3):
-        remote(wt.at[:, (second + d) % 4], ww.at[c, second], along_second(d), w_two)
-    own_ww = stay(wt.at[:, second], ww.at[c, second])
 
     b0 = (1 - yh) * 2
     b1 = b0 + 1
@@ -345,6 +336,20 @@
         at1 = nb.at[b1, rows((x * 4 + z) * 16, 16)]
         remote(at0, at0, xp(d), n_one)
         remote(at1, at1, zp(d), n_one)
+
+    def span(h):
+        return slice(h * SPAN, (h + 1) * SPAN)
+
+    tgt_load.wait()
+    project(0, HS, (0, 4))
+
+    for copy in own_w:
+        copy.wait()
+    arrived([w_one])
+    w_two = group(ww.at[0, pl.ds(0, 3)])
+    for d in (1, 2, 3):
+        remote(wt.at[:, (second + d) % 4], ww.at[c, second], along_second(d), w_two)
+    own_ww = stay(wt.at[:, second], ww.at[c, second])
 
     project(0, HS, (4, D // STEP))
 
@@ -378,11 +383,11 @@
     def turned(source, start):
         def turn(i, carry):
             for a in range(2):
-                value = source[a, i].reshape(4 * HALF, PART).astype(F32)
-                wpt[a, i, start : start + PART] = value.T.astype(BF)
+                value = source[a, pl.ds(2 * i, 2)].reshape(8 * HALF, PART).astype(F32)
+                wpt[a, start : start + PART, lanes(i * 8 * HALF, 8 * HALF)] = value.T.astype(BF)
             return carry
 
-        lax.fori_loop(0, 4, turn, 0)
+        lax.fori_loop(0, 2, turn, 0)
 
     turned(pp, PART)
 
@@ -506,12 +511,10 @@
     lax.fori_loop(0, SHARE // TOK, sign_cols, 0)
 
     def products(h, t, tall):
-        total = jnp.zeros((tall, SPAN), F32)
-        for a, ref in enumerate((ga, gb)):
-            for i in range(4):
-                right = ref[h, i, :, :, t * SPAN : (t + 1) * SPAN].reshape(4 * HALF, SPAN)
-                total = total + dot(wpt[a, i, 0:tall], right, NN)
-        return total
+        right = [
+            ref[h, :, :, :, t * SPAN : (t + 1) * SPAN].reshape(16 * HALF, SPAN) for ref in (ga, gb)
+        ]
+        return dot(wpt[0, 0:tall], right[0], NN) + dot(wpt[1, 0:tall], right[1], NN)
 
     def trade(h, t):
         part = side(t)
@@ -541,18 +544,12 @@
             total = total + resid[:, span(h)]
         grad[h, :, part] = (total * (1 / 1024)).astype(BF)
 
-        def step(a, carry):
-            right = grad[h, :, part]
-            for i in range(4):
-                first = dot(ww[a, i].reshape(4 * HALF, PART), right, NN)
-                if t == 0:
-                    back_acc[h, a, i] = dot(pp[a, i].reshape(4 * HALF, PART), right, NN)
-                else:
-                    first = first + back_acc[h, a, i]
-                sab[h, a, i, :, :, part] = first.astype(BF).reshape(4, HALF, SPAN)
-            return carry
-
-        lax.fori_loop(0, 2, step, 0)
+        right = grad[h, :, part]
+        for a in range(2):
+            first = dot(ww[a].reshape(16 * HALF, PART), right, NN)
+            if t == 1:
+                first = first + back_acc[h, a]
+            sab[h, a, :, :, :, part] = first.astype(BF).reshape(4, 4, HALF, SPAN)
         held = group(ra1.at[:, :, :, :, part])
         for d in (1, 2, 3):
             remote(
@@ -561,6 +558,9 @@
             remote(
                 sab.at[h, 1, (x + d) % 4, :, :, part], rb1.at[h, d - 1, :, :, part], xp(d), held
             )
+        if t == 0:
+            for a in range(2):
+                back_acc[h, a] = dot(pp[a].reshape(16 * HALF, PART), right, NN)
         return held
 
     def total_of(own, others):
@@ -585,44 +585,44 @@
         second = total_of(sb2[h, z], [rb2[h, k] for k in range(3)])
         return jnp.concatenate([first.astype(BF), second.astype(BF)], axis=0)
 
-    def out_terms(h):
-        for k in range(2):
-            at = slice((2 * h + k) * SPAN, (2 * h + k + 1) * SPAN)
-            turn[at] = grad[h, :, (1 - k) * SPAN : (2 - k) * SPAN].astype(F32).T.astype(BF)
-
-        def term(i, carry):
-            right = turn[2 * h * SPAN : 2 * (h + 1) * SPAN]
-            for a, (ref, to) in enumerate(((ga, ha), (gb, hb))):
-                total = dot(ref[h, i].reshape(4 * HALF, 2 * SPAN), right, NN)
-                if h == 0:
-                    out_acc[a, i] = total
-                else:
-                    to[i] = (out_acc[a, i] + total).astype(BF).reshape(4, HALF, PART)
-            return carry
-
-        lax.fori_loop(0, 4, term, 0)
-
+    def out_terms(h, t):
+        right = grad[h, :, side(t)].astype(F32).T.astype(BF)
+        for a, (ref, to) in enumerate(((ga, ha), (gb, hb))):
+            left = ref[h, :, :, :, (1 - t) * SPAN : (2 - t) * SPAN].reshape(16 * HALF, SPAN)
+            total = dot(left, right, NN)
+            if (h, t) == (0, 0):
+                out_acc[a] = total
+            elif (h, t) == (1, 1):
+                to[...] = (out_acc[a] + total).astype(BF).reshape(4, 4, HALF, PART)
+                half, come = ((ha, ca), (hb, cb))[a]
+                held = group(come)
+                for k in range(2):
+                    from_one = half.at[:, 2 * k + 1 - c] if a == 0 else half.at[2 * k + 1 - c]
+                    remote(from_one, come.at[k], sib, held)
+                o_core.append(held)
+            else:
+                out_acc[a] += total
+
+    o_core = []
     r_one = [[back(0, 0)], []]
     m_part[1, 1] = mix(1, 1)
     r_one[0].append(back(0, 1))
-    out_terms(0)
+    out_terms(0, 0)
+    out_terms(0, 1)
     r_one[1].append(back(1, 0))
+    out_terms(1, 0)
     r_one[1].append(back(1, 1))
-    out_terms(1)
-
-    o_core = group(ha)
-    for k in range(2):
-        remote(ha.at[:, 2 * k + 1 - c], ca.at[k], sib, o_core)
-        remote(hb.at[2 * k + 1 - c], cb.at[k], sib, o_core)
-    arrived([o_core])
+    out_terms(1, 1)
+
+    r_two = [scatter_two(0)]
+
     near, far = kept // 2, 1 - kept // 2
+    arrived([o_core[0]])
     xa[...] = total_of(ha[:, 2 * far + c], [ca[far]]).astype(BF)
+    o_crs = [remote(xa, ya, crs)]
+    arrived([o_core[1]])
     xb[...] = total_of(hb[2 * far + c], [cb[far]]).astype(BF)
-    o_crs = group(ca)
-    remote(xa, ya, crs, o_crs)
-    remote(xb, yb, crs, o_crs)
-
-    r_two = [scatter_two(0)]
+    o_crs.append(remote(xb, yb, crs))
 
     cv_acc[...] = jnp.zeros_like(cv_acc)
     ck_acc[...] = jnp.zeros_like(ck_acc)
@@ -667,7 +667,13 @@
 
     def query_terms(h):
         terms = joint(pl.ds(0, 2 * HS), slope, h)
-        cq_acc[:, span(h)] = terms[:HS, :SPAN] + terms[HS:, SPAN:]
+        total = (terms[:HS, :SPAN] + terms[HS:, SPAN:]) * root
+        turned_back = rotate(total.astype(BF).astype(F32), own_trig, -1.0, span(h))
+        cot[s, 0:HS, span(h)] = turned_back.astype(BF)
+
+    def send_query(h, within):
+        at = cot.at[s, pl.ds(0, HS), pl.ds(h * SPAN, SPAN)]
+        return remote(at, at, crs, within)
 
     def chip_sums(own, other, kept):
         for k in range(2):
@@ -679,6 +685,31 @@
     slopes(0, g_first)
     key_terms(0)
     query_terms(0)
+    q_far = group(cot.at[0, pl.ds(0, HS)])
+    send_query(0, q_far)
+
+    def hand_out(k, source, to):
+        held = group(ca.at[0, pl.ds(0, 3)])
+        for d in (1, 2, 3):
+            remote(source.at[(z + d) % 4], to.at[z], fin(d), held)
+        lone = Group(source.at[z], send.at[count[0]], recv.at[count[0]])
+        count[0] += 1
+        there = remote(source.at[z], to.at[z], fin(0), lone, begin=False)
+        here = nearby(source.at[z], to.at[z])
+
+        @pl.when(jnp.logical_not(alone))
+        def _():
+            there.start()
+
+        @pl.when(alone)
+        def _():
+            here.start()
+
+        return held, there, here
+
+    arrived([o_crs[0]])
+    fa[...] = total_of(ha[:, kept], [ca[near], ya[...]]).astype(BF)
+    o_fin = [hand_out(0, fa, oa)]
 
     g_second = scattered(1)
     n_two.append(spread_normed(pl.ds(SHARE // 2, SHARE // 2)))
@@ -688,6 +719,7 @@
     for k in range(2):
         remote(cv.at[2 * k + 1 - c], cvr.at[k], sib, v_core)
     slopes(1, g_second)
+
     arrived([v_core])
     chip_sums(cv, cvr, cvs)
     v_far = remote(cvs, cvf, crs)
@@ -698,40 +730,46 @@
     for k in range(2):
         remote(ck.at[2 * k + 1 - c], ckr.at[k], sib, k_core)
     query_terms(1)
-    q_part, k_rows, head_part = pl.ds(0, HS), pl.ds(HS, HS), pl.ds(0, 2 * HS)
+    k_rows, head_part = pl.ds(HS, HS), pl.ds(0, 2 * HS)
     tail_part = pl.ds(2 * HS, HS)
-    cot[s, q_part] = rotate((cq_acc[...] * root).astype(BF).astype(F32), own_trig, -1.0).astype(BF)
     arrived([k_core])
     chip_sums(ck, ckr, cks)
     k_far = remote(cks, ckf, crs)
-    q_far = remote(cot.at[s, q_part], cot.at[s, q_part], crs)
-
-    arrived([o_crs])
-    fa[...] = total_of(ha[:, kept], [ca[near], ya[...]]).astype(BF)
+    send_query(1, q_far)
+
+    arrived([o_crs[1]])
     fb[...] = total_of(hb[kept], [cb[near], yb[...]]).astype(BF)
-    o_fin = group(ca.at[0, pl.ds(0, 3)])
-    o_fin_b = group(ca.at[0, pl.ds(0, 3)])
-    for d in (1, 2, 3):
-        other = (z + d) % 4
-        remote(fa.at[other], oa.at[z], fin(d), o_fin)
-        remote(fb.at[other], ob.at[z], fin(d), o_fin_b)
-    lone = [Group(fa.at[z], send.at[count[0] + k], recv.at[count[0] + k]) for k in range(2)]
-    count[0] += 2
-    o_far = [
-        remote(fa.at[z], oa.at[z], fin(0), lone[0], begin=False),
-        remote(fb.at[z], ob.at[z], fin(0), lone[1], begin=False),
-    ]
-    o_near = [nearby(fa.at[z], oa.at[z]), nearby(fb.at[z], ob.at[z])]
-
-    @pl.when(jnp.logical_not(alone))
-    def _():
-        for copy in o_far:
-            copy.start()
-
-    @pl.when(alone)
-    def _():
-        for copy in o_near:
-            copy.start()
+    o_fin.append(hand_out(1, fb, ob))
+
+
+    e_base = (
+        lax.broadcasted_iota(jnp.int32, (HALF, PART), 0) * D
+        + lax.broadcasted_iota(jnp.int32, (HALF, PART), 1)
+        + (D * WIDE + fs * HS * D + s * SHARE)
+    ) * jnp.int32(MIX[0]) + seeded
+    scale = math.sqrt(INNER)
+    leaving = []
+
+    def result(half):
+        held, there, here = o_fin[half]
+        arrived([held])
+
+        @pl.when(jnp.logical_not(alone))
+        def _():
+            there.wait_recv()
+            there.wait_send()
+
+        @pl.when(alone)
+        def _():
+            here.wait()
+
+        at = pl.ds(half * HALF, HALF)
+        for k in range(4):
+            bit = sign_bit(e_base + jnp.int32(wrap((half * HALF * D + k * PART) * MIX[0])))
+            signed = (oa, ob)[half][k].astype(F32) * jnp.where(bit == 0, F32(scale), F32(-scale))
+            oo[at, k * PART : (k + 1) * PART] = signed.astype(BF)
+        leaving.append(stay(oo.at[at], oo_out.at[at]))
+
 
     arrived([v_far])
     for k in range(2):
@@ -769,7 +807,7 @@
     first_terms(tail_part)
     arrived([t_tail])
     last_terms(tail_part, 0, 6)
-    leaving = [stay(oq.at[tail_part], oq_out.at[tail_part])]
+    leaving.append(stay(oq.at[tail_part], oq_out.at[tail_part]))
 
     arrived([k_far])
     for k in range(2):
@@ -781,39 +819,14 @@
         remote(cot.at[2 * k + c, head_part], cot.at[2 * k + c, head_part], sib, t_head)
     first_terms(head_part)
 
-    arrived([o_fin, o_fin_b])
-
-    @pl.when(jnp.logical_not(alone))
-    def _():
-        for copy in o_far:
-            copy.wait_recv()
-            copy.wait_send()
-
-    @pl.when(alone)
-    def _():
-        for copy in o_near:
-            copy.wait()
-
-    e_base = (
-        lax.broadcasted_iota(jnp.int32, (HALF, PART), 0) * D
-        + lax.broadcasted_iota(jnp.int32, (HALF, PART), 1)
-        + (D * WIDE + fs * HS * D + s * SHARE)
-    ) * jnp.int32(MIX[0]) + seeded
-    scale = math.sqrt(INNER)
-    for half, ref in enumerate((oa, ob)):
-        for k in range(4):
-            bit = sign_bit(e_base + jnp.int32(wrap((half * HALF * D + k * PART) * MIX[0])))
-            oo[half * HALF : (half + 1) * HALF, k * PART : (k + 1) * PART] = (
-                ref[k].astype(F32) * jnp.where(bit == 0, F32(scale), F32(-scale))
-            ).astype(BF)
-
-
-    leaving.append(stay(oo, oo_out))
+    result(0)
+
     arrived([t_head])
     for k in range(2):
         last_terms(head_part, k * 3, k * 3 + 3)
         cols = pl.ds(k * SHARE // 2, SHARE // 2)
         leaving.append(stay(oq.at[head_part, cols], oq_out.at[head_part, cols]))
+    result(1)
     for copy in leaving:
         copy.wait()
 
@@ -822,8 +835,8 @@
 
 
 def widen(product_in, out_in, product, out, narrow, narrow_out, wide, wide_out, loads, stores):
-    thirds = [pl.ds(k * SHARE // 3, SHARE // 3) for k in range(3)]
-    parts = [(product_in.at[:, at], narrow.at[k], wide.at[k], product.at[:, at]) for k, at in enumerate(thirds)]
+    pieces = [pl.ds(k * SHARE // 6, SHARE // 6) for k in range(6)]
+    parts = [(product_in.at[:, at], narrow.at[k], wide.at[k], product.at[:, at]) for k, at in enumerate(pieces)]
     parts.append((out_in, narrow_out, wide_out, out))
     arrive = [pltpu.make_async_copy(part[0], part[1], loads.at[k]) for k, part in enumerate(parts)]
     leave = [pltpu.make_async_copy(part[2], part[3], stores.at[k]) for k, part in enumerate(parts)]
@@ -855,16 +868,16 @@
         pltpu.SMEM((1,), jnp.int32), pltpu.SMEM((1,), jnp.int32),
         v((COLS, SHARE), BF), v((HS, SHARE), BF), v((1, D), F32), v((2, ROT, TOK), F32), v((4, 2, ROT, TOK), F32),
         v((TOK, D), BF), v((TOK, PART), BF), v((COLS, D), BF), v((TOK, D), BF), v((2, COLS, TOK), F32),
-        v((2, TOK, 128), F32), v((4, TOK, SHARE), BF), v((4, 4 * HS + 16, TOK), BF),
+        v((2, TOK, 128), F32), v((16, D), BF), v((4, TOK, SHARE), BF), v((4, 4 * HS + 16, TOK), BF),
         v((4, 4, HALF, PART), BF), v((2, 4, 4, HALF, PART), BF), v((2, 4, 4, HALF, PART), BF),
-        v((2, 4, 2 * PART, 4 * HALF), BF),
+        v((2, 2 * PART, 16 * HALF), BF),
         v((2, 4, 4, HALF, 2 * SPAN), BF), v((2, 4, 4, HALF, 2 * SPAN), BF),
         v((2, 2 * SPAN, 2 * HS), BF), v((2, HS, 2 * SPAN), BF), v((2, 2 * SPAN, 2 * HS), BF),
         v((2, 2 * SPAN, 1024), F32), v((TOK, 1024), F32), v((TOK, 1024), F32),
         v((2, 2 * SPAN, 1024), BF), v((2, 2 * SPAN, 1024), BF),
-        v((4, HS, TOK), F32), v((4, HS, TOK), F32), v((HS, TOK), F32),
+        v((4, HS, TOK), F32), v((4, HS, TOK), F32),
         v((2, PART, 2 * SPAN), F32), v((2, PART, 2 * SPAN), BF), v((2, PART, 2 * SPAN), BF),
-        v((2, 2, 4, 4 * HALF, SPAN), F32), v((2, PART, 2 * SPAN), BF), v((4 * SPAN, PART), BF), v((PART, TOK), F32),
+        v((2, 2, 16 * HALF, SPAN), F32), v((2, PART, 2 * SPAN), BF), v((PART, TOK), F32),
         v((2, 2, 4, 4, HALF, 2 * SPAN), BF),
         v((2, 3, 4, HALF, 2 * SPAN), BF), v((2, 3, 4, HALF, 2 * SPAN), BF),
         v((2, 4, HALF, 2 * SPAN), BF), v((2, 4, HALF, 2 * SPAN), BF),
@@ -875,7 +888,7 @@
         v((4, HALF, PART), BF), v((4, HALF, PART), BF), v((4, HALF, PART), BF), v((4, HALF, PART), BF),
         v((4, HS, TOK), BF), v((2, HS, TOK), BF), v((2, HS, TOK), BF), v((2, HS, TOK), BF),
         v((4, HS, TOK), BF), v((2, HS, TOK), BF), v((2, HS, TOK), BF), v((2, HS, TOK), BF),
-        v((4, 3 * HS, TOK), BF), v((COLS, SHARE), F32), v((COLS, SHARE), F32), v((2, 4, 4 * HALF, PART), F32),
+        v((4, 3 * HS, TOK), BF), v((COLS, SHARE), F32), v((COLS, SHARE), F32), v((2, 16 * HALF, PART), F32),
         pltpu.SemaphoreType.DMA((N_REMOTE,)), pltpu.SemaphoreType.DMA((N_REMOTE,)),
         pltpu.SemaphoreType.DMA((N_LOCAL,)),
     ]
@@ -904,9 +917,9 @@
         in_specs=[anywhere, anywhere],
         out_specs=(anywhere, anywhere),
         scratch_shapes=[
-            v((3, COLS, SHARE // 3), BF), v((HS, SHARE), BF),
-            v((3, COLS, SHARE // 3), F32), v((HS, SHARE), F32),
-            pltpu.SemaphoreType.DMA((4,)), pltpu.SemaphoreType.DMA((4,)),
+            v((6, COLS, SHARE // 6), BF), v((HS, SHARE), BF),
+            v((6, COLS, SHARE // 6), F32), v((HS, SHARE), F32),
+            pltpu.SemaphoreType.DMA((7,)), pltpu.SemaphoreType.DMA((7,)),
         ],
     )(product, out_curv)
     return product.T, out_curv

time: 76 us -> 74.7 us (0.983)
  Pallas kernels: 73.9 us -> 72.4 us
    pallas_call x1, Pallas kernels: 71.4 us -> 70 us  [per_device(): pl.pallas_call(kernel, out_shape=(jax.ShapeDtypeStruct((COLS, SHARE), BF)...]
where the time goes in v8:
time: 74.7 us; the launch traced here: 74.5 us
  Pallas kernels  72.4 us (97%)
  between operations  2.09 us (3%)
    pallas_call x1, Pallas kernels, per_device(): pl.pallas_call(kernel, out_shape=(jax.ShapeDtypeStruct((COLS, SHARE), BF)...  70 us
    pallas_call x1, Pallas kernels, per_device(): pl.pallas_call(widen, out_shape=(jax.ShapeDtypeStruct((COLS, SHARE), F32)...  2.45 us

profile of v8, /device:TPU:1, one launch (start us, length us, event | category | flops | bytes accessed | tf_op | source)
XLA Modules:
  0.0 74.5 jit_solution(11260734226460346639)
XLA Ops:
  1.9 70.0 %shard_map.104 = (bf16[288,1536]{1,0:T(8,128)(2,1)}, bf16[96,1536]{1,0:T(8,128)(2,1)}) custom-call(bf16[256,6144]{1,0:T(8,128)(2,1)} %tok_in.1, bf16[256,6144]{1,0:T(8,128)(2,1)} %tgt_in.1, f32[1,6144]{1,0:T(1,128)} %bitcast.4, bf16[288,6144]{1,0:T(8,128)(2,1)} %bitcast.3, bf16[96,6144]{1,0:T(8,128)(2,1)} %wo_in.1, s32[1]{0:T(128)S(6)} %copy.11.seed_in, ...), custom_call_target="tpu_custom_call" | custom-call | tf_op jit(solution)/shard_map/pallas_call | solution.py:895
  71.9 2.5 %shard_map.105 = (f32[288,1536]{1,0:T(8,128)}, f32[96,1536]{1,0:T(8,128)}) custom-call(bf16[288,1536]{1,0:T(8,128)(2,1)} %get-tuple-element.6.product_in, bf16[96,1536]{1,0:T(8,128)(2,1)} %get-tuple-element.7.out_in), custom_call_target="tpu_custom_call" | custom-call | tf_op jit(solution)/shard_map/pallas_call | solution.py:911

commit v9 on v8

--- a/solution.py
+++ b/solution.py
@@ -191,32 +191,27 @@
 
     def norm_sums(i, carry):
         at = rows(i * 16, 16)
-        totals = [jnp.zeros((16, 128), F32) for _ in range(2)]
+        middle = stat[0, at, :]
+        totals = [jnp.zeros((16, 128), F32) for _ in range(4)]
         for k in range(D // 128):
-            totals[k % 2] += tok[at, k * 128 : (k + 1) * 128].astype(F32)
-        stat[0, at, :] = totals[0] + totals[1]
+            moved = tok[at, k * 128 : (k + 1) * 128].astype(F32) - middle
+            totals[k % 2] += moved
+            totals[2 + k % 2] += moved * moved
+        stat[1, at, :] = totals[0] + totals[1]
+        stat[2, at, :] = totals[2] + totals[3]
         return carry
 
     for k in range(4):
         tok_loads[k].wait()
+        at = pl.ds(k * 64, 64)
+        pivot = jnp.mean(tok[at, 0:128].astype(F32), axis=-1, keepdims=True)
+        stat[0, at] = jnp.broadcast_to(pivot, (64, 128))
         lax.fori_loop(k * 4, (k + 1) * 4, norm_sums, 0, unroll=2)
     wq_load = stay(wq_in, wq)
-    average = jnp.sum(stat[0], axis=-1, keepdims=True) * (1 / D)
-    stat[0] = jnp.broadcast_to(average, (TOK, 128))
-
-    def norm_squares(i, carry):
-        at = rows(i * 16, 16)
-        middle = stat[0, at, :]
-        totals = [jnp.zeros((16, 128), F32) for _ in range(2)]
-        for k in range(D // 128):
-            centred = tok[at, k * 128 : (k + 1) * 128].astype(F32) - middle
-            totals[k % 2] += centred * centred
-        stat[1, at, :] = totals[0] + totals[1]
-        return carry
-
-    lax.fori_loop(0, TOK // 16, norm_squares, 0, unroll=2)
-    spread = jnp.sum(stat[1], axis=-1, keepdims=True) * (1 / D)
-    stat[1] = jnp.broadcast_to(lax.rsqrt(spread + 1e-05), (TOK, 128))
+    drift = jnp.sum(stat[1], axis=-1, keepdims=True) * (1 / D)
+    spread = jnp.sum(stat[2], axis=-1, keepdims=True) * (1 / D) - drift * drift
+    stat[0] += jnp.broadcast_to(drift, (TOK, 128))
+    stat[1] = jnp.broadcast_to(lax.rsqrt(jnp.maximum(spread, 0.0) + 1e-05), (TOK, 128))
 
     pl.semaphore_wait(barrier, jnp.where(alone, 13, 14))
 
@@ -476,6 +471,8 @@
     )
     pulls(qq, pl.ds(0, 2 * HS), 0, (s_sib, s_crd))
     pulls(qq, pl.ds(0, 2 * HS), 1, (s_sib, s_crd))
+    arrived([n_one])
+    n_two = [spread_normed(pl.ds(0, SHARE // 4))]
     arrived([v_crs])
     v_rel = spread_kv(s_crs, v_part, sib)
     soft(0)
@@ -494,8 +491,7 @@
     turned(ww, 0)
     arrived([g_one[1]])
     g_two.append(gather_two(1))
-    arrived([n_one])
-    n_two = [spread_normed(pl.ds(0, SHARE // 2))]
+    n_two.append(spread_normed(pl.ds(SHARE // 4, SHARE // 4)))
 
     s_base = (
         (lax.broadcasted_iota(jnp.int32, (COLS, TOK), 1) + s * SHARE) * WIDE
@@ -614,12 +610,12 @@
     r_one[1].append(back(1, 1))
     out_terms(1, 1)
 
-    r_two = [scatter_two(0)]
 
     near, far = kept // 2, 1 - kept // 2
     arrived([o_core[0]])
     xa[...] = total_of(ha[:, 2 * far + c], [ca[far]]).astype(BF)
     o_crs = [remote(xa, ya, crs)]
+    r_two = [scatter_two(0)]
     arrived([o_core[1]])
     xb[...] = total_of(hb[2 * far + c], [cb[far]]).astype(BF)
     o_crs.append(remote(xb, yb, crs))
@@ -737,11 +733,6 @@
     k_far = remote(cks, ckf, crs)
     send_query(1, q_far)
 
-    arrived([o_crs[1]])
-    fb[...] = total_of(hb[kept], [cb[near], yb[...]]).astype(BF)
-    o_fin.append(hand_out(1, fb, ob))
-
-
     e_base = (
         lax.broadcasted_iota(jnp.int32, (HALF, PART), 0) * D
         + lax.broadcasted_iota(jnp.int32, (HALF, PART), 1)
@@ -777,6 +768,11 @@
     t_tail = group(cvr)
     for k in range(2):
         remote(cot.at[2 * k + c, tail_part], cot.at[2 * k + c, tail_part], sib, t_tail)
+    arrived([o_crs[1]])
+    fb[...] = total_of(hb[kept], [cb[near], yb[...]]).astype(BF)
+    o_fin.append(hand_out(1, fb, ob))
+
+
     turns = [
         trig(jnp.broadcast_to(gkv[2 * k + c, KEYS - 16 : KEYS].astype(F32)[0:1], (ROT, TOK)))
         for k in range(2)
@@ -868,7 +864,7 @@
         pltpu.SMEM((1,), jnp.int32), pltpu.SMEM((1,), jnp.int32),
         v((COLS, SHARE), BF), v((HS, SHARE), BF), v((1, D), F32), v((2, ROT, TOK), F32), v((4, 2, ROT, TOK), F32),
         v((TOK, D), BF), v((TOK, PART), BF), v((COLS, D), BF), v((TOK, D), BF), v((2, COLS, TOK), F32),
-        v((2, TOK, 128), F32), v((16, D), BF), v((4, TOK, SHARE), BF), v((4, 4 * HS + 16, TOK), BF),
+        v((3, TOK, 128), F32), v((16, D), BF), v((4, TOK, SHARE), BF), v((4, 4 * HS + 16, TOK), BF),
         v((4, 4, HALF, PART), BF), v((2, 4, 4, HALF, PART), BF), v((2, 4, 4, HALF, PART), BF),
         v((2, 2 * PART, 16 * HALF), BF),
         v((2, 4, 4, HALF, 2 * SPAN), BF), v((2, 4, 4, HALF, 2 * SPAN), BF),

time: 74.7 us -> 72.5 us (0.971)
  Pallas kernels: 72.4 us -> 69.7 us
    pallas_call x1, Pallas kernels: 70 us -> 67.3 us  [per_device(): pl.pallas_call(kernel, out_shape=(jax.ShapeDtypeStruct((COLS, SHARE), BF)...]
where the time goes in v9:
time: 72.5 us; the launch traced here: 71.8 us
  Pallas kernels  69.7 us (96%)
  between operations  2.09 us (3%)
    pallas_call x1, Pallas kernels, per_device(): pl.pallas_call(kernel, out_shape=(jax.ShapeDtypeStruct((COLS, SHARE), BF)...  67.3 us
    pallas_call x1, Pallas kernels, per_device(): pl.pallas_call(widen, out_shape=(jax.ShapeDtypeStruct((COLS, SHARE), F32)...  2.45 us

profile of v9, /device:TPU:1, one launch (start us, length us, event | category | flops | bytes accessed | tf_op | source)
XLA Modules:
  0.0 71.8 jit_solution(13902603838369814466)
XLA Ops:
  1.9 67.3 %shard_map.104 = (bf16[288,1536]{1,0:T(8,128)(2,1)}, bf16[96,1536]{1,0:T(8,128)(2,1)}) custom-call(bf16[256,6144]{1,0:T(8,128)(2,1)} %tok_in.1, bf16[256,6144]{1,0:T(8,128)(2,1)} %tgt_in.1, f32[1,6144]{1,0:T(1,128)} %bitcast.4, bf16[288,6144]{1,0:T(8,128)(2,1)} %bitcast.3, bf16[96,6144]{1,0:T(8,128)(2,1)} %wo_in.1, s32[1]{0:T(128)S(6)} %copy.11.seed_in, ...), custom_call_target="tpu_custom_call" | custom-call | tf_op jit(solution)/shard_map/pallas_call | solution.py:891
  69.2 2.5 %shard_map.105 = (f32[288,1536]{1,0:T(8,128)}, f32[96,1536]{1,0:T(8,128)}) custom-call(bf16[288,1536]{1,0:T(8,128)(2,1)} %get-tuple-element.6.product_in, bf16[96,1536]{1,0:T(8,128)(2,1)} %get-tuple-element.7.out_in), custom_call_target="tpu_custom_call" | custom-call | tf_op jit(solution)/shard_map/pallas_call | solution.py:907

commit v10 on v9

--- a/solution.py
+++ b/solution.py
@@ -38,12 +38,12 @@
     return lax.shift_right_logical(state, jnp.full(state.shape, places, jnp.int32))
 
 
-def sign_bit(state):
+def sign_word(state):
     state = state ^ shifted(state, 16)
     state = state * jnp.int32(MIX[1])
     state = state ^ shifted(state, 13)
-    state = state * jnp.int32(MIX[2])
-    return (state ^ shifted(state, 16)) & jnp.int32(128)
+    state = state * jnp.int32(wrap(MIX[2] * 256))
+    return state ^ lax.shift_left(state, jnp.full(state.shape, 16, jnp.int32))
 
 
 def dot(a, b, contract):
@@ -275,8 +275,8 @@
 
         def step(i, carry):
             at = pl.ds(pl.multiple_of(i * STEP, STEP), STEP)
-            bit = sign_bit(q_base + i * jnp.int32(wrap(STEP * WIDE * MIX[0])))
-            probe = jnp.where(bit == 0, F32(q_probe), F32(-q_probe)).astype(BF)
+            word = sign_word(q_base + i * jnp.int32(wrap(STEP * WIDE * MIX[0])))
+            probe = jnp.where(word >= 0, F32(q_probe), F32(-q_probe)).astype(BF)
             both = dot(jnp.concatenate([wq[to, at], probe], axis=0), nrm[:, at], NT)
             acc[0, to] += both[:size]
             acc[1, to] += both[size:]
@@ -358,33 +358,6 @@
         ).astype(F32).T.astype(BF)
         qk[h] = jnp.concatenate([one, two], axis=1)
     resid[...] = (tok[:, lanes(own_cols, PART)].astype(F32) - tgt[...].astype(F32)).T
-
-    o_rows = lax.broadcasted_iota(jnp.int32, (HALF, PART), 0)
-    o_lanes = lax.broadcasted_iota(jnp.int32, (HALF, PART), 1)
-    o_base = (o_rows * D + o_lanes + (D * WIDE + own_cols)) * jnp.int32(MIX[0]) + seeded
-
-    def probe_piece(i, carry):
-        for k in range(4):
-            first = ((k * 2 + yl) * 4 + i) * HS
-            second = ((i * 2 + yl) * 4 + k) * HS + HALF
-            bit = sign_bit(o_base + first * jnp.int32(wrap(D * MIX[0])))
-            pp[0, i, k] = jnp.where(bit == 0, F32(o_probe), F32(-o_probe)).astype(BF)
-            bit = sign_bit(o_base + second * jnp.int32(wrap(D * MIX[0])))
-            pp[1, i, k] = jnp.where(bit == 0, F32(o_probe), F32(-o_probe)).astype(BF)
-        return carry
-
-    lax.fori_loop(0, 4, probe_piece, 0)
-
-    def turned(source, start):
-        def turn(i, carry):
-            for a in range(2):
-                value = source[a, pl.ds(2 * i, 2)].reshape(8 * HALF, PART).astype(F32)
-                wpt[a, start : start + PART, lanes(i * 8 * HALF, 8 * HALF)] = value.T.astype(BF)
-            return carry
-
-        lax.fori_loop(0, 2, turn, 0)
-
-    turned(pp, PART)
 
     def spread_normed(cols):
         held = group(nb.at[pl.ds(0, 2), pl.ds(0, 192), cols])
@@ -485,6 +458,33 @@
 
     g_one.append(attn_products(1))
 
+    o_rows = lax.broadcasted_iota(jnp.int32, (HALF, PART), 0)
+    o_lanes = lax.broadcasted_iota(jnp.int32, (HALF, PART), 1)
+    o_base = (o_rows * D + o_lanes + (D * WIDE + own_cols)) * jnp.int32(MIX[0]) + seeded
+
+    def probe_piece(i, carry):
+        for k in range(4):
+            first = ((k * 2 + yl) * 4 + i) * HS
+            second = ((i * 2 + yl) * 4 + k) * HS + HALF
+            word = sign_word(o_base + first * jnp.int32(wrap(D * MIX[0])))
+            pp[0, i, k] = jnp.where(word >= 0, F32(o_probe), F32(-o_probe)).astype(BF)
+            word = sign_word(o_base + second * jnp.int32(wrap(D * MIX[0])))
+            pp[1, i, k] = jnp.where(word >= 0, F32(o_probe), F32(-o_probe)).astype(BF)
+        return carry
+
+    lax.fori_loop(0, 4, probe_piece, 0)
+
+    def turned(source, start):
+        def turn(i, carry):
+            for a in range(2):
+                value = source[a, pl.ds(2 * i, 2)].reshape(8 * HALF, PART).astype(F32)
+                wpt[a, start : start + PART, lanes(i * 8 * HALF, 8 * HALF)] = value.T.astype(BF)
+            return carry
+
+        lax.fori_loop(0, 2, turn, 0)
+
+    turned(pp, PART)
+
     arrived([g_one[0]])
     g_two = [gather_two(0)]
     arrived([w_sib])
@@ -500,8 +500,8 @@
     ) * jnp.int32(MIX[0]) + seeded
 
     def sign_cols(i, carry):
-        bit = sign_bit(s_base + i * jnp.int32(wrap(TOK * WIDE * MIX[0])))
-        sgn[:, lanes(i * TOK, TOK)] = jnp.where(bit == 0, F32(math.sqrt(D)), F32(-math.sqrt(D)))
+        word = sign_word(s_base + i * jnp.int32(wrap(TOK * WIDE * MIX[0])))
+        sgn[:, lanes(i * TOK, TOK)] = jnp.where(word >= 0, F32(math.sqrt(D)), F32(-math.sqrt(D)))
         return carry
 
     lax.fori_loop(0, SHARE // TOK, sign_cols, 0)
@@ -756,10 +756,17 @@
 
         at = pl.ds(half * HALF, HALF)
         for k in range(4):
-            bit = sign_bit(e_base + jnp.int32(wrap((half * HALF * D + k * PART) * MIX[0])))
-            signed = (oa, ob)[half][k].astype(F32) * jnp.where(bit == 0, F32(scale), F32(-scale))
+            word = sign_word(e_base + jnp.int32(wrap((half * HALF * D + k * PART) * MIX[0])))
+            signed = (oa, ob)[half][k].astype(F32) * jnp.where(word >= 0, F32(scale), F32(-scale))
             oo[at, k * PART : (k + 1) * PART] = signed.astype(BF)
         leaving.append(stay(oo.at[at], oo_out.at[at]))
+
+
+    result(0)
+
+    arrived([o_crs[1]])
+    fb[...] = total_of(hb[kept], [cb[near], yb[...]]).astype(BF)
+    o_fin.append(hand_out(1, fb, ob))
 
 
     arrived([v_far])
@@ -768,11 +775,6 @@
     t_tail = group(cvr)
     for k in range(2):
         remote(cot.at[2 * k + c, tail_part], cot.at[2 * k + c, tail_part], sib, t_tail)
-    arrived([o_crs[1]])
-    fb[...] = total_of(hb[kept], [cb[near], yb[...]]).astype(BF)
-    o_fin.append(hand_out(1, fb, ob))
-
-
     turns = [
         trig(jnp.broadcast_to(gkv[2 * k + c, KEYS - 16 : KEYS].astype(F32)[0:1], (ROT, TOK)))
         for k in range(2)
@@ -801,10 +803,6 @@
         lax.fori_loop(start, stop, term, 0, unroll=3)
 
     first_terms(tail_part)
-    arrived([t_tail])
-    last_terms(tail_part, 0, 6)
-    leaving.append(stay(oq.at[tail_part], oq_out.at[tail_part]))
-
     arrived([k_far])
     for k in range(2):
         both = total_of(cks[k], [ckf[k]]).astype(BF).astype(F32)
@@ -813,9 +811,11 @@
     t_head = group(cot.at[pl.ds(0, 2), head_part])
     for k in range(2):
         remote(cot.at[2 * k + c, head_part], cot.at[2 * k + c, head_part], sib, t_head)
+    arrived([t_tail])
+    last_terms(tail_part, 0, 6)
+    leaving.append(stay(oq.at[tail_part], oq_out.at[tail_part]))
+
     first_terms(head_part)
-
-    result(0)
 
     arrived([t_head])
     for k in range(2):

time: 72.5 us -> 73.7 us (1.017)
  Pallas kernels: 69.7 us -> 71.5 us
    pallas_call x1, Pallas kernels: 67.3 us -> 69 us  [per_device(): pl.pallas_call(kernel, out_shape=(jax.ShapeDtypeStruct((COLS, SHARE), BF)...]
where the time goes in v10:
time: 73.7 us; the launch traced here: 73.6 us
  Pallas kernels  71.5 us (97%)
  between operations  2.09 us (3%)
    pallas_call x1, Pallas kernels, per_device(): pl.pallas_call(kernel, out_shape=(jax.ShapeDtypeStruct((COLS, SHARE), BF)...  69 us
    pallas_call x1, Pallas kernels, per_device(): pl.pallas_call(widen, out_shape=(jax.ShapeDtypeStruct((COLS, SHARE), F32)...  2.45 us

profile of v10, /device:TPU:1, one launch (start us, length us, event | category | flops | bytes accessed | tf_op | source)
XLA Modules:
  0.0 73.6 jit_solution(7252008252547572740)
XLA Ops:
  1.9 69.0 %shard_map.104 = (bf16[288,1536]{1,0:T(8,128)(2,1)}, bf16[96,1536]{1,0:T(8,128)(2,1)}) custom-call(bf16[256,6144]{1,0:T(8,128)(2,1)} %tok_in.1, bf16[256,6144]{1,0:T(8,128)(2,1)} %tgt_in.1, f32[1,6144]{1,0:T(1,128)} %bitcast.4, bf16[288,6144]{1,0:T(8,128)(2,1)} %bitcast.3, bf16[96,6144]{1,0:T(8,128)(2,1)} %wo_in.1, s32[1]{0:T(128)S(6)} %copy.11.seed_in, ...), custom_call_target="tpu_custom_call" | custom-call | tf_op jit(solution)/shard_map/pallas_call | solution.py:891
  71.0 2.5 %shard_map.105 = (f32[288,1536]{1,0:T(8,128)}, f32[96,1536]{1,0:T(8,128)}) custom-call(bf16[288,1536]{1,0:T(8,128)(2,1)} %get-tuple-element.6.product_in, bf16[96,1536]{1,0:T(8,128)(2,1)} %get-tuple-element.7.out_in), custom_call_target="tpu_custom_call" | custom-call | tf_op jit(solution)/shard_map/pallas_call | solution.py:907
